TPU v7x, 32 devices: a whole 2x2x4 slice. The times are simulated.
32 devices in a mesh: pipe: 2 (over core), dp: 4 (over z), tensor: 4 (over y, x).
Axes of the slice: x: 2, y: 2, z: 4, core: 2. Of those that a mesh axis runs over, the one named last changes fastest.
Arguments:
- peak_data: bfloat16 [8192, 100352], P('dp', 'tensor'), may hold values from 0 to 1, as said below
- region_weights: bfloat16 [2, 100352, 128], P('pipe', 'tensor'), may hold values from -0.35355339 to 0.35355339
- out_bias: float32 [100352], P('tensor'), may hold values from -4 to 4
- region_factor: float32 [100352], P('tensor'), may hold values from 0.3 to 0.95
- region_keep: int32 [100352], P('tensor'), may hold values 0 or 1
- cell_factor: float32 [8192], P('dp'), may hold values from 0.3 to 0.95
- batch_ids: int32 [8192], P('dp'), may hold values from 0 to 9
- latent_noise: float32 [8192, 10], P('dp'), may hold values from -4 to 4
- enc_bias_in: float32 [128], replicated, may hold values from -3 to 3
- enc_square: float32 [128, 128], replicated, may hold values from -0.5 to 0.5
- enc_bias_two: float32 [128], replicated, may hold values from -3 to 3
- enc_heads: float32 [128, 20], replicated, may hold values from -0.5 to 0.5
- head_bias: float32 [20], replicated, may hold values from -3 to 3
- dec_first: float32 [20, 128], replicated, may hold values from -2 to 2
- dec_bias_one: float32 [128], replicated, may hold values from -3 to 3
- dec_square: float32 [128, 128], replicated, may hold values from -0.5 to 0.5
- dec_bias_two: float32 [128], replicated, may hold values from -3 to 3
Outputs:
- region_grad: float32 [2, 100352, 128], P('pipe', 'tensor', 'dp')
- out_bias_grad: float32 [100352], P('tensor')
- enc_bias_in_grad: float32 [128], replicated
- enc_square_grad: float32 [128, 128], replicated
- enc_bias_two_grad: float32 [128], replicated
- enc_heads_grad: float32 [128, 20], replicated
- head_bias_grad: float32 [20], replicated
- dec_first_grad: float32 [20, 128], replicated
- dec_bias_one_grad: float32 [128], replicated
- dec_square_grad: float32 [128, 128], replicated
- dec_bias_two_grad: float32 [128], replicated
- mean_loss: float32 [], replicated
Inputs may be any that keep to these rules, and one draw needn't show every extreme that they name: `peak_data`: each entry is 0 or 1.
All inputs are finite; a program needn't handle non-finite values. No bound on the sum of `region_keep` on one device may be relied on, other than what follows from the above.
Results may differ from a plain program's by a relative error of at most 0.00059.
Values may be sent and summed in bfloat16 or wider, within the bound.
No kernel may reach another device: no remote copies, remote signals or barrier semaphores. Data moves between devices by JAX's collectives and lax.ppermute only.
A program may use at most 384 MiB of HBM per device.

v0:
```python
import jax
import jax.numpy as jnp
from jax import lax
from jax.sharding import PartitionSpec as P

R = 100352
MB = 4


EXACT = lax.Precision.HIGHEST
NORM_EPS = 1e-05


def swapped(block, axis, distance):
    count = lax.axis_size(axis)
    route = []
    for low in range(count):
        high = low | 1 << distance
        if high != low and high < count:
            route += [(low, high), (high, low)]
    return lax.ppermute(block, axis, route)


def layer_norm(values):
    centred = values - jnp.mean(values, axis=-1, keepdims=True)
    return centred * lax.rsqrt(jnp.mean(centred * centred, axis=-1, keepdims=True) + NORM_EPS)


def encoder_small(summed, bias_in, square, bias_two, head_w, head_bias, noise_rows):
    hidden = jax.nn.silu(layer_norm(summed + bias_in))
    hidden = jax.nn.silu(layer_norm(jnp.dot(hidden, square, precision=EXACT) + bias_two))
    head_out = jnp.dot(hidden, head_w, precision=EXACT) + head_bias
    latent = noise_rows.shape[1]
    average = head_out[:, :latent]
    variance = jnp.exp(head_out[:, latent:]) + 0.0001
    sample = average + jnp.sqrt(variance) * noise_rows
    kl_sum = 0.5 * jnp.sum(average * average + variance - jnp.log(variance) - 1.0)
    return (sample, kl_sum)


def decoder_small(inputs, first_w, bias_one, square, bias_two):
    hidden = jax.nn.silu(layer_norm(jnp.dot(inputs, first_w, precision=EXACT) + bias_one))
    return jax.nn.silu(layer_norm(jnp.dot(hidden, square, precision=EXACT) + bias_two))


def region_slope(logit, peak_rows, keep_mask, region_factor, cell_rows):
    factor = region_factor[None, :] * cell_rows[:, None]
    chance = jax.nn.sigmoid(logit)
    log_prob = jax.nn.log_sigmoid(logit) + jnp.log(factor)
    log_rest = jnp.log1p(-chance * factor)
    loss_sum = -jnp.sum(keep_mask[None, :] * (peak_rows * log_prob + (1.0 - peak_rows) * log_rest))
    slopes = -keep_mask[None, :] * (
        peak_rows * (1.0 - chance)
        - (1.0 - peak_rows) * factor * chance * (1.0 - chance) / (1.0 - chance * factor)
    )
    return (loss_sum, slopes)


def body(
    peak_data,
    region_weights,
    out_bias,
    region_factor,
    region_keep,
    cell_factor,
    batch_ids,
    latent_noise,
    enc_bias_in,
    enc_square,
    enc_bias_two,
    enc_heads,
    head_bias,
    dec_first,
    dec_bias_one,
    dec_square,
    dec_bias_two,
):
    weight = region_weights[0]
    regions_local, hidden_width = weight.shape
    block_rows = peak_data.shape[0] // MB
    latent = latent_noise.shape[1]
    cell_total = peak_data.shape[0] * lax.axis_size("dp")
    norm_scale = float(cell_total) ** (-0.5)
    keep_mask = region_keep.astype(jnp.float32)
    is_encoder = lax.axis_index("pipe") == 0
    batch_codes = jnp.arange(dec_first.shape[0] - latent, dtype=jnp.int32)
    enc_params = (enc_bias_in, enc_square, enc_bias_two, enc_heads, head_bias)
    dec_params = (dec_first, dec_bias_one, dec_square, dec_bias_two)
    enc_zero = tuple((jnp.zeros_like(weights) for weights in enc_params))
    dec_zero = tuple((jnp.zeros_like(weights) for weights in dec_params))
    region_zero = jnp.zeros((regions_local, hidden_width), jnp.float32)
    bias_zero = jnp.zeros((regions_local,), jnp.float32)
    scalar_zero = jnp.zeros((), jnp.float32)
    feature_zero = jnp.zeros((block_rows, hidden_width), jnp.float32)
    send_zero = jnp.zeros((block_rows, latent), jnp.bfloat16)

    def rows_of(values, which):
        return values[which * block_rows : (which + 1) * block_rows]

    def decoder_inputs(received, which):
        onehot = (rows_of(batch_ids, which)[:, None] == batch_codes[None, :]).astype(jnp.float32)
        return jnp.concatenate([received.astype(jnp.float32), onehot], axis=1)

    def encoder_first(moment, kept):

        def branch(received):
            partial_sum = feature_zero
            region_delta = region_zero
            enc_delta = enc_zero
            if moment < MB:
                partial_sum = jnp.dot(
                    rows_of(peak_data, moment), weight, preferred_element_type=jnp.float32
                )
            if moment >= 2:
                earlier = moment - 2
                noise_rows = rows_of(latent_noise, earlier)

                def encoder_local(summed, *weights):
                    return encoder_small(summed, *weights, noise_rows)

                unused, pull = jax.vjp(encoder_local, kept[earlier], *enc_params)
                pulled = pull((received.astype(jnp.float32), jnp.float32(norm_scale)))
                region_delta = lax.dot_general(
                    rows_of(peak_data, earlier),
                    pulled[0].astype(jnp.bfloat16),
                    (((0,), (0,)), ((), ())),
                    preferred_element_type=jnp.float32,
                )
                enc_delta = tuple(pulled[1:])
            return (partial_sum, scalar_zero, region_delta, bias_zero, enc_delta)

        return branch

    def decoder_first(moment):

        def branch(received):
            if 1 <= moment <= MB:
                earlier = moment - 1
                hidden = decoder_small(decoder_inputs(received, earlier), *dec_params)
                hidden_low = hidden.astype(jnp.bfloat16)
                logit = (
                    lax.dot_general(
                        hidden_low,
                        weight,
                        (((1,), (1,)), ((), ())),
                        preferred_element_type=jnp.float32,
                    )
                    + out_bias[None, :]
                )
                loss_sum, slopes = region_slope(
                    logit,
                    rows_of(peak_data, earlier).astype(jnp.float32),
                    keep_mask,
                    region_factor,
                    rows_of(cell_factor, earlier),
                )
                scaled = slopes * norm_scale
                scaled_low = scaled.astype(jnp.bfloat16)
                region_delta = lax.dot_general(
                    scaled_low,
                    hidden_low,
                    (((0,), (0,)), ((), ())),
                    preferred_element_type=jnp.float32,
                )
                partial_sum = jnp.dot(scaled_low, weight, preferred_element_type=jnp.float32)
                return (partial_sum, loss_sum, region_delta, jnp.sum(scaled, axis=0), enc_zero)
            return (feature_zero, scalar_zero, region_zero, bias_zero, enc_zero)

        return branch

    def encoder_second(moment):

        def branch(operands):
            summed, received = operands
            if moment < MB:
                sample, kl_sum = encoder_small(summed, *enc_params, rows_of(latent_noise, moment))
                return (sample.astype(jnp.bfloat16), kl_sum, dec_zero)
            return (send_zero, scalar_zero, dec_zero)

        return branch

    def decoder_second(moment):

        def branch(operands):
            summed, received = operands
            if 1 <= moment <= MB:
                earlier = moment - 1
                unused, pull = jax.vjp(
                    decoder_small, decoder_inputs(received, earlier), *dec_params
                )
                pulled = pull(summed)
                return (pulled[0][:, :latent].astype(jnp.bfloat16), scalar_zero, tuple(pulled[1:]))
            return (send_zero, scalar_zero, dec_zero)

        return branch

    received = send_zero
    kept = []
    region_total = region_zero
    bias_total = bias_zero
    recon_total = scalar_zero
    kl_total = scalar_zero
    enc_totals = enc_zero
    dec_totals = dec_zero
    for moment in range(MB + 2):
        partial_sum, loss_piece, region_delta, bias_delta, enc_delta = lax.cond(
            is_encoder, encoder_first(moment, kept), decoder_first(moment), received
        )
        bias_total = bias_total + bias_delta
        enc_totals = jax.tree.map(jnp.add, enc_totals, enc_delta)
        if moment >= 1:
            region_total = region_total + region_delta
        if moment <= MB:
            summed = lax.psum(partial_sum, "tensor")
            recon_total = recon_total + loss_piece
            if moment < MB:
                kept.append(summed)
            payload, kl_piece, dec_delta = lax.cond(
                is_encoder, encoder_second(moment), decoder_second(moment), (summed, received)
            )
            kl_total = kl_total + kl_piece
            dec_totals = jax.tree.map(jnp.add, dec_totals, dec_delta)
            received = swapped(payload, "pipe", 0)
    region_share = lax.psum_scatter(region_total, "dp", scatter_dimension=1, tiled=True)
    recon_total = lax.psum(recon_total, "tensor")
    loss_total = recon_total + kl_total
    summed_small = lax.psum(
        (
            enc_totals[0],
            enc_totals[1],
            enc_totals[2],
            enc_totals[3],
            enc_totals[4],
            dec_totals[0],
            dec_totals[1],
            dec_totals[2],
            dec_totals[3],
            bias_total,
            loss_total,
        ),
        ("pipe", "dp"),
    )
    mean_loss = summed_small[10] / (cell_total * R)
    region_grad = region_share.reshape(1, regions_local, region_share.shape[1])
    return (
        region_grad,
        summed_small[9],
        summed_small[0],
        summed_small[1],
        summed_small[2],
        summed_small[3],
        summed_small[4],
        summed_small[5],
        summed_small[6],
        summed_small[7],
        summed_small[8],
        mean_loss,
    )


def solution(mesh):
    in_specs = (
        P("dp", "tensor"),
        P("pipe", "tensor", None),
        P("tensor"),
        P("tensor"),
        P("tensor"),
        P("dp"),
        P("dp"),
        P("dp", None),
        P(),
        P(),
        P(),
        P(),
        P(),
        P(),
        P(),
        P(),
        P(),
    )
    out_specs = (
        P("pipe", "tensor", "dp"),
        P("tensor"),
        P(),
        P(),
        P(),
        P(),
        P(),
        P(),
        P(),
        P(),
        P(),
        P(),
    )
    return jax.shard_map(body, mesh=mesh, in_specs=in_specs, out_specs=out_specs, check_vma=False)
```

profile of v0, /device:TPU:0, one launch (start us, length us, event | category | flops | bytes accessed | tf_op | source)
XLA Modules:
  0.0 1176.6 jit_solution(17040458607632129420)
XLA Ops:
  7.2 13.7 %conditional.14 = (f32[512,128]{1,0:T(8,128)S(1)}) conditional(s32[]{:T(128)} %convert_element_type.143, () %tuple.122, (bf16[2048,25088]{1,0:T(8,128)(2,1)}, bf16[25088,128]{1,0:T(8,128)(2,1)}) %tuple.287), branch_computations={%region_0.0_spmd, %region_1.0_spmd} | conditional | flops 3288334336 | bytes 32374792 | solution.py:206
  7.2 13.7 %fusion = f32[512,128]{1,0:T(8,128)S(1)} fusion(bf16[25088,128]{1,0:T(8,128)(2,1)} %get-tuple-element.333, bf16[2048,25088]{1,0:T(8,128)(2,1)} %get-tuple-element.332), kind=kOutput, calls=%fused_computation | convolution fusion | flops 3288334336 | bytes 32374784 | tf_op jit(solution)/shard_map/cond/branch_1_fun/dot_general | solution.py:111
  21.8 45.7 %all-reduce.17.cloned.1.call-done = f32[512,128]{0,1:T(8,128)} async-done(((f32[512,128]{0,1:T(8,128)}), f32[512,128]{0,1:T(8,128)}) %all-reduce.17.cloned.1.call-update) | async-done | bytes 262160 | tf_op jit(solution)/shard_map/psum | solution.py:214
  67.6 6.8 conditional.15
  68.6 1.1 multiply_reduce_fusion.1
  69.7 1.5 fusion.501
  72.3 1.4 add_reduce_fusion.1
  75.8 26.8 %conditional.16 = (f32[512,128]{1,0:T(8,128)S(1)}, f32[]{:T(128)}, f32[25088]{0:T(1024)S(1)}, f32[25088,128]{0,1:T(8,128)}) conditional(s32[]{:T(128)} %convert_element_type.143, (f32[25088]{0:T(1024)S(1)}, bf16[2048,25088]{1,0:T(8,128)(2,1)}, bf16[512,10]{0,1:T(8,128)(2,1)}, s32[2048]{0:T(1024)}, s32[10]{0:T(128)S(1)}, ...), branch_computations={%region_10.17_spmd, %region_17.18_spmd} | conditional | flops 10432964608 | bytes 157162608 | solution.py:206
  83.0 6.0 broadcast_in_dim.92.clone
  89.0 13.7 %fusion.61 = f32[512,128]{1,0:T(8,128)S(1)} fusion(bf16[25088,128]{1,0:T(8,128)(2,1)} %get-tuple-element.355, bf16[2048,25088]{1,0:T(8,128)(2,1)} %get-tuple-element.354), kind=kOutput, calls=%fused_computation.93 | convolution fusion | flops 3288334336 | bytes 32374784 | tf_op jit(solution)/shard_map/cond/branch_1_fun/dot_general | solution.py:111
  103.6 158.4 %all-reduce.19.cloned.1.call-done = f32[512,128]{0,1:T(8,128)} async-done(((f32[512,128]{0,1:T(8,128)}), f32[512,128]{0,1:T(8,128)}) %all-reduce.19.cloned.1.call-update) | async-done | bytes 262160 | tf_op jit(solution)/shard_map/psum | solution.py:214
  262.0 5.4 conditional.17
  262.0 1.0 add_reduce_fusion.4
  263.1 1.1 multiply_reduce_fusion.9
  264.2 1.5 fusion.502
  267.5 3.7 collective-permute-start.1
  272.3 42.5 %conditional.18 = (f32[512,128]{1,0:T(8,128)S(1)}, f32[]{:T(128)}, f32[25088,128]{0,1:T(8,128)}, f32[25088]{0:T(1024)S(1)}, f32[128]{0:T(128)S(1)}, /*index=5*/f...) conditional(s32[]{:T(128)} %convert_element_type.143, (f32[25088]{0:T(1024)S(1)}, ...), branch_computations={%region_36.43_spmd, %region_43.55_spmd} | conditional | flops 10432964608 | bytes 157239520 | solution.py:206
  284.1 14.8 %convolution_bitcast_fusion = f32[25088,128]{0,1:T(8,128)} fusion(bf16[2048,25088]{1,0:T(8,128)(2,1)} %get-tuple-element.384, f32[512,128]{0,1:T(8,128)S(1)} %get-tuple-element.670, f32[512]{0:T(512)S(1)} %negate_multiply_fusion.2), kind=kOutput, calls=%fused_computation.233 | convolution fusion | flops 3288465408 | bytes 38799360 | tf_op jit(solution)/shard_map/cond/branch_1_fun/dot_general | solution.py:123
  299.1 1.1 fusion.159
  300.7 14.1 %fusion.151 = f32[512,128]{1,0:T(8,128)S(1)} fusion(bf16[25088,128]{1,0:T(8,128)(2,1)} %get-tuple-element.385, bf16[2048,25088]{1,0:T(8,128)(2,1)} %get-tuple-element.384), kind=kOutput, calls=%fused_computation.235 | convolution fusion | flops 3288334336 | bytes 32374784 | tf_op jit(solution)/shard_map/cond/branch_1_fun/dot_general | solution.py:111
  315.8 143.3 %all-reduce.21.cloned.1.call-done = f32[512,128]{0,1:T(8,128)} async-done(((f32[512,128]{0,1:T(8,128)}), f32[512,128]{0,1:T(8,128)}) %all-reduce.21.cloned.1.call-update) | async-done | bytes 262160 | tf_op jit(solution)/shard_map/psum | solution.py:214
  459.1 16.6 %conditional.19 = (bf16[512,10]{0,1:T(8,128)(2,1)S(1)}, f32[]{:T(128)}, f32[20,128]{1,0:T(8,128)S(1)}, f32[128]{0:T(128)S(1)}, f32[128,128]{1,0:T(8,128)S(1)}, /*index=5*/f32[128]{0:T(128)S(1)}) conditional(s32[]{:T(128)} %convert_element_type.143, (bf16[512,10]{0,1:T(8,128)(2,1)}, s32[2048]{0:T(1024)}, s32[10]{0:T(128)S(1)}, f32[20,128]{1,0:T(8,128)}, ...), branch_computations={%region_56.67_spmd, %region_67.0_spmd} | conditional | flops 346466048 | bytes 6242400
  459.1 1.0 add_reduce_fusion.11
  460.2 1.1 multiply_reduce_fusion.21
  461.3 1.5 fusion.503
  475.9 1.3 collective-permute-done.2
  477.3 40.3 %conditional.20 = (f32[512,128]{1,0:T(8,128)S(1)}, f32[]{:T(128)}, f32[25088,128]{0,1:T(8,128)}, f32[25088]{0:T(1024)S(1)}, f32[128]{0:T(128)S(1)}, /*index=5*/f...) conditional(s32[]{:T(128)} %convert_element_type.143, (f32[25088]{0:T(1024)S(1)}, ...), branch_computations={%region_73.80_spmd, %region_80.92_spmd} | conditional | flops 10432964608 | bytes 157239520 | solution.py:206
  487.6 14.8 %convolution_bitcast_fusion.1 = f32[25088,128]{0,1:T(8,128)} fusion(bf16[2048,25088]{1,0:T(8,128)(2,1)} %get-tuple-element.422, f32[512,128]{0,1:T(8,128)S(1)} %get-tuple-element.680, f32[512]{0:T(512)S(1)} %negate_multiply_fusion.6), kind=kOutput, calls=%fused_computation.428 | convolution fusion | flops 3288465408 | bytes 38799360 | tf_op jit(solution)/shard_map/cond/branch_1_fun/dot_general | solution.py:123
  503.5 14.1 %fusion.270 = f32[512,128]{1,0:T(8,128)S(1)} fusion(bf16[25088,128]{1,0:T(8,128)(2,1)} %get-tuple-element.423, bf16[2048,25088]{1,0:T(8,128)(2,1)} %get-tuple-element.422), kind=kOutput, calls=%fused_computation.430 | convolution fusion | flops 3288334336 | bytes 32374784 | tf_op jit(solution)/shard_map/cond/branch_1_fun/dot_general | solution.py:111
  518.6 145.2 %all-reduce.23.cloned.1.call-done = f32[512,128]{0,1:T(8,128)} async-done(((f32[512,128]{0,1:T(8,128)}), f32[512,128]{0,1:T(8,128)}) %all-reduce.23.cloned.1.call-update) | async-done | bytes 262160 | tf_op jit(solution)/shard_map/psum | solution.py:214
  663.8 5.6 conditional.21
  664.9 1.1 multiply_reduce_fusion.33
  666.0 1.5 fusion.504
  669.4 3.7 collective-permute-start.3
  674.3 20.6 %conditional.22 = (f32[512,128]{1,0:T(8,128)S(1)}, f32[]{:T(128)}, f32[25088,128]{0,1:T(8,128)}, f32[25088]{0:T(1024)S(1)}, f32[128]{0:T(128)S(1)}, /*index=5*/f...) conditional(s32[]{:T(128)} %convert_element_type.143, ...), branch_computations={%region_110.117_spmd, %region_117.129_spmd} | conditional | flops 10432964608 | bytes 157239520 | solution.py:206
  678.9 14.8 %convolution_bitcast_fusion.2 = f32[25088,128]{0,1:T(8,128)} fusion(bf16[2048,25088]{1,0:T(8,128)(2,1)} %get-tuple-element.468, f32[512,128]{0,1:T(8,128)S(1)} %get-tuple-element.690, f32[512]{0:T(512)S(1)} %negate_multiply_fusion.10), kind=kOutput, calls=%fused_computation.623 | convolution fusion | flops 3288465408 | bytes 38799360 | tf_op jit(solution)/shard_map/cond/branch_1_fun/dot_general | solution.py:123
  695.9 1.6 add_add_fusion.17
  697.4 163.3 %all-reduce.25.cloned.1.call-done = f32[512,128]{0,1:T(8,128)} async-done(((f32[512,128]{0,1:T(8,128)}), f32[512,128]{0,1:T(8,128)}) %all-reduce.25.cloned.1.call-update) | async-done | bytes 262160 | tf_op jit(solution)/shard_map/psum | solution.py:214
  860.7 9.1 collective-permute-start.4
  870.7 18.7 %conditional.24 = (f32[25088,128]{0,1:T(8,128)}, f32[128]{0:T(128)S(1)}, f32[128,128]{1,0:T(8,128)S(1)}, f32[128]{0:T(128)S(1)}, f32[128,20]{0,1:T(8,128)S(1)}, /*index=5*/f32[20]{0:T(128)S(1)}) conditional(s32[]{:T(128)} %convert_element_type.143, () %tuple.138, (f32[128]{0:T(128)S(1)}, f32[512,128]{0,1:T(8,128)S(1)}, ...), branch_computations={%region_142.143_spmd, %region_143.155_spmd} | conditional | flops 3643200256 | bytes 45177552 | solution.py:206
  873.5 14.8 %convolution_bitcast_fusion.3 = f32[25088,128]{0,1:T(8,128)} fusion(bf16[2048,25088]{1,0:T(8,128)(2,1)} %get-tuple-element.485, f32[512,128]{0,1:T(8,128)S(1)} %get-tuple-element.698, f32[512]{0:T(512)S(1)} %negate_multiply_fusion.14), kind=kOutput, calls=%fused_computation.725 | convolution fusion | flops 3288465408 | bytes 38799360 | tf_op jit(solution)/shard_map/cond/branch_1_fun/dot_general | solution.py:123
  890.4 25.7 %add_add_fusion.16 = f32[25088,128]{0,1:T(8,128)} fusion(f32[25088,128]{0,1:T(8,128)} %get-tuple-element.573, f32[25088,128]{0,1:T(8,128)} %get-tuple-element.570, f32[25088,128]{0,1:T(8,128)} %get-tuple-element.567, f32[25088,128]{0,1:T(8,128)} %get-tuple-element.649, f32[25088,128]{0,1:T(8,128)} %get-tuple-element.564), kind=kLoop, calls=%fused_computation.782 | loop fusion | flops 12845056 | bytes 77070336 | tf_op jit(solution)/shard_map/add | solution.py:212
  916.1 9.4 psum.134
  926.5 28.3 %all-reduce.8 = (f32[128]{0:T(128)}, f32[128]{0:T(128)}, f32[128,20]{0,1:T(8,128)}, f32[20]{0:T(128)}, f32[20,128]{1,0:T(8,128)}, /*index=5*/f32[128]{0:T(128)}, f32[128]{0:T(128)}, f32[]{:T(128)}) all-reduce(f32[128]{0:T(128)S(1)} %get-tuple-element.806, ...), channel_id=1, replica_groups=mesh['pipe'=2,'dp'=4,'tensor'=4] {'pipe','dp'}, use_global_device_ids=true, to_apply=%region_157.158 | all-reduce | flops 5653 | bytes 45224 | tf_op jit(solution)/shard_map/psum | solution.py:227
  955.5 208.2 %reduce-scatter.2.cloned.1.call-done = f32[25088,32]{0,1:T(8,128)} async-done(((f32[25088,128]{0,1:T(8,128)}), f32[25088,32]{0,1:T(8,128)}) %reduce-scatter.2.cloned.1.call-update) | async-done | bytes 3211280 | tf_op jit(solution)/shard_map/reduce_scatter | solution.py:224
  1163.7 1.5 copy.194
  1165.3 1.5 copy.195
  1166.7 1.5 copy.196
  (330 shorter events, 32.3 us)
Async XLA Ops:
  7.2 60.4 %all-reduce.17.cloned.1.call-start = ((), (), s32[]{:S(2)}) async-start(), calls=%async_computation.1 | async-start | bytes 524288 | tf_op jit(solution)/shard_map/psum | solution.py:214
  21.8 240.2 %all-reduce.19.cloned.1.call-start = ((), (), s32[]{:S(2)}) async-start(), calls=%async_computation.2 | async-start | bytes 524288 | tf_op jit(solution)/shard_map/psum | solution.py:214
  74.4 1.4 collective-permute-start
  75.8 186.2 %copy-start.4 = (f32[2048,10]{0,1:T(8,128)S(1)}, f32[2048,10]{0,1:T(8,128)}, u32[]{:S(2)}) copy-start(f32[2048,10]{0,1:T(8,128)} %param.46) | copy-start | bytes 245764
  75.8 186.2 %copy-start.9 = (f32[128]{0:T(128)S(1)}, f32[128]{0:T(128)}, u32[]{:S(2)}) copy-start(f32[128]{0:T(128)} %param.47) | copy-start | bytes 1540
  75.8 186.2 %copy-start.61 = (f32[128,128]{1,0:T(8,128)S(1)}, f32[128,128]{1,0:T(8,128)}, u32[]{:S(2)}) copy-start(f32[128,128]{1,0:T(8,128)} %param.48) | copy-start | bytes 196612
  75.8 186.2 %copy-start.65 = (f32[128,20]{0,1:T(8,128)S(1)}, f32[128,20]{0,1:T(8,128)}, u32[]{:S(2)}) copy-start(f32[128,20]{0,1:T(8,128)} %param.50) | copy-start | bytes 30724
  75.8 186.2 %copy-start.69 = (f32[128]{0:T(128)S(1)}, f32[128]{0:T(128)}, u32[]{:S(2)}) copy-start(f32[128]{0:T(128)} %param.49) | copy-start | bytes 1540
  75.8 186.2 %copy-start.73 = (f32[20]{0:T(128)S(1)}, f32[20]{0:T(128)}, u32[]{:S(2)}) copy-start(f32[20]{0:T(128)} %param.51) | copy-start | bytes 244
  75.8 196.4 %copy-start.3 = (f32[512,128]{0,1:T(8,128)S(1)}, f32[512,128]{0,1:T(8,128)}, u32[]{:S(2)}) copy-start(f32[512,128]{0,1:T(8,128)} %all-reduce.17.cloned.1.call-done) | copy-start | bytes 786436
  75.8 196.4 %copy-start.62 = (f32[128,128]{1,0:T(8,128)S(1)}, f32[128,128]{1,0:T(8,128)}, u32[]{:S(2)}) copy-start(f32[128,128]{1,0:T(8,128)} %param.48) | copy-start | bytes 196612
  102.7 169.6 %copy-start.15 = (f32[25088]{0:T(1024)}, f32[25088]{0:T(1024)S(1)}, u32[]{:S(2)}) copy-start(f32[25088]{0:T(1024)S(1)} %get-tuple-element.574) | copy-start | bytes 301060
  103.5 355.6 %all-reduce.21.cloned.1.call-start = ((), (), s32[]{:S(2)}) async-start(), calls=%async_computation.3 | async-start | bytes 524288 | tf_op jit(solution)/shard_map/psum | solution.py:214
  267.5 4.7 collective-permute-start.1
  272.2 186.9 %copy-start.10 = (f32[128]{0:T(128)S(1)}, f32[128]{0:T(128)}, u32[]{:S(2)}) copy-start(f32[128]{0:T(128)} %param.47) | copy-start | bytes 1540
  272.2 186.9 %copy-start.66 = (f32[128,20]{0,1:T(8,128)S(1)}, f32[128,20]{0,1:T(8,128)}, u32[]{:S(2)}) copy-start(f32[128,20]{0,1:T(8,128)} %param.50) | copy-start | bytes 30724
  272.2 186.9 %copy-start.70 = (f32[128]{0:T(128)S(1)}, f32[128]{0:T(128)}, u32[]{:S(2)}) copy-start(f32[128]{0:T(128)} %param.49) | copy-start | bytes 1540
  272.2 186.9 %copy-start.74 = (f32[20]{0:T(128)S(1)}, f32[20]{0:T(128)}, u32[]{:S(2)}) copy-start(f32[20]{0:T(128)} %param.51) | copy-start | bytes 244
  272.3 204.9 %copy-start.1 = (f32[512,128]{0,1:T(8,128)S(1)}, f32[512,128]{0,1:T(8,128)}, u32[]{:S(2)}) copy-start(f32[512,128]{0,1:T(8,128)} %all-reduce.19.cloned.1.call-done) | copy-start | bytes 786436
  272.3 204.9 %copy-start.71 = (f32[128]{0:T(128)S(1)}, f32[128]{0:T(128)}, u32[]{:S(2)}) copy-start(f32[128]{0:T(128)} %param.49) | copy-start | bytes 1540
  272.3 204.9 %copy-start.75 = (f32[20]{0:T(128)S(1)}, f32[20]{0:T(128)}, u32[]{:S(2)}) copy-start(f32[20]{0:T(128)} %param.51) | copy-start | bytes 244
  314.8 162.4 %copy-start.23 = (f32[128,20]{0,1:T(8,128)}, f32[128,20]{0,1:T(8,128)S(1)}, u32[]{:S(2)}) copy-start(f32[128,20]{0,1:T(8,128)S(1)} %get-tuple-element.590) | copy-start | bytes 30724
  314.9 162.4 %copy-start.45 = (f32[128]{0:T(128)}, f32[128]{0:T(128)S(1)}, u32[]{:S(2)}) copy-start(f32[128]{0:T(128)S(1)} %get-tuple-element.578) | copy-start | bytes 1540
  314.9 162.4 %copy-start.47 = (f32[128]{0:T(128)}, f32[128]{0:T(128)S(1)}, u32[]{:S(2)}) copy-start(f32[128]{0:T(128)S(1)} %get-tuple-element.586) | copy-start | bytes 1540
  314.9 162.4 %copy-start.49 = (f32[20]{0:T(128)}, f32[20]{0:T(128)S(1)}, u32[]{:S(2)}) copy-start(f32[20]{0:T(128)S(1)} %get-tuple-element.594) | copy-start | bytes 244
  314.9 162.4 %copy-start.5 = (f32[128,128]{1,0:T(8,128)}, f32[128,128]{1,0:T(8,128)S(1)}, u32[]{:S(2)}) copy-start(f32[128,128]{1,0:T(8,128)S(1)} %get-tuple-element.582) | copy-start | bytes 196612
  314.9 162.4 %copy-start.12 = (f32[25088]{0:T(1024)}, f32[25088]{0:T(1024)S(1)}, u32[]{:S(2)}) copy-start(f32[25088]{0:T(1024)S(1)} %get-tuple-element.575) | copy-start | bytes 301060
  315.8 348.0 %all-reduce.23.cloned.1.call-start = ((), (), s32[]{:S(2)}) async-start(), calls=%async_computation.4 | async-start | bytes 524288 | tf_op jit(solution)/shard_map/psum | solution.py:214
  475.8 1.4 collective-permute-start.2
  477.2 186.5 %copy-start.63 = (f32[128,128]{1,0:T(8,128)S(1)}, f32[128,128]{1,0:T(8,128)}, u32[]{:S(2)}) copy-start(f32[128,128]{1,0:T(8,128)} %param.48) | copy-start | bytes 196612
  477.2 186.5 %copy-start.67 = (f32[128,20]{0,1:T(8,128)S(1)}, f32[128,20]{0,1:T(8,128)}, u32[]{:S(2)}) copy-start(f32[128,20]{0,1:T(8,128)} %param.50) | copy-start | bytes 30724
  477.3 196.9 %copy-start = (f32[512,128]{0,1:T(8,128)S(1)}, f32[512,128]{0,1:T(8,128)}, u32[]{:S(2)}) copy-start(f32[512,128]{0,1:T(8,128)} %all-reduce.21.cloned.1.call-done) | copy-start | bytes 786436
  477.3 196.9 %copy-start.64 = (f32[128,128]{1,0:T(8,128)S(1)}, f32[128,128]{1,0:T(8,128)}, u32[]{:S(2)}) copy-start(f32[128,128]{1,0:T(8,128)} %param.48) | copy-start | bytes 196612
  517.7 156.6 %copy-start.7 = (f32[128,128]{1,0:T(8,128)}, f32[128,128]{1,0:T(8,128)S(1)}, u32[]{:S(2)}) copy-start(f32[128,128]{1,0:T(8,128)S(1)} %get-tuple-element.583) | copy-start | bytes 196612
  518.5 342.2 %all-reduce.25.cloned.1.call-start = ((), (), s32[]{:S(2)}) async-start(), calls=%async_computation.5 | async-start | bytes 524288 | tf_op jit(solution)/shard_map/psum | solution.py:214
  669.4 4.7 collective-permute-start.3
  674.2 195.6 %copy-start.18 = (f32[128,128]{1,0:T(8,128)S(1)}, f32[128,128]{1,0:T(8,128)}, u32[]{:S(2)}) copy-start(f32[128,128]{1,0:T(8,128)} %copy-done.17) | copy-start | bytes 196612
  674.2 195.6 %copy-start.20 = (f32[128,128]{1,0:T(8,128)S(1)}, f32[128,128]{1,0:T(8,128)}, u32[]{:S(2)}) copy-start(f32[128,128]{1,0:T(8,128)} %copy-done.19) | copy-start | bytes 196612
  674.2 195.6 %copy-start.22 = (f32[128,128]{1,0:T(8,128)S(1)}, f32[128,128]{1,0:T(8,128)}, u32[]{:S(2)}) copy-start(f32[128,128]{1,0:T(8,128)} %copy-done.21) | copy-start | bytes 196612
  674.2 196.5 %copy-start.2 = (f32[512,128]{0,1:T(8,128)S(1)}, f32[512,128]{0,1:T(8,128)}, u32[]{:S(2)}) copy-start(f32[512,128]{0,1:T(8,128)} %all-reduce.23.cloned.1.call-done) | copy-start | bytes 786436
  674.2 196.5 %copy-start.68 = (f32[128,20]{0,1:T(8,128)S(1)}, f32[128,20]{0,1:T(8,128)}, u32[]{:S(2)}) copy-start(f32[128,20]{0,1:T(8,128)} %param.50) | copy-start | bytes 30724
  674.3 196.4 %copy-start.72 = (f32[128]{0:T(128)S(1)}, f32[128]{0:T(128)}, u32[]{:S(2)}) copy-start(f32[128]{0:T(128)} %param.49) | copy-start | bytes 1540
  674.3 196.4 %copy-start.76 = (f32[20]{0:T(128)S(1)}, f32[20]{0:T(128)}, u32[]{:S(2)}) copy-start(f32[20]{0:T(128)} %param.51) | copy-start | bytes 244
  694.9 194.7 %copy-start.6 = (f32[128,128]{1,0:T(8,128)S(1)}, f32[128,128]{1,0:T(8,128)}, u32[]{:S(2)}) copy-start(f32[128,128]{1,0:T(8,128)} %copy-done.5) | copy-start | bytes 196612
  694.9 194.7 %copy-start.8 = (f32[128,128]{1,0:T(8,128)S(1)}, f32[128,128]{1,0:T(8,128)}, u32[]{:S(2)}) copy-start(f32[128,128]{1,0:T(8,128)} %copy-done.7) | copy-start | bytes 196612
  695.8 259.7 %all-reduce.27.cloned.1.call-start = ((), (), s32[]{:S(2)}) async-start(), calls=%async_computation.7 | async-start | bytes 466944 | tf_op jit(solution)/shard_map/psum | solution.py:227
  860.7 10.0 collective-permute-start.4
  890.3 273.4 %reduce-scatter.2.cloned.1.call-start = ((), (), s32[]{:S(2)}) async-start(), calls=%async_computation.6 | async-start | bytes 16056320 | tf_op jit(solution)/shard_map/reduce_scatter | solution.py:224
  (37 other events, 1472.0 us)
Sparse Core Ops, SparseCore 0:
  21.9 45.6 all-reduce.16
  103.7 158.2 all-reduce.18
  315.9 143.1 all-reduce.20
  518.7 145.0 all-reduce.22
  695.9 164.7 all-reduce.24
  890.4 52.8 all-reduce.26
  946.2 217.4 reduce-scatter.1
where the time goes:
time: 1180 us
  waiting for transfers between devices  868 us (74%)
  matrix products  134 us (11%)
  other arithmetic  47.3 us (4%)
  loops' own time  39.1 us (3%)
  blocking collectives  37.8 us (3%)
  between operations  18.1 us (2%)
  starting transfers between devices  17 us (1%)
  local copies, waits for them, and re-layouts  15.2 us (1%)
    psum x5, waiting for transfers between devices, body(): summed = lax.psum(partial_sum, 'tensor')  656 us
    reduce_scatter x1, waiting for transfers between devices, body(): lax.psum_scatter(region_total, 'dp', scatter_dimension=1, tiled=True)  208 us
    dot_general x4, matrix products, branch(): lax.dot_general(rows_of(peak_data, earlier), pulled[0].astype(jnp.bfloat1...  59.3 us
    dot_general x4, matrix products, branch(): jnp.dot(rows_of(peak_data, moment), weight, preferred_element_type=jnp.fl...  55.5 us
    psum x1, blocking collectives, body(): lax.psum((enc_totals[0], enc_totals[1], enc_totals[2], enc_totals[3], enc...  28.3 us
    add x1, other arithmetic, body(): region_total = region_total + region_delta  25.7 us
    another operation x6, loops' own time, body(): lax.cond(is_encoder, encoder_first(moment, kept), decoder_first(moment),...  24.8 us
  transfers between devices with their start and end apart: 12, of which 11 were waited for; matrix products, arithmetic and copies ran while one was open for 2% of the time, Pallas kernels for 0%

commit v1 on v0

v1 whole, which is shorter than its diff:
```python
import functools

import jax
import jax.numpy as jnp
import numpy as np
from jax import lax
from jax.experimental import pallas as pl
from jax.experimental.pallas import tpu as pltpu
from jax.sharding import PartitionSpec as P

EXACT = lax.Precision.HIGHEST
NORM_EPS = 1e-05
LOG2E = float(np.log2(np.e))
LN2 = float(np.log(2.0))
BIG_BITS = 56
BIG = float(2.0**BIG_BITS)
MIB = 1 << 20
EXTRA = 16


def params_of(mib):
    return pltpu.CompilerParams(vmem_limit_bytes=mib * MIB)


def layer_norm(values):
    centred = values - jnp.mean(values, axis=-1, keepdims=True)
    return centred * lax.rsqrt(jnp.mean(centred * centred, axis=-1, keepdims=True) + NORM_EPS)


def silu(values):
    return values * jax.nn.sigmoid(values)


def mm(a, b):
    return lax.dot_general(a, b, (((1,), (0,)), ((), ())), precision=EXACT, preferred_element_type=jnp.float32)


def encoder_small(summed, bias_in, square, bias_two, mean_w, var_w, mean_b, var_b, noise_rows):
    hidden = silu(layer_norm(summed + bias_in))
    hidden = silu(layer_norm(mm(hidden, square) + bias_two))
    average = mm(hidden, mean_w) + mean_b
    variance = jnp.exp(mm(hidden, var_w) + var_b) + 0.0001
    sample = average + jnp.sqrt(variance) * noise_rows
    kl_rows = 0.5 * jnp.sum(average * average + variance - jnp.log(variance) - 1.0, axis=1, keepdims=True)
    return (sample, jnp.sum(kl_rows, axis=0, keepdims=True))


def decoder_small(latent_rows, onehot, first_z, first_b, bias_one, square, bias_two):
    hidden = silu(layer_norm(mm(latent_rows, first_z) + mm(onehot, first_b) + bias_one))
    return silu(layer_norm(mm(hidden, square) + bias_two))


def onehot_of(ids, width):
    codes = lax.broadcasted_iota(jnp.int32, (ids.shape[0], width), 1)
    return (ids == codes).astype(jnp.float32)


def forward_kernel(count, *refs):
    parts = refs[:count]
    noise, ids = refs[count : count + 2]
    enc = [r[...] for r in refs[count + 2 : count + 9]]
    dec = [r[...] for r in refs[count + 9 : count + 14]]
    summed_out, z_out, g2_out, kl_out = refs[count + 14 :]
    summed = parts[0][...]
    for part in parts[1:]:
        summed = summed + part[...]
    sample, kl_sum = encoder_small(summed, *enc, noise[...])
    z_low = sample.astype(jnp.bfloat16)
    hidden = decoder_small(z_low.astype(jnp.float32), onehot_of(ids[...], dec[1].shape[0]), *dec)
    summed_out[...] = summed
    z_out[...] = z_low
    g2_out[...] = hidden.astype(jnp.bfloat16)
    kl_out[...] = kl_sum


def backward_kernel(count, norm_scale, *refs):
    parts = refs[:count]
    summed, z_low, noise, ids = refs[count : count + 4]
    enc = [r[...] for r in refs[count + 4 : count + 11]]
    dec = [r[...] for r in refs[count + 11 : count + 16]]
    outs = refs[count + 16 :]
    dg2 = parts[0][...]
    for part in parts[1:]:
        dg2 = dg2 + part[...]
    onehot = onehot_of(ids[...], dec[1].shape[0])
    unused, pull = jax.vjp(lambda z, *w: decoder_small(z, onehot, *w), z_low[...].astype(jnp.float32), *dec)
    dz, *dec_grads = pull(dg2)
    noise_rows = noise[...]
    unused, pull = jax.vjp(lambda s, *w: encoder_small(s, *w, noise_rows), summed[...], *enc)
    dz_low = dz.astype(jnp.bfloat16).astype(jnp.float32)
    dp, *enc_grads = pull((dz_low, jnp.full((1, 1), norm_scale, jnp.float32)))
    outs[0][...] = dp.astype(jnp.bfloat16)
    for out, grad in zip(outs[1:], enc_grads + dec_grads):
        out[...] = grad


def project_kernel(half_ref, x_ref, w_ref, out_ref):
    out_ref[...] = jnp.dot(x_ref[...], w_ref[...], preferred_element_type=jnp.float32)


def project(half, peaks, weight):
    cells, width = peaks.shape[0], weight.shape[1]
    regions = weight.shape[0]
    rows = min(256, cells)
    return pl.pallas_call(
        project_kernel,
        grid_spec=pltpu.PrefetchScalarGridSpec(
            num_scalar_prefetch=1,
            grid=(cells // rows,),
            in_specs=[
                pl.BlockSpec((rows, regions), lambda i, h: (i, h[0])),
                pl.BlockSpec((regions, width), lambda i, h: (0, 0)),
            ],
            out_specs=pl.BlockSpec((rows, width), lambda i, h: (i, 0)),
        ),
        out_shape=jax.ShapeDtypeStruct((cells, width), jnp.float32),
        compiler_params=params_of(48),
        cost_estimate=pl.CostEstimate(
            flops=2 * cells * regions * width, bytes_accessed=2 * cells * regions, transcendentals=0
        ),
        name="project",
    )(half, peaks, weight)


def regions_kernel(
    tile, rows_at_once, piece, half_ref, x_ref, w_ref, g_ref, gt_ref, a_ref, fa_ref, ck_ref, cf_ref, before_ref,
    dg_ref, dw_ref, st_ref, m0, m1, e0, e1, g_s,
):
    cells, chunk = x_ref.shape
    blocks = cells // rows_at_once
    M, E = (m0, m1), (e0, e1)

    @pl.when(pl.program_id(0) == 0)
    def first():
        dg_ref[...] = before_ref[...]
        scaled = g_ref[...].astype(jnp.float32) * (-LOG2E)
        high = scaled.astype(jnp.bfloat16)
        g_s[:, :128] = high
        g_s[:, 128:] = (scaled - high.astype(jnp.float32)).astype(jnp.bfloat16)

    def one_tile(t, carry):
        cols = pl.ds(pl.multiple_of(t * tile, 128), tile)
        w = w_ref[cols, :]
        w2 = jnp.concatenate([w, w], axis=1)
        wide = (8, tile)
        a = jnp.broadcast_to(a_ref[:, cols], wide)[None]
        fa = jnp.broadcast_to(fa_ref[:, cols], wide)[None]
        ck = jnp.broadcast_to(ck_ref[:, cols], wide)[None]

        def rows(i, o=0, n=rows_at_once):
            return pl.ds(pl.multiple_of(i * rows_at_once + o, 16), n)

        def logit(i, s, o, n):
            M[s][o : o + n, :] = lax.dot_general(
                g_s[rows(i, o, n), :], w2, (((1,), (1,)), ((), ())), preferred_element_type=jnp.float32
            )

        def elementwise(i, s, o, sums):
            e_sum, l_sum = sums
            shape = (piece // 8, 8, tile)
            u = jnp.exp2(M[s][o : o + piece, :]).reshape(shape)
            cf = cf_ref[rows(i, o, piece), :]
            cf = jnp.concatenate([cf] * (tile // 128), axis=1).reshape(shape)
            seen = (x_ref[rows(i, o, piece), cols] * jnp.bfloat16(BIG)).astype(jnp.float32).reshape(shape)
            total = u + a
            rest = (total - fa * cf) + seen
            d = pltpu.reciprocal(rest, approx=True)
            slope = (u * ck) * (d - pltpu.reciprocal(total, approx=True))
            ratio = (d * total).reshape(piece // 16, 2, 8, tile)
            E[s][o : o + piece, :] = slope.reshape(piece, tile).astype(jnp.bfloat16)
            e_sum = e_sum + jnp.sum(slope, axis=0)
            l_sum = l_sum + jnp.sum(jnp.log2(ratio[:, 0] * ratio[:, 1]), axis=0)
            return e_sum, l_sum

        def cell_grad(i, s):
            dg_ref[rows(i), :] += jnp.dot(E[s][...], w, preferred_element_type=jnp.float32)

        def region_grad(i, s, start=False):
            part = jnp.dot(gt_ref[i], E[s][...], preferred_element_type=jnp.float32)
            if start:
                dw_ref[:, cols] = part
            else:
                dw_ref[:, cols] += part

        def step(i, s, sums, logits=True, grads=True, start=False):
            dots = rows_at_once // 2
            for o in range(0, rows_at_once, piece):
                if logits and o % dots == 0:
                    logit(i + 1, 1 - s, o, dots)
                sums = elementwise(i, s, o, sums)
                if grads and o == dots:
                    cell_grad(i - 1, 1 - s)
            if grads:
                region_grad(i - 1, 1 - s, start)
            return sums

        zero = jnp.zeros(wide, jnp.float32)
        sums = (zero, zero)
        logit(0, 0, 0, rows_at_once)
        sums = step(0, 0, sums, grads=False)
        for i in range(1, blocks):
            sums = step(i, i % 2, sums, logits=i < blocks - 1, start=i == 1)
        cell_grad(blocks - 1, (blocks - 1) % 2)
        region_grad(blocks - 1, (blocks - 1) % 2, blocks == 1)
        st_ref[0:8, cols] = sums[0]
        st_ref[8:16, cols] = sums[1]
        return carry

    lax.fori_loop(0, chunk // tile, one_tile, 0)


def regions_pass(half, peaks, weight, hidden, hidden_t, a, fa, ck, cf, before, first, count, chunk, per_half):
    cells, width = hidden.shape
    tile, rows, piece = min(256, chunk), min(512, cells // 2), 64
    blocks = cells // rows
    return pl.pallas_call(
        functools.partial(regions_kernel, tile, rows, piece),
        grid_spec=pltpu.PrefetchScalarGridSpec(
            num_scalar_prefetch=1,
            grid=(count,),
            in_specs=[
                pl.BlockSpec((cells, chunk), lambda j, h: (0, h[0] * per_half + first + j)),
                pl.BlockSpec((chunk, width), lambda j, h: (first + j, 0)),
                pl.BlockSpec((cells, width), lambda j, h: (0, 0)),
                pl.BlockSpec((blocks, width, rows), lambda j, h: (0, 0, 0)),
                pl.BlockSpec((1, chunk), lambda j, h: (0, first + j)),
                pl.BlockSpec((1, chunk), lambda j, h: (0, first + j)),
                pl.BlockSpec((1, chunk), lambda j, h: (0, first + j)),
                pl.BlockSpec((cells, 128), lambda j, h: (0, 0)),
                pl.BlockSpec((cells, width), lambda j, h: (0, 0)),
            ],
            out_specs=[
                pl.BlockSpec((cells, width), lambda j, h: (0, 0)),
                pl.BlockSpec((width, chunk), lambda j, h: (0, j)),
                pl.BlockSpec((16, chunk), lambda j, h: (0, j)),
            ],
            scratch_shapes=[pltpu.VMEM((rows, tile), jnp.float32)] * 2
            + [pltpu.VMEM((rows, tile), jnp.bfloat16)] * 2
            + [pltpu.VMEM((cells, 2 * width), jnp.bfloat16)],
        ),
        out_shape=[
            jax.ShapeDtypeStruct((cells, width), jnp.float32),
            jax.ShapeDtypeStruct((width, count * chunk), jnp.float32),
            jax.ShapeDtypeStruct((16, count * chunk), jnp.float32),
        ],
        compiler_params=params_of(56),
        cost_estimate=pl.CostEstimate(
            flops=10 * cells * count * chunk * width,
            bytes_accessed=2 * cells * count * chunk,
            transcendentals=16 * cells * count * chunk,
        ),
        name="regions",
    )(half, peaks, weight, hidden, hidden_t, a, fa, ck, cf, before)


def outer_kernel(half_ref, x_ref, t_ref, dw_ref, extra_ref):
    width = dw_ref.shape[0]
    tile = min(256, x_ref.shape[1])
    for c in range(0, x_ref.shape[1], tile):
        part = jnp.dot(t_ref[...], x_ref[:, c : c + tile], preferred_element_type=jnp.float32)
        dw_ref[:, c : c + tile] = part[:width]
        extra_ref[:, c : c + tile] = part[width:]


def outer(half, peaks, left, first, count, chunk, per_half):
    cells = peaks.shape[0]
    width = left.shape[0] - EXTRA
    return pl.pallas_call(
        outer_kernel,
        grid_spec=pltpu.PrefetchScalarGridSpec(
            num_scalar_prefetch=1,
            grid=(count,),
            in_specs=[
                pl.BlockSpec((cells, chunk), lambda j, h: (0, h[0] * per_half + first + j)),
                pl.BlockSpec((width + EXTRA, cells), lambda j, h: (0, 0)),
            ],
            out_specs=[
                pl.BlockSpec((width, chunk), lambda j, h: (0, j)),
                pl.BlockSpec((EXTRA, chunk), lambda j, h: (0, j)),
            ],
        ),
        out_shape=[
            jax.ShapeDtypeStruct((width, count * chunk), jnp.float32),
            jax.ShapeDtypeStruct((EXTRA, count * chunk), jnp.float32),
        ],
        compiler_params=params_of(48),
        cost_estimate=pl.CostEstimate(
            flops=2 * cells * count * chunk * width, bytes_accessed=2 * cells * count * chunk, transcendentals=0
        ),
        name="outer",
    )(half, peaks, left)


def part_of(values, which, size, axis=0):
    return lax.dynamic_slice_in_dim(values, which * size, size, axis)


def across_cores(values):
    return lax.ppermute(values, "pipe", [(0, 1), (1, 0)])


def shift_of(step, index, count):
    if count & (count - 1) == 0:
        return index ^ step
    return (index + step) % count


def scatter_cells(partial):
    cells = partial.shape[0]
    pipe, mine, count = lax.axis_index("pipe"), lax.axis_index("tensor"), lax.axis_size("tensor")
    half = cells // 2
    got = across_cores(part_of(partial, 1 - pipe, half))
    chip_sum = part_of(partial, pipe, half) + got
    rows = half // count
    pieces = [part_of(chip_sum, mine, rows)]
    for step in range(1, count):
        there = shift_of(step, mine, count)
        route = [(i, shift_of(step, i, count)) for i in range(count)]
        pieces.append(lax.ppermute(part_of(chip_sum, there, rows), "tensor", route))
    return pieces


def gather_cells(own):
    pipe, mine, count = lax.axis_index("pipe"), lax.axis_index("tensor"), lax.axis_size("tensor")
    rows = own.shape[0]
    half = jnp.zeros((rows * count, own.shape[1]), own.dtype)
    half = lax.dynamic_update_slice_in_dim(half, own, mine * rows, 0)
    for step in range(1, count):
        route = [(i, shift_of(step, i, count)) for i in range(count)]
        got = lax.ppermute(own, "tensor", route)
        sender = mine ^ step if count & (count - 1) == 0 else (mine - step) % count
        half = lax.dynamic_update_slice_in_dim(half, got, sender * rows, 0)
    other = across_cores(half)
    return jnp.concatenate([jnp.where(pipe == 0, half, other), jnp.where(pipe == 0, other, half)], axis=0)


def three_terms(values):
    high = values.astype(jnp.bfloat16)
    rest = values - high.astype(jnp.float32)
    middle = rest.astype(jnp.bfloat16)
    return high, middle, (rest - middle.astype(jnp.float32)).astype(jnp.bfloat16)


def body(
    peak_data,
    region_weights,
    out_bias,
    region_factor,
    region_keep,
    cell_factor,
    batch_ids,
    latent_noise,
    enc_bias_in,
    enc_square,
    enc_bias_two,
    enc_heads,
    head_bias,
    dec_first,
    dec_bias_one,
    dec_square,
    dec_bias_two,
):
    cells, regions_local = peak_data.shape
    weight = region_weights[0]
    width = weight.shape[1]
    latent = latent_noise.shape[1]
    batches = dec_first.shape[0] - latent
    window = -(-regions_local // 256) * 128
    overlap = 2 * window - regions_local
    pipe, mine, tensors = lax.axis_index("pipe"), lax.axis_index("tensor"), lax.axis_size("tensor")
    cell_total = cells * lax.axis_size("dp")
    region_total = regions_local * tensors
    norm_scale = float(cell_total) ** (-0.5)

    def of_core(values, core, axis=0):
        return lax.dynamic_slice_in_dim(values, core * (regions_local - window), window, axis)

    kept = of_core(weight, pipe)
    got = across_cores(of_core(weight, 1 - pipe))
    w_enc = jnp.where(pipe == 0, kept, got)
    w_dec = jnp.where(pipe == 0, got, kept)
    keep = of_core(region_keep, pipe).astype(jnp.float32)
    half = jnp.reshape(pipe, (1,)).astype(jnp.int32)
    if overlap:
        mine_alone = (pipe == 0) | (jnp.arange(window) >= overlap)
        w_enc = jnp.where(mine_alone[:, None], w_enc, 0)
        keep = jnp.where(mine_alone, keep, 0.0)
        peak_data = of_core(peak_data, pipe, 1)
        half = jnp.zeros_like(half)

    own_rows = cells // (2 * tensors)
    own_at = pipe * tensors + mine
    noise_own = part_of(latent_noise, own_at, own_rows)
    ids_own = part_of(batch_ids[:, None], own_at, own_rows)
    enc = (
        enc_bias_in[None], enc_square, enc_bias_two[None], enc_heads[:, :latent], enc_heads[:, latent:],
        head_bias[None, :latent], head_bias[None, latent:],
    )
    dec = (dec_first[:latent], dec_first[latent:], dec_bias_one[None], dec_square, dec_bias_two[None])

    a = jnp.exp(of_core(out_bias, pipe))
    fa = a * of_core(region_factor, pipe)
    cf_wide = jnp.broadcast_to(cell_factor[:, None], (cells, 128))
    log_cf = jnp.log(cell_factor)

    vmem = pl.BlockSpec(memory_space=pltpu.VMEM)
    partial = project(half, peak_data, w_enc)
    pieces = scatter_cells(partial)
    summed, z_low, g2_own, kl_sum = pl.pallas_call(
        functools.partial(forward_kernel, len(pieces)),
        in_specs=[vmem] * (len(pieces) + 14),
        out_specs=[vmem] * 4,
        out_shape=[
            jax.ShapeDtypeStruct((own_rows, width), jnp.float32),
            jax.ShapeDtypeStruct((own_rows, latent), jnp.bfloat16),
            jax.ShapeDtypeStruct((own_rows, width), jnp.bfloat16),
            jax.ShapeDtypeStruct((1, 1), jnp.float32),
        ],
        compiler_params=params_of(32),
        name="small_forward",
    )(*pieces, noise_own, ids_own, *enc, *dec)
    hidden = gather_cells(g2_own)

    chunk = next(c for c in (1792, 256, 128) if window % c == 0 and (regions_local - window) % c == 0)
    chunks = window // chunk
    rows_b = min(512, cells // 2)
    hidden_t = jnp.transpose(hidden.reshape(cells // rows_b, rows_b, width), (0, 2, 1))
    ck = (keep * norm_scale)[None]
    cuts = [0, 3, 5, chunks] if chunks == 7 else [0, chunks]
    dg2 = jnp.zeros((cells, width), jnp.float32)
    dw_dec, stats = [], []
    for first, end in zip(cuts[:-1], cuts[1:]):
        dg2, dw, st = regions_pass(
            half, peak_data, w_dec, hidden, hidden_t, a[None], fa[None], ck, cf_wide, dg2, first, end - first, chunk, chunks
        )
        dw_dec.append(lax.psum_scatter(dw, "dp", scatter_dimension=0, tiled=True))
        stats.append(st)
    stats = jnp.concatenate(stats, axis=1)

    pieces = scatter_cells(dg2)
    enc_dec = enc + dec
    grads = pl.pallas_call(
        functools.partial(backward_kernel, len(pieces), norm_scale),
        in_specs=[vmem] * (len(pieces) + 16),
        out_specs=[vmem] * (1 + len(enc_dec)),
        out_shape=[jax.ShapeDtypeStruct((own_rows, width), jnp.bfloat16)]
        + [jax.ShapeDtypeStruct(w.shape, jnp.float32) for w in enc_dec],
        compiler_params=params_of(32),
        name="small_backward",
    )(*pieces, summed, z_low, noise_own, ids_own, *enc, *dec)
    dp_low = gather_cells(grads[0])

    ones = jnp.ones((1, cells), jnp.bfloat16)
    logs = [t[None] for t in three_terms(log_cf)]
    left = jnp.concatenate(
        [jnp.transpose(dp_low), ones, *logs, jnp.zeros((EXTRA - 4, cells), jnp.bfloat16)], axis=0
    )
    dw_enc, extra = outer(half, peak_data, left, 0, chunks, chunk, chunks)
    dw_enc = lax.psum_scatter(dw_enc, "dp", scatter_dimension=0, tiled=True)
    dw_dec = jnp.concatenate(dw_dec, axis=1)

    give = jnp.where(pipe == 0, dw_dec, dw_enc)
    hold = jnp.where(pipe == 0, dw_enc, dw_dec)
    taken = across_cores(give)
    region_grad = jnp.concatenate(
        [jnp.where(pipe == 0, hold, taken), jnp.where(pipe == 0, taken, hold)[:, overlap:]], axis=1
    )
    region_grad = jnp.transpose(region_grad)[None]

    bias_half = jnp.sum(stats[:8], axis=0)
    bias_grad = lax.dynamic_update_slice_in_dim(
        jnp.zeros((regions_local,), jnp.float32), bias_half, pipe * (regions_local - window), 0
    )
    bias_grad = lax.psum(bias_grad, ("pipe", "dp"))

    seen, seen_log = extra[0], extra[1] + extra[2] + extra[3]
    per_region = LN2 * jnp.sum(stats[8:], axis=0) + seen * (BIG_BITS * LN2 - jnp.log(fa)) - seen_log
    loss = jnp.sum(keep * per_region) + kl_sum[0, 0]
    small = lax.psum((*grads[1:], loss), ("pipe", "dp", "tensor"))
    (d_bias_in, d_square, d_bias_two, d_mean_w, d_var_w, d_mean_b, d_var_b, d_first_z, d_first_b, d_bias_one, d_dec_square,
     d_dec_bias_two, loss_total) = small
    mean_loss = loss_total / (cell_total * region_total)
    return (
        region_grad,
        bias_grad,
        d_bias_in[0],
        d_square,
        d_bias_two[0],
        jnp.concatenate([d_mean_w, d_var_w], axis=1),
        jnp.concatenate([d_mean_b[0], d_var_b[0]], axis=0),
        jnp.concatenate([d_first_z, d_first_b], axis=0),
        d_bias_one[0],
        d_dec_square,
        d_dec_bias_two[0],
        mean_loss,
    )


def solution(mesh):
    in_specs = (
        P("dp", "tensor"),
        P("pipe", "tensor", None),
        P("tensor"),
        P("tensor"),
        P("tensor"),
        P("dp"),
        P("dp"),
        P("dp", None),
        *[P()] * 9,
    )
    out_specs = (P("pipe", "tensor", "dp"), P("tensor"), *[P()] * 10)
    return jax.shard_map(body, mesh=mesh, in_specs=in_specs, out_specs=out_specs, check_vma=False)
```

time: 1180 us -> 566 us (0.48)
  waiting for transfers between devices: 868 us -> 297 us
  Pallas kernels: 0 us -> 151 us
  matrix products: 134 us -> 0 us
  loops' own time: 39.1 us -> 0 us
  other arithmetic: 47.3 us -> 13.8 us
    psum x6 -> x2, waiting for transfers between devices: 656 us -> 131 us  [the longest x1 131 us: body(): small = lax.psum((*grads[1:], loss), ('pipe', 'dp', 'tensor'))]
    pallas_call x0 -> x7, Pallas kernels: none -> 151 us  [the longest x3 99.9 us: regions_pass(): pl.pallas_call(functools.partial(regions_kernel, tile, rows, piece), grid...]
    dot_general x40 -> x0, matrix products: 134 us -> none  [the longest x4 59.3 us: branch(): lax.dot_general(rows_of(peak_data, earlier), pulled[0].astype(jnp.bfloat1...]
    reduce_scatter x1 -> x4, waiting for transfers between devices: 208 us -> 137 us  [the longest x1 113 us: body(): dw_enc = lax.psum_scatter(dw_enc, 'dp', scatter_dimension=0, tiled=True)]
    add x12 -> x2, other arithmetic: 28.7 us -> 0.11 us  [scatter_cells(): chip_sum = part_of(partial, pipe, half) + got]
    another operation x8 -> x0, loops' own time: 25.5 us -> none  [the longest x6 24.8 us: body(): lax.cond(is_encoder, encoder_first(moment, kept), decoder_first(moment),...]
    ppermute x5 -> x18, waiting for transfers between devices: 3.83 us -> 28.4 us  [the longest x6 12.7 us: scatter_cells(): pieces.append(lax.ppermute(part_of(chip_sum, there, rows), 'tensor', route))]
    reduce_sum x44 -> x2, other arithmetic: 15 us -> 0.9 us  [the longest x1 0.7 us: body(): loss = jnp.sum(keep * per_region) + kl_sum[0, 0]]
  transfers between devices with their start and end apart: 12 -> 24, of which waited for: 11 -> 17; matrix products, arithmetic and copies ran while one was open for 2% -> 3% of each run, Pallas kernels for 0% -> 15%
where the time goes in v1:
time: 566 us
  waiting for transfers between devices  297 us (52%)
  Pallas kernels  151 us (27%)
  blocking collectives  43.5 us (8%)
  local copies, waits for them, and re-layouts  22.8 us (4%)
  between operations  19.1 us (3%)
  starting transfers between devices  18.5 us (3%)
  other arithmetic  13.8 us (2%)
    psum x1, waiting for transfers between devices, body(): small = lax.psum((*grads[1:], loss), ('pipe', 'dp', 'tensor'))  131 us
    reduce_scatter x1, waiting for transfers between devices, body(): dw_enc = lax.psum_scatter(dw_enc, 'dp', scatter_dimension=0, tiled=True)  113 us
    pallas_call x3, Pallas kernels, regions_pass(): pl.pallas_call(functools.partial(regions_kernel, tile, rows, piece), grid...  99.9 us
    psum x1, blocking collectives, body(): small = lax.psum((*grads[1:], loss), ('pipe', 'dp', 'tensor'))  43.5 us
    reduce_scatter x3, waiting for transfers between devices, body(): dw_dec.append(lax.psum_scatter(dw, 'dp', scatter_dimension=0, tiled=True))  24.2 us
    pallas_call x1, Pallas kernels, outer(): pl.pallas_call(outer_kernel, grid_spec=pltpu.PrefetchScalarGridSpec(num_s...  21.7 us
    pallas_call x1, Pallas kernels, project(): pl.pallas_call(project_kernel, grid_spec=pltpu.PrefetchScalarGridSpec(num...  21.1 us
    ppermute x6, waiting for transfers between devices, scatter_cells(): pieces.append(lax.ppermute(part_of(chip_sum, there, rows), 'tensor', route))  12.7 us
  transfers between devices with their start and end apart: 24, of which 17 were waited for; matrix products, arithmetic and copies ran while one was open for 3% of the time, Pallas kernels for 15%

profile of v1, /device:TPU:0, one launch (start us, length us, event | category | flops | bytes accessed | tf_op | source)
XLA Modules:
  0.0 565.6 jit_solution(637904886397289926)
XLA Ops:
  8.1 2.0 dynamic-slice_bitcast_fusion
  10.6 5.5 collective-permute-done
  16.2 4.6 bitcast_select_fusion
  20.8 21.1 %project.1 = f32[2048,128]{1,0:T(8,128)S(1)} custom-call(s32[1]{0:T(128)} %bitcast.half_ref, bf16[2048,25088]{1,0:T(8,128)(2,1)} %x_ref.9, bf16[12544,128]{1,0:T(8,128)(2,1)S(1)} %get-tuple-element.109.w_ref), custom_call_target="tpu_custom_call" | custom-call | flops 6576668672 | bytes 51380224 | tf_op jit(solution)/shard_map/project/pallas_call | solution.py:105
  44.2 2.9 collective-permute-start.2
  47.1 1.5 collective-permute-start.3
  48.7 2.3 collective-permute-done.2.refs_1_
  51.0 4.2 collective-permute-done.3.refs_2_
  55.2 2.6 small_forward.1
  57.9 1.3 collective-permute-start.5
  60.0 1.4 collective-permute-start.7
  61.5 1.0 collective-permute-done.5
  62.6 1.0 collective-permute-done.6
  63.6 1.6 collective-permute-done.7
  67.6 1.0 copy.74.g_ref
  69.5 1.4 broadcast_in_dim.71.cf_ref
  70.8 1.1 broadcast_in_dim.72.before_ref
  71.9 41.0 %regions.3 = (f32[2048,128]{1,0:T(8,128)}, f32[128,5376]{1,0:T(8,128)}, f32[16,5376]{1,0:T(8,128)}) custom-call(s32[1]{0:T(128)} %bitcast.half_ref, bf16[2048,25088]{1,0:T(8,128)(2,1)} %x_ref.9, bf16[12544,128]{1,0:T(8,128)(2,1)} %get-tuple-element.110.w_ref, bf16[2048,128]{1,0:T(8,128)(2,1)} %copy.74.g_ref, bf16[4,128,512]{2,1,0:T(8,128)(2,1)} %bitcast.50, ...), custom_call_target="tpu_custom_call" | custom-call | flops 14092861440 | bytes 22020096 | tf_op jit(solution)/shard_map/regions/pallas_call | solution.py:216
  112.9 29.5 %regions.4 = (f32[2048,128]{1,0:T(8,128)}, f32[128,3584]{1,0:T(8,128)}, f32[16,3584]{1,0:T(8,128)}) custom-call(s32[1]{0:T(128)} %bitcast.half_ref, bf16[2048,25088]{1,0:T(8,128)(2,1)} %x_ref.9, bf16[12544,128]{1,0:T(8,128)(2,1)} %get-tuple-element.110.w_ref, bf16[2048,128]{1,0:T(8,128)(2,1)} %copy.74.g_ref, bf16[4,128,512]{2,1,0:T(8,128)(2,1)} %bitcast.51, ...), custom_call_target="tpu_custom_call" | custom-call | flops 9395240960 | bytes 14680064 | tf_op jit(solution)/shard_map/regions/pallas_call | solution.py:216
  142.7 29.4 %regions.5 = (f32[2048,128]{1,0:T(8,128)}, f32[128,3584]{1,0:T(8,128)}, f32[16,3584]{1,0:T(8,128)}) custom-call(s32[1]{0:T(128)} %bitcast.half_ref, bf16[2048,25088]{1,0:T(8,128)(2,1)} %x_ref.9, bf16[12544,128]{1,0:T(8,128)(2,1)} %get-tuple-element.110.w_ref, bf16[2048,128]{1,0:T(8,128)(2,1)} %copy.74.g_ref, bf16[4,128,512]{2,1,0:T(8,128)(2,1)} %bitcast.52, ...), custom_call_target="tpu_custom_call" | custom-call | flops 9395240960 | bytes 14680064 | tf_op jit(solution)/shard_map/regions/pallas_call | solution.py:216
  172.2 1.1 copy-done.21
  173.9 1.6 collective-permute-done.9
  175.6 1.5 collective-permute-start.10
  177.6 1.5 collective-permute-start.12
  179.1 2.6 collective-permute-done.10.refs_1_
  181.7 3.7 collective-permute-done.11.refs_2_
  185.5 5.6 small_backward.1
  191.7 1.2 collective-permute-start.14
  192.9 1.8 collective-permute-start.15
  194.7 1.2 collective-permute-done.13
  196.7 1.4 collective-permute-done.15
  198.3 1.4 collective-permute-done.16
  200.2 21.7 %outer.1 = (f32[128,12544]{1,0:T(8,128)}, f32[16,12544]{1,0:T(8,128)S(1)}) custom-call(s32[1]{0:T(128)} %bitcast.half_ref, bf16[2048,25088]{1,0:T(8,128)(2,1)} %x_ref.9, bf16[144,2048]{1,0:T(8,128)(2,1)S(1)} %concatenate.29.t_ref), custom_call_target="tpu_custom_call" | custom-call | flops 6576668672 | bytes 51380224 | tf_op jit(solution)/shard_map/outer/pallas_call | solution.py:268
  222.0 0.9 copy-done.25
  223.7 1.1 constant_dynamic-update-slice_fusion.2
  224.8 1.1 constant_dynamic-update-slice_fusion.1
  225.9 24.1 %reduce-scatter.11.cloned.1.call-done = f32[32,3584]{1,0:T(8,128)} async-done(((f32[128,3584]{1,0:T(8,128)}), f32[32,3584]{1,0:T(8,128)}) %reduce-scatter.11.cloned.1.call-update) | async-done | bytes 458768 | tf_op jit(solution)/shard_map/reduce_scatter | solution.py:436
  250.0 1.0 constant_dynamic-update-slice_fusion
  251.1 113.2 %reduce-scatter.5.cloned.1.call-done = f32[32,12544]{1,0:T(8,128)} async-done(((f32[128,12544]{1,0:T(8,128)}), f32[32,12544]{1,0:T(8,128)}) %reduce-scatter.5.cloned.1.call-update) | async-done | bytes 1605648 | tf_op jit(solution)/shard_map/reduce_scatter | solution.py:459
  364.3 1.5 broadcast_select_fusion.2
  365.7 1.4 collective-permute-start.17
  371.7 43.5 %all-reduce = (f32[128]{0:T(128)}, f32[128]{0:T(128)}, f32[128,10]{1,0:T(8,128)S(1)}, f32[128,10]{1,0:T(8,128)S(1)}, f32[10]{0:T(128)S(1)}, /*index=5*/f32[10]{0...) all-reduce(f32[128]{0:T(128)S(1)} %bitcast.43, ...), channel_id=1, replica_groups=mesh['pipe'=2,'dp'=4,'tensor'=4] {'pipe','dp','tensor'}, use_global_device_ids=true, to_apply=%region_6.7 | all-reduce | flops 5653 | bytes 45224 | tf_op jit(solution)/shard_map/psum | solution.py:479
  417.8 2.3 broadcast_select_fusion.1
  420.2 1.9 maximum_bitcast_fusion
  422.1 130.8 %all-reduce.7.cloned.1.call-done = (f32[128,128]{1,0:T(8,128)}, f32[128,128]{1,0:T(8,128)}) async-done(((f32[128,128]{1,0:T(8,128)}, f32[128,128]{1,0:T(8,128)}), (f32[128,128]{1,0:T(8,128)}, f32[128,128]{1,0:T(8,128)})) %all-reduce.7.cloned.1.call-update) | async-done | bytes 131088 | tf_op jit(solution)/shard_map/psum | solution.py:479
  552.9 1.5 copy.104
  554.4 1.5 copy.105
  555.9 1.5 copy.106
  (159 shorter events, 16.6 us)
Async XLA Ops:
  8.0 34.5 %copy-start = (f32[2048,10]{0,1:T(8,128)S(1)}, f32[2048,10]{0,1:T(8,128)}, u32[]{:S(2)}) copy-start(f32[2048,10]{0,1:T(8,128)} %param.24) | copy-start | bytes 245764
  8.0 215.6 %reduce-scatter.7.cloned.1.call-start = ((), (), s32[]{:S(2)}) async-start(), calls=%async_computation.5 | async-start | bytes 3440640 | tf_op jit(solution)/shard_map/reduce_scatter | solution.py:436
  10.1 6.0 %collective-permute-start = (bf16[12544,128]{1,0:T(8,128)(2,1)S(1)}, bf16[12544,128]{1,0:T(8,128)(2,1)}, u32[]{:S(2)}, u32[]{:S(2)}) collective-permute-start(bf16[12544,128]{1,0:T(8,128)(2,1)S(1)} %dynamic-slice_bitcast_fusion), channel_id=1, source_target_pairs={{0,16},{16,0},{1,17},{17,1},{2,18},{18,2},{3,19},{19,3},{4,20},{20... | collective-permute-start | bytes 9633800 | tf_op jit(solution)/shard_map/ppermute | solution.py:299
  20.8 22.7 %copy-start.34 = (f32[128,20]{0,1:T(8,128)S(1)}, f32[128,20]{0,1:T(8,128)}, u32[]{:S(2)}) copy-start(f32[128,20]{0,1:T(8,128)} %param.28) | copy-start | bytes 30724
  20.8 23.0 %copy-start.35 = (f32[20,128]{1,0:T(8,128)S(1)}, f32[20,128]{1,0:T(8,128)}, u32[]{:S(2)}) copy-start(f32[20,128]{1,0:T(8,128)} %param.30) | copy-start | bytes 30724
  42.0 13.2 %copy-start.2 = (f32[128,128]{1,0:T(8,128)S(1)}, f32[128,128]{1,0:T(8,128)}, u32[]{:S(2)}) copy-start(f32[128,128]{1,0:T(8,128)} %refs_9_.1) | copy-start | bytes 196612
  42.0 13.2 %copy-start.3 = (f32[128,128]{1,0:T(8,128)S(1)}, f32[128,128]{1,0:T(8,128)}, u32[]{:S(2)}) copy-start(f32[128,128]{1,0:T(8,128)} %refs_18_.1) | copy-start | bytes 196612
  42.0 13.2 %copy-start.12 = (f32[128]{0:T(128)S(1)}, f32[128]{0:T(128)}, u32[]{:S(2)}) copy-start(f32[128]{0:T(128)} %param.25) | copy-start | bytes 1540
  42.0 13.2 %copy-start.14 = (f32[128]{0:T(128)S(1)}, f32[128]{0:T(128)}, u32[]{:S(2)}) copy-start(f32[128]{0:T(128)} %param.27) | copy-start | bytes 1540
  42.0 13.2 %copy-start.16 = (f32[128]{0:T(128)S(1)}, f32[128]{0:T(128)}, u32[]{:S(2)}) copy-start(f32[128]{0:T(128)} %param.31) | copy-start | bytes 1540
  42.0 13.2 %copy-start.18 = (f32[128]{0:T(128)S(1)}, f32[128]{0:T(128)}, u32[]{:S(2)}) copy-start(f32[128]{0:T(128)} %param.33) | copy-start | bytes 1540
  42.1 2.0 collective-permute-start.1
  43.8 14.0 %copy-start.4 = (f32[10,128]{1,0:T(8,128)}, f32[10,128]{1,0:T(8,128)S(1)}, u32[]{:S(2)}) copy-start(f32[10,128]{1,0:T(8,128)S(1)} %get-tuple-element.127.refs_14_.refs_16_) | copy-start | bytes 15364
  43.8 14.0 %copy-start.6 = (f32[10,128]{1,0:T(8,128)}, f32[10,128]{1,0:T(8,128)S(1)}, u32[]{:S(2)}) copy-start(f32[10,128]{1,0:T(8,128)S(1)} %get-tuple-element.128.refs_13_.refs_15_) | copy-start | bytes 15364
  44.1 21.2 %copy-start.32 = (f32[25088]{0:T(1024)S(1)}, f32[25088]{0:T(1024)}, u32[]{:S(2)}) copy-start(f32[25088]{0:T(1024)} %param.20) | copy-start | bytes 301060
  44.1 21.2 %copy-start.33 = (f32[25088]{0:T(1024)S(1)}, f32[25088]{0:T(1024)}, u32[]{:S(2)}) copy-start(f32[25088]{0:T(1024)} %param.19) | copy-start | bytes 301060
  44.1 22.6 %copy-start.28 = (s32[25088]{0:T(1024)S(1)}, s32[25088]{0:T(1024)}, u32[]{:S(2)}) copy-start(s32[25088]{0:T(1024)} %param.21) | copy-start | bytes 301060
  44.2 6.8 %collective-permute-start.2 = (f32[256,128]{1,0:T(8,128)S(1)}, f32[256,128]{1,0:T(8,128)S(1)}, u32[]{:S(2)}, u32[]{:S(2)}) collective-permute-start(f32[256,128]{1,0:T(8,128)S(1)} %get-tuple-element.123), channel_id=1, source_target_pairs={{0,1},{1,0},{2,3},{3,2},{4,5},{5,4},{6,7},{7,6},{8,9},{9,8},{10,11... | collective-permute-start | bytes 393224 | tf_op jit(solution)/shard_map/ppermute | solution.py:319
  47.1 8.1 %collective-permute-start.3 = (f32[256,128]{1,0:T(8,128)S(1)}, f32[256,128]{1,0:T(8,128)S(1)}, u32[]{:S(2)}, u32[]{:S(2)}) collective-permute-start(f32[256,128]{1,0:T(8,128)S(1)} %get-tuple-element.122), channel_id=1, source_target_pairs={{0,2},{1,3},{2,0},{3,1},{4,6},{5,7},{6,4},{7,5},{8,10},{9,11},{10,... | collective-permute-start | bytes 393224 | tf_op jit(solution)/shard_map/ppermute | solution.py:319
  48.6 6.6 %collective-permute-start.4 = (f32[256,128]{1,0:T(8,128)S(1)}, f32[256,128]{1,0:T(8,128)S(1)}, u32[]{:S(2)}, u32[]{:S(2)}) collective-permute-start(f32[256,128]{1,0:T(8,128)S(1)} %get-tuple-element.121), channel_id=1, source_target_pairs={{0,3},{1,2},{2,1},{3,0},{4,7},{5,6},{6,5},{7,4},{8,11},{9,10},{10,... | collective-permute-start | bytes 393224 | tf_op jit(solution)/shard_map/ppermute | solution.py:319
  57.9 4.6 collective-permute-start.5
  59.2 4.4 collective-permute-start.6
  60.0 5.2 collective-permute-start.7
  65.2 2.3 collective-permute-start.8
  112.9 111.9 %reduce-scatter.9.cloned.1.call-start = ((), (), s32[]{:S(2)}) async-start(), calls=%async_computation.6 | async-start | bytes 2293760 | tf_op jit(solution)/shard_map/reduce_scatter | solution.py:436
  142.4 107.6 %reduce-scatter.11.cloned.1.call-start = ((), (), s32[]{:S(2)}) async-start(), calls=%async_computation.7 | async-start | bytes 2293760 | tf_op jit(solution)/shard_map/reduce_scatter | solution.py:436
  172.1 192.1 %reduce-scatter.5.cloned.1.call-start = ((), (), s32[]{:S(2)}) async-start(), calls=%async_computation.4 | async-start | bytes 8028160 | tf_op jit(solution)/shard_map/reduce_scatter | solution.py:459
  173.3 12.1 %copy-start.9 = (f32[1,10]{1,0:T(1,128)S(1)}, f32[1,10]{1,0:T(1,128)}, u32[]{:S(2)}) copy-start(f32[1,10]{1,0:T(1,128)} %copy-done.8) | copy-start | bytes 124
  173.3 12.1 %copy-start.11 = (f32[1,10]{1,0:T(1,128)S(1)}, f32[1,10]{1,0:T(1,128)}, u32[]{:S(2)}) copy-start(f32[1,10]{1,0:T(1,128)} %copy-done.10) | copy-start | bytes 124
  173.4 12.1 %copy-start.13 = (f32[128]{0:T(128)S(1)}, f32[128]{0:T(128)}, u32[]{:S(2)}) copy-start(f32[128]{0:T(128)} %param.25) | copy-start | bytes 1540
  173.4 12.1 %copy-start.15 = (f32[128]{0:T(128)S(1)}, f32[128]{0:T(128)}, u32[]{:S(2)}) copy-start(f32[128]{0:T(128)} %param.27) | copy-start | bytes 1540
  173.4 12.1 %copy-start.17 = (f32[128]{0:T(128)S(1)}, f32[128]{0:T(128)}, u32[]{:S(2)}) copy-start(f32[128]{0:T(128)} %param.31) | copy-start | bytes 1540
  173.4 12.1 %copy-start.19 = (f32[128]{0:T(128)S(1)}, f32[128]{0:T(128)}, u32[]{:S(2)}) copy-start(f32[128]{0:T(128)} %param.33) | copy-start | bytes 1540
  173.5 2.0 collective-permute-start.9
  175.5 22.7 %copy-start.31 = (f32[2048]{0:T(1024)S(1)}, f32[2048]{0:T(1024)}, u32[]{:S(2)}) copy-start(f32[2048]{0:T(1024)} %param.22) | copy-start | bytes 24580
  175.6 6.2 %collective-permute-start.10 = (f32[256,128]{1,0:T(8,128)S(1)}, f32[256,128]{1,0:T(8,128)S(1)}, u32[]{:S(2)}, u32[]{:S(2)}) collective-permute-start(f32[256,128]{1,0:T(8,128)S(1)} %get-tuple-element.117), channel_id=1, source_target_pairs={{0,1},{1,0},{2,3},{3,2},{4,5},{5,4},{6,7},{7,6},{8,9},{9,8},{10,11... | collective-permute-start | bytes 393224 | tf_op jit(solution)/shard_map/ppermute | solution.py:319
  177.1 8.3 %collective-permute-start.11 = (f32[256,128]{1,0:T(8,128)S(1)}, f32[256,128]{1,0:T(8,128)S(1)}, u32[]{:S(2)}, u32[]{:S(2)}) collective-permute-start(f32[256,128]{1,0:T(8,128)S(1)} %get-tuple-element.116), channel_id=1, source_target_pairs={{0,2},{1,3},{2,0},{3,1},{4,6},{5,7},{6,4},{7,5},{8,10},{9,11},{10,... | collective-permute-start | bytes 393224 | tf_op jit(solution)/shard_map/ppermute | solution.py:319
  177.6 7.8 %collective-permute-start.12 = (f32[256,128]{1,0:T(8,128)S(1)}, f32[256,128]{1,0:T(8,128)S(1)}, u32[]{:S(2)}, u32[]{:S(2)}) collective-permute-start(f32[256,128]{1,0:T(8,128)S(1)} %get-tuple-element.115), channel_id=1, source_target_pairs={{0,3},{1,2},{2,1},{3,0},{4,7},{5,6},{6,5},{7,4},{8,11},{9,10},{10,... | collective-permute-start | bytes 393224 | tf_op jit(solution)/shard_map/ppermute | solution.py:319
  191.1 4.8 collective-permute-start.13
  191.7 5.0 collective-permute-start.14
  192.9 5.2 collective-permute-start.15
  198.1 1.6 collective-permute-start.16
  221.9 200.1 %all-reduce.5.cloned.1.call-start = ((), (), s32[]{:S(2)}) async-start(), calls=%async_computation.8 | async-start | bytes 204800 | tf_op jit(solution)/shard_map/psum | solution.py:474
  251.1 116.0 %copy-start.26 = (f32[16,3584]{1,0:T(8,128)S(1)}, f32[16,3584]{1,0:T(8,128)}, u32[]{:S(2)}) copy-start(f32[16,3584]{1,0:T(8,128)} %get-tuple-element.52) | copy-start | bytes 688132
  251.1 116.0 %copy-start.27 = (f32[16,3584]{1,0:T(8,128)S(1)}, f32[16,3584]{1,0:T(8,128)}, u32[]{:S(2)}) copy-start(f32[16,3584]{1,0:T(8,128)} %get-tuple-element.53) | copy-start | bytes 688132
  365.7 52.1 %collective-permute-start.17 = (f32[32,12544]{1,0:T(8,128)}, f32[32,12544]{1,0:T(8,128)}, u32[]{:S(2)}, u32[]{:S(2)}) collective-permute-start(f32[32,12544]{1,0:T(8,128)} %broadcast_select_fusion.2), channel_id=1, source_target_pairs={{0,16},{16,0},{1,17},{17,1},{2,18},{18,2},{3,19},{19,3},{4,20},{20... | collective-permute-start | bytes 4816904 | tf_op jit(solution)/shard_map/ppermute | solution.py:299
  368.8 184.1 %all-reduce.7.cloned.1.call-start = ((), (), s32[]{:S(2)}) async-start(), calls=%async_computation.9 | async-start | bytes 262144 | tf_op jit(solution)/shard_map/psum | solution.py:479
  420.1 137.2 %copy-start.1 = (f32[2048,10]{0,1:T(8,128)S(1)}, f32[2048,10]{0,1:T(8,128)}, u32[]{:S(2)}) copy-start(f32[2048,10]{0,1:T(8,128)} %param.24) | copy-start | bytes 245764
  (13 other events, 67.7 us)
Sparse Core Ops, SparseCore 0:
  113.0 54.5 reduce-scatter.6
  169.9 39.1 reduce-scatter.8
  211.4 38.5 reduce-scatter.10
  252.2 112.0 reduce-scatter.4
Sparse Core Ops, SparseCore 1:
  368.9 52.2 all-reduce.4
  428.8 124.0 all-reduce.6

commit v2 on v1

v2 whole, which is shorter than its diff:
```python
import functools

import jax
import jax.numpy as jnp
import numpy as np
from jax import lax
from jax.experimental import pallas as pl
from jax.experimental.pallas import tpu as pltpu
from jax.sharding import PartitionSpec as P

EXACT = lax.Precision.HIGHEST
NORM_EPS = 1e-05
LOG2E = float(np.log2(np.e))
LN2 = float(np.log(2.0))
BIG_BITS = 56
BIG = float(2.0**BIG_BITS)
MIB = 1 << 20
EXTRA = 16


def params_of(mib):
    return pltpu.CompilerParams(vmem_limit_bytes=mib * MIB)


def layer_norm(values):
    centred = values - jnp.mean(values, axis=-1, keepdims=True)
    return centred * lax.rsqrt(jnp.mean(centred * centred, axis=-1, keepdims=True) + NORM_EPS)


def silu(values):
    return values * jax.nn.sigmoid(values)


def mm(a, b):
    return lax.dot_general(a, b, (((1,), (0,)), ((), ())), precision=EXACT, preferred_element_type=jnp.float32)


def mm_t(a, b):
    return lax.dot_general(a, b, (((1,), (1,)), ((), ())), precision=EXACT, preferred_element_type=jnp.float32)


def encoder_small(summed, bias_in, square, bias_two, mean_w, var_w, mean_b, var_b, noise_rows):
    hidden = silu(layer_norm(summed + bias_in))
    hidden = silu(layer_norm(mm(hidden, square) + bias_two))
    average = mm_t(hidden, mean_w) + mean_b
    variance = jnp.exp(mm_t(hidden, var_w) + var_b) + 0.0001
    sample = average + jnp.sqrt(variance) * noise_rows
    kl_rows = 0.5 * jnp.sum(average * average + variance - jnp.log(variance) - 1.0, axis=1, keepdims=True)
    return (sample, jnp.sum(kl_rows, axis=0, keepdims=True))


def decoder_small(latent_rows, onehot, first_z, first_b, bias_one, square, bias_two):
    hidden = silu(layer_norm(mm(latent_rows, first_z) + mm(onehot, first_b) + bias_one))
    return silu(layer_norm(mm(hidden, square) + bias_two))


def onehot_of(ids, width):
    codes = lax.broadcasted_iota(jnp.int32, (ids.shape[0], width), 1)
    return (ids == codes).astype(jnp.float32)


def forward_kernel(count, *refs):
    parts = refs[:count]
    noise, ids = refs[count : count + 2]
    enc = [r[...] for r in refs[count + 2 : count + 9]]
    dec = [r[...] for r in refs[count + 9 : count + 14]]
    summed_out, z_out, g2_out, kl_out = refs[count + 14 :]
    summed = parts[0][...]
    for part in parts[1:]:
        summed = summed + part[...]
    sample, kl_sum = encoder_small(summed, *enc, noise[...])
    z_low = sample.astype(jnp.bfloat16)
    hidden = decoder_small(z_low.astype(jnp.float32), onehot_of(ids[...], dec[1].shape[0]), *dec)
    summed_out[...] = summed
    z_out[...] = z_low
    g2_out[...] = hidden.astype(jnp.bfloat16)
    kl_out[...] = kl_sum


def pack_places(shapes):
    places, row = [], 0
    for rows, _ in shapes:
        places.append(row)
        row += rows if rows == 1 else -(-rows // 8) * 8
    return places, -(-(row + 1) // 16) * 16


def backward_kernel(count, norm_scale, *refs):
    parts = refs[:count]
    summed, z_low, noise, ids = refs[count : count + 4]
    enc = [r[...] for r in refs[count + 4 : count + 11]]
    dec = [r[...] for r in refs[count + 11 : count + 16]]
    dp_out, pack_out = refs[count + 16 :]
    dg2 = parts[0][...]
    for part in parts[1:]:
        dg2 = dg2 + part[...]
    onehot = onehot_of(ids[...], dec[1].shape[0])
    unused, pull = jax.vjp(lambda z, *w: decoder_small(z, onehot, *w), z_low[...].astype(jnp.float32), *dec)
    dz, *dec_grads = pull(dg2)
    noise_rows = noise[...]
    unused, pull = jax.vjp(lambda s, *w: encoder_small(s, *w, noise_rows), summed[...], *enc)
    dz_low = dz.astype(jnp.bfloat16).astype(jnp.float32)
    dp, *enc_grads = pull((dz_low, jnp.full((1, 1), norm_scale, jnp.float32)))
    dp_out[...] = dp.astype(jnp.bfloat16)
    pack_out[...] = jnp.zeros_like(pack_out)
    grads = ordered(enc_grads + dec_grads)
    for row, grad in zip(pack_places([g.shape for g in grads])[0], grads):
        pack_out[row : row + grad.shape[0], : grad.shape[1]] = grad


def ordered(values):
    return [v for v in values if v.shape[0] > 1] + [v for v in values if v.shape[0] == 1]


STRIP = 16
TOP = 32767.0


def coded_rows(share, chunk):
    return chunk // 256 * share + STRIP


def code(values, out_ref, base, tile, share, strip):
    largest = jnp.maximum(jnp.max(jnp.abs(values), axis=0, keepdims=True), 1e-30)
    level = jnp.ceil(jnp.log2(largest) * 64.0 + 0.01)
    scaled = values * (TOP * jnp.exp2(level * (-1.0 / 64.0)))
    at = base + tile * share
    out_ref[at : at + share, :] = jnp.floor(scaled + 0.5).astype(jnp.int32).astype(jnp.int16)
    row = lax.broadcasted_iota(jnp.int32, (STRIP, 256), 0)
    return jnp.where(row == tile, level, strip)


def code_all(parts, out_ref, base, share):
    strip = jnp.zeros((STRIP, 256), jnp.float32)
    for tile, values in enumerate(parts):
        strip = code(values, out_ref, base, tile, share, strip)
    at = base + len(parts) * share
    out_ref[at : at + STRIP, :] = strip.astype(jnp.int32).astype(jnp.int16)


def decode(in_ref, base, tiles, share, tile):
    at = base + tiles * share
    level = in_ref[at : at + STRIP, :].astype(jnp.int32).astype(jnp.float32)[tile : tile + 1, :]
    at = base + tile * share
    values = in_ref[at : at + share, :].astype(jnp.int32).astype(jnp.float32)
    return values * (jnp.exp2(level * (1.0 / 64.0)) * (1.0 / TOP))


def give_shares(z, dw_ref, sent_ref, own_ref, other_ref):
    share, chunk = own_ref.shape

    def rows(which):
        return pl.ds(pl.multiple_of(which * share, 16), share)

    for place, which in enumerate((z ^ 1, z ^ 3)):
        parts = [dw_ref[rows(which), c : c + 256] for c in range(0, chunk, 256)]
        code_all(parts, sent_ref, place * coded_rows(share, chunk), share)
    own_ref[...] = dw_ref[rows(z), :]
    other_ref[...] = dw_ref[rows(z ^ 2), :]


def share_outputs(width, chunk, count, coded):
    if not coded:
        return [pl.BlockSpec((width, chunk), lambda j, h: (0, j))], [jax.ShapeDtypeStruct((width, count * chunk), jnp.float32)]
    share = width // 4
    rows = 2 * coded_rows(share, chunk)
    specs = [pl.BlockSpec((rows, 256), lambda j, h: (j, 0))] + [pl.BlockSpec((share, chunk), lambda j, h: (0, j))] * 2
    shapes = [jax.ShapeDtypeStruct((count * rows, 256), jnp.int16)]
    return specs, shapes + [jax.ShapeDtypeStruct((share, count * chunk), jnp.float32)] * 2


def join_kernel(got_ref, own_ref, other_ref, sent_ref, sum_ref, *, chunk):
    share, width = own_ref.shape
    tiles, rows = chunk // 256, coded_rows(share, chunk)
    for j in range(width // chunk):
        parts = []
        for tile in range(tiles):
            cols = slice(j * chunk + tile * 256, j * chunk + tile * 256 + 256)
            sum_ref[:, cols] = own_ref[:, cols] + decode(got_ref, 2 * j * rows, tiles, share, tile)
            parts.append(other_ref[:, cols] + decode(got_ref, (2 * j + 1) * rows, tiles, share, tile))
        code_all(parts, sent_ref, j * rows, share)


def total_kernel(sum_ref, got_ref, out_ref, *, chunk):
    share, width = sum_ref.shape
    tiles, rows = chunk // 256, coded_rows(share, chunk)
    for j in range(width // chunk):
        for tile in range(tiles):
            cols = slice(j * chunk + tile * 256, j * chunk + tile * 256 + 256)
            out_ref[:, cols] = sum_ref[:, cols] + decode(got_ref, j * rows, tiles, share, tile)


def line_call(kernel, args, out_shape, name):
    vmem = pl.BlockSpec(memory_space=pltpu.VMEM)
    return pl.pallas_call(
        kernel,
        in_specs=[vmem] * len(args),
        out_specs=[vmem] * len(out_shape),
        out_shape=out_shape,
        compiler_params=params_of(48),
        name=name,
    )(*args)


def line_start(pieces):
    if len(pieces) == 1:
        return [lax.psum_scatter(pieces[0], "dp", scatter_dimension=0, tiled=True)]
    return [lax.ppermute(pieces[0], "dp", [(i, i ^ 1) for i in range(4)]), *pieces[1:]]


def line_joined(state, chunk):
    if len(state) == 1:
        return state
    got, own, other = state
    sent = jax.ShapeDtypeStruct((got.shape[0] // 2, 256), jnp.int16)
    kernel = functools.partial(join_kernel, chunk=chunk)
    return line_call(kernel, state, [sent, jax.ShapeDtypeStruct(own.shape, jnp.float32)], "join")


def line_last(state):
    if len(state) == 1:
        return state
    return [lax.ppermute(state[0], "dp", [(i, i ^ 2) for i in range(4)]), state[1]]


def line_end(state, chunk):
    if len(state) == 1:
        return state[0]
    got, own = state
    kernel = functools.partial(total_kernel, chunk=chunk)
    return line_call(kernel, [own, got], [jax.ShapeDtypeStruct(own.shape, jnp.float32)], "total")[0]


def after(value, *others):
    return lax.optimization_barrier((value, *others))[0]


def chosen(core, encoder, kept_ref, got_ref):
    own = core == (0 if encoder else 1)
    return jnp.where(own, kept_ref[...], got_ref[...])


def project_kernel(started, half_ref, x_ref, kept_ref, got_ref, *refs):
    out_ref = refs[-1]
    size = x_ref.shape[0]
    rows = pl.ds(pl.multiple_of(pl.program_id(1) * size, 16), size)
    part = jnp.dot(x_ref[...], chosen(half_ref[1], True, kept_ref, got_ref), preferred_element_type=jnp.float32)

    @pl.when(pl.program_id(0) == 0)
    def first():
        out_ref[rows, :] = part + refs[0][rows, :] if started else part

    @pl.when(pl.program_id(0) != 0)
    def later():
        out_ref[rows, :] += part


def project(half, peaks, kept, got, before, first, got_first, count, chunk, per_half):
    cells, width = peaks.shape[0], kept.shape[1]
    started = before is not None
    whole = pl.BlockSpec((cells, width), lambda j, i, h: (0, 0))
    return pl.pallas_call(
        functools.partial(project_kernel, started),
        grid_spec=pltpu.PrefetchScalarGridSpec(
            num_scalar_prefetch=1,
            grid=(count, 2),
            in_specs=[
                pl.BlockSpec((cells // 2, chunk), lambda j, i, h: (i, h[0] * per_half + first + j)),
                pl.BlockSpec((chunk, width), lambda j, i, h: (h[0] * per_half + first + j, 0)),
                pl.BlockSpec((chunk, width), lambda j, i, h: (got_first + j, 0)),
            ]
            + [whole] * started,
            out_specs=whole,
        ),
        out_shape=jax.ShapeDtypeStruct((cells, width), jnp.float32),
        compiler_params=params_of(48),
        cost_estimate=pl.CostEstimate(
            flops=2 * cells * count * chunk * width, bytes_accessed=2 * cells * count * chunk, transcendentals=0
        ),
        name="project",
    )(half, peaks, kept, got, *([before] if started else []))


def regions_kernel(
    tile, rows_at_once, piece, started, coded, half_ref, x_ref, kept_ref, got_ref, g_ref, gt_ref, a_ref, fa_ref, ck_ref, cf_ref,
    *refs,
):
    outs = refs[1 if started else 0 :]
    dg_ref, st_ref = outs[:2]
    m0, m1, e0, e1, w_ref, dw_ref = outs[-6:] if coded else (*outs[3:], outs[2])
    cells, chunk = x_ref.shape
    blocks = cells // rows_at_once
    M, E = (m0, m1), (e0, e1)

    w_ref[...] = chosen(half_ref[1], False, kept_ref, got_ref)

    @pl.when(pl.program_id(0) == 0)
    def first():
        dg_ref[...] = refs[0][...] if started else jnp.zeros_like(dg_ref)

    def one_tile(t, carry):
        cols = pl.ds(pl.multiple_of(t * tile, 128), tile)
        w = w_ref[cols, :]
        w2 = jnp.concatenate([w, w], axis=1)
        wide = (8, tile)
        a = jnp.broadcast_to(a_ref[:, cols], wide)[None]
        fa = jnp.broadcast_to(fa_ref[:, cols], wide)[None]
        ck = jnp.broadcast_to(ck_ref[:, cols], wide)[None]

        def rows(i, o=0, n=rows_at_once):
            return pl.ds(pl.multiple_of(i * rows_at_once + o, 16), n)

        def logit(i, s, o, n):
            M[s][o : o + n, :] = lax.dot_general(
                g_ref[rows(i, o, n), :], w2, (((1,), (1,)), ((), ())), preferred_element_type=jnp.float32
            )

        def elementwise(i, s, o, sums):
            e_sum, l_sum = sums
            shape = (piece // 8, 8, tile)
            u = jnp.exp2(M[s][o : o + piece, :]).reshape(shape)
            cf = cf_ref[rows(i, o, piece), :]
            cf = jnp.concatenate([cf] * (tile // 128), axis=1).reshape(shape)
            seen = (x_ref[rows(i, o, piece), cols] * jnp.bfloat16(BIG)).astype(jnp.float32).reshape(shape)
            total = u + a
            rest = (total - fa * cf) + seen
            d = pltpu.reciprocal(rest, approx=True)
            slope = (u * ck) * (d - pltpu.reciprocal(total, approx=True))
            ratio = (d * total).reshape(piece // 16, 2, 8, tile)
            E[s][o : o + piece, :] = slope.reshape(piece, tile).astype(jnp.bfloat16)
            e_sum = e_sum + jnp.sum(slope, axis=0)
            l_sum = l_sum + jnp.sum(jnp.log2(ratio[:, 0] * ratio[:, 1]), axis=0)
            return e_sum, l_sum

        def cell_grad(i, s):
            dg_ref[rows(i), :] += jnp.dot(E[s][...], w, preferred_element_type=jnp.float32)

        def region_grad(i, s, start=False):
            part = jnp.dot(gt_ref[i], E[s][...], preferred_element_type=jnp.float32)
            if start:
                dw_ref[:, cols] = part
            else:
                dw_ref[:, cols] += part

        def step(i, s, sums, logits=True, grads=True, start=False):
            dots = rows_at_once // 2
            for o in range(0, rows_at_once, piece):
                if logits and o % dots == 0:
                    logit(i + 1, 1 - s, o, dots)
                sums = elementwise(i, s, o, sums)
                if grads and o == dots:
                    cell_grad(i - 1, 1 - s)
            if grads:
                region_grad(i - 1, 1 - s, start)
            return sums

        zero = jnp.zeros(wide, jnp.float32)
        sums = (zero, zero)
        logit(0, 0, 0, rows_at_once)
        sums = step(0, 0, sums, grads=False)
        for i in range(1, blocks):
            sums = step(i, i % 2, sums, logits=i < blocks - 1, start=i == 1)
        cell_grad(blocks - 1, (blocks - 1) % 2)
        region_grad(blocks - 1, (blocks - 1) % 2, blocks == 1)
        st_ref[0:8, cols] = sums[0]
        st_ref[8:16, cols] = sums[1]
        return carry

    lax.fori_loop(0, chunk // tile, one_tile, 0)
    if coded:
        give_shares(half_ref[2], dw_ref, *outs[2:5])


def regions_pass(half, peaks, kept, got, hidden, hidden_t, a, fa, ck, cf, before, first, at, count, chunk, per_half, coded):
    cells, width = peaks.shape[0], kept.shape[1]
    blocks, _, rows = hidden_t.shape
    tile, piece = min(256, chunk), 64
    started = before is not None
    whole = pl.BlockSpec((cells, width), lambda j, h: (0, 0))
    row = pl.BlockSpec((1, chunk), lambda j, h: (0, first + j))
    share_specs, share_shapes = share_outputs(width, chunk, count, coded)
    return pl.pallas_call(
        functools.partial(regions_kernel, tile, rows, piece, started, coded),
        grid_spec=pltpu.PrefetchScalarGridSpec(
            num_scalar_prefetch=1,
            grid=(count,),
            in_specs=[
                pl.BlockSpec((cells, chunk), lambda j, h: (0, h[0] * per_half + first + j)),
                pl.BlockSpec((chunk, width), lambda j, h: (h[0] * per_half + first + j, 0)),
                pl.BlockSpec((chunk, width), lambda j, h: (at + j, 0)),
                pl.BlockSpec((cells, 2 * width), lambda j, h: (0, 0)),
                pl.BlockSpec((blocks, width, rows), lambda j, h: (0, 0, 0)),
                row, row, row, whole,
            ]
            + [whole] * started,
            out_specs=[whole, pl.BlockSpec((16, chunk), lambda j, h: (0, j)), *share_specs],
            scratch_shapes=[pltpu.VMEM((rows, tile), jnp.float32)] * 2
            + [pltpu.VMEM((rows, tile), jnp.bfloat16)] * 2
            + [pltpu.VMEM((chunk, width), jnp.bfloat16)]
            + [pltpu.VMEM((width, chunk), jnp.float32)] * coded,
        ),
        out_shape=[
            jax.ShapeDtypeStruct((cells, width), jnp.float32),
            jax.ShapeDtypeStruct((16, count * chunk), jnp.float32),
            *share_shapes,
        ],
        compiler_params=params_of(56),
        cost_estimate=pl.CostEstimate(
            flops=10 * cells * count * chunk * width,
            bytes_accessed=2 * cells * count * chunk,
            transcendentals=16 * cells * count * chunk,
        ),
        name="regions",
    )(half, peaks, kept, got, hidden, hidden_t, a, fa, ck, cf, *([before] if started else []))


def outer_kernel(coded, half_ref, x_ref, left_ref, extra_ref, *outs):
    dw_ref = outs[-1] if coded else outs[0]
    width = dw_ref.shape[0]
    tile = min(256, x_ref.shape[1])
    for c in range(0, x_ref.shape[1], tile):
        cols = slice(c, c + tile)
        part = jnp.dot(left_ref[...], x_ref[:, cols], preferred_element_type=jnp.float32)
        dw_ref[:, cols] = part[:width]
        extra_ref[:, cols] = part[width:]
    if coded:
        give_shares(half_ref[2], dw_ref, *outs[:3])


def outer(half, peaks, left, first, count, chunk, per_half, coded):
    cells = peaks.shape[0]
    width = left.shape[0] - EXTRA
    share_specs, share_shapes = share_outputs(width, chunk, count, coded)
    return pl.pallas_call(
        functools.partial(outer_kernel, coded),
        grid_spec=pltpu.PrefetchScalarGridSpec(
            num_scalar_prefetch=1,
            grid=(count,),
            in_specs=[
                pl.BlockSpec((cells, chunk), lambda j, h: (0, h[0] * per_half + first + j)),
                pl.BlockSpec((width + EXTRA, cells), lambda j, h: (0, 0)),
            ],
            out_specs=[pl.BlockSpec((EXTRA, chunk), lambda j, h: (0, j)), *share_specs],
            scratch_shapes=[pltpu.VMEM((width, chunk), jnp.float32)] * coded,
        ),
        out_shape=[jax.ShapeDtypeStruct((EXTRA, count * chunk), jnp.float32), *share_shapes],
        compiler_params=params_of(48),
        cost_estimate=pl.CostEstimate(
            flops=2 * cells * count * chunk * width, bytes_accessed=2 * cells * count * chunk, transcendentals=0
        ),
        name="outer",
    )(half, peaks, left)


def part_of(values, which, size, axis=0):
    return lax.dynamic_slice_in_dim(values, which * size, size, axis)


def across_cores(values):
    return lax.ppermute(values, "pipe", [(0, 1), (1, 0)])


def shift_of(step, index, count):
    if count & (count - 1) == 0:
        return index ^ step
    return (index + step) % count


def scatter_cells(partial):
    cells = partial.shape[0]
    pipe, mine, count = lax.axis_index("pipe"), lax.axis_index("tensor"), lax.axis_size("tensor")
    half = cells // 2
    got = across_cores(part_of(partial, 1 - pipe, half))
    chip_sum = part_of(partial, pipe, half) + got
    rows = half // count
    pieces = [part_of(chip_sum, mine, rows)]
    for step in range(1, count):
        there = shift_of(step, mine, count)
        route = [(i, shift_of(step, i, count)) for i in range(count)]
        pieces.append(lax.ppermute(part_of(chip_sum, there, rows), "tensor", route))
    return pieces


def gather_cells(own):
    count = lax.axis_size("tensor")
    pieces = [own]
    for step in range(1, count):
        route = [(i, shift_of(step, i, count)) for i in range(count)]
        pieces.append(lax.ppermute(own, "tensor", route))
    return pieces + [across_cores(piece) for piece in pieces]


def rows_at(place_ref, index, count, rows):
    core, mine = place_ref[0], place_ref[1]
    step = index % count
    if count & (count - 1) == 0:
        sender = mine ^ step
    else:
        sender = lax.rem(mine - step + count, jnp.int32(count))
    here = core if index < count else 1 - core
    return (here * count + sender) * rows


def hidden_kernel(count, place_ref, *refs):
    pieces, (wide_ref, turned_ref, all_s) = refs[:-3], refs[-3:]
    rows, width = pieces[0].shape
    for index, piece in enumerate(pieces):
        at = pl.ds(pl.multiple_of(rows_at(place_ref, index, count, rows), 16), rows)
        all_s[at, :] = piece[...].astype(jnp.float32)
    scaled = all_s[...] * (-LOG2E)
    high = scaled.astype(jnp.bfloat16)
    wide_ref[:, :width] = high
    wide_ref[:, width:] = (scaled - high.astype(jnp.float32)).astype(jnp.bfloat16)
    size = turned_ref.shape[2]
    for block in range(turned_ref.shape[0]):
        turned_ref[block] = jnp.transpose(all_s[block * size : (block + 1) * size, :]).astype(jnp.bfloat16)


def left_kernel(count, place_ref, log_ref, *refs):
    pieces, (left_ref, all_s) = refs[:-2], refs[-2:]
    rows, width = pieces[0].shape
    for index, piece in enumerate(pieces):
        at = pl.ds(pl.multiple_of(rows_at(place_ref, index, count, rows), 16), rows)
        all_s[at, :] = piece[...].astype(jnp.float32)
    left_ref[:width, :] = jnp.transpose(all_s[...]).astype(jnp.bfloat16)
    left_ref[width:, :] = log_ref[...]


def assemble(kernel, place, pieces, before, out_shape, name):
    vmem = pl.BlockSpec(memory_space=pltpu.VMEM)
    rows, width = pieces[0].shape
    return pl.pallas_call(
        functools.partial(kernel, len(pieces) // 2),
        in_specs=[pl.BlockSpec(memory_space=pltpu.SMEM)] + [vmem] * (len(before) + len(pieces)),
        out_specs=[vmem] * len(out_shape),
        out_shape=out_shape,
        scratch_shapes=[pltpu.VMEM((rows * len(pieces), width), jnp.float32)],
        compiler_params=params_of(32),
        name=name,
    )(place, *before, *pieces)


def exchange_bits(axis):
    count = lax.axis_size(axis)
    return [1 << i for i in range((count - 1).bit_length())]


def exchanged(values, axis, bit):
    count = lax.axis_size(axis)
    return values + lax.ppermute(values, axis, [(i, i ^ bit) for i in range(count)])


def all_sum(values, axes):
    for axis in axes:
        for bit in exchange_bits(axis):
            values = exchanged(values, axis, bit)
    return values


def join_cores(own):
    other = across_cores(own)
    first = lax.axis_index("pipe") == 0
    return jnp.where(first, own, other), jnp.where(first, other, own)


def three_terms(values):
    high = values.astype(jnp.bfloat16)
    rest = values - high.astype(jnp.float32)
    middle = rest.astype(jnp.bfloat16)
    return high, middle, (rest - middle.astype(jnp.float32)).astype(jnp.bfloat16)


def body(
    peak_data,
    region_weights,
    out_bias,
    region_factor,
    region_keep,
    cell_factor,
    batch_ids,
    latent_noise,
    enc_bias_in,
    enc_square,
    enc_bias_two,
    enc_heads,
    head_bias,
    dec_first,
    dec_bias_one,
    dec_square,
    dec_bias_two,
):
    cells, regions_local = peak_data.shape
    weight = region_weights[0]
    width = weight.shape[1]
    latent = latent_noise.shape[1]
    batches = dec_first.shape[0] - latent
    window = -(-regions_local // 256) * 128
    overlap = 2 * window - regions_local
    pipe, mine, tensors = lax.axis_index("pipe"), lax.axis_index("tensor"), lax.axis_size("tensor")
    cell_total = cells * lax.axis_size("dp")
    region_total = regions_local * tensors
    norm_scale = float(cell_total) ** (-0.5)

    def of_core(values, core, axis=0):
        return lax.dynamic_slice_in_dim(values, core * (regions_local - window), window, axis)

    keep = of_core(region_keep, pipe).astype(jnp.float32)
    dp_at = lax.axis_index("dp")
    place = jnp.stack([pipe, mine, dp_at]).astype(jnp.int32)
    chunk = next(c for c in (1792, 256, 128) if window % c == 0 and (regions_local - window) % c == 0)
    chunks = window // chunk
    ahead = min(2, chunks - 1) * chunk
    coded = lax.axis_size("dp") == 4 and chunk % 256 == 0
    if overlap:
        mine_alone = (pipe == 0) | (jnp.arange(window) >= overlap)
        keep = jnp.where(mine_alone, keep, 0.0)
        peak_data = of_core(peak_data, pipe, 1)
        own = of_core(weight, pipe)
        got = across_cores(of_core(weight, 1 - pipe))
        kept_enc = got_enc = jnp.where(mine_alone[:, None], jnp.where(pipe == 0, own, got), 0)
        weight = jnp.where(pipe == 0, got, own)
        got_spans = [(weight, 0, 0, chunks)]
        got_parts = [(kept_enc, got_enc, 0, 0, chunks)]
        half = jnp.stack([jnp.zeros_like(place[0]), place[0], place[2]])
    else:
        other_at = (1 - pipe) * (regions_local - window)
        got_first = across_cores(lax.dynamic_slice_in_dim(weight, other_at, ahead, 0))
        got_rest = across_cores(lax.dynamic_slice_in_dim(weight, other_at + ahead, window - ahead, 0))
        got_parts = [(weight, got_first, 0, 0, ahead // chunk), (weight, got_rest, ahead // chunk, 0, chunks - ahead // chunk)]
        cut = ahead // chunk
        middle = cut + (chunks - cut + 1) // 2
        got_spans = [(got_first, 0, 0, cut), (got_rest, 0, cut, middle), (got_rest, middle - cut, middle, chunks)]
        half = jnp.stack([place[0], place[0], place[2]])

    own_rows = cells // (2 * tensors)
    own_at = pipe * tensors + mine
    noise_own = part_of(latent_noise, own_at, own_rows)
    ids_own = part_of(batch_ids[:, None], own_at, own_rows)
    heads_t = jnp.transpose(enc_heads)
    enc = (
        enc_bias_in[None], enc_square, enc_bias_two[None], heads_t[:latent], heads_t[latent:],
        head_bias[None, :latent], head_bias[None, latent:],
    )
    dec = (dec_first[:latent], dec_first[latent:], dec_bias_one[None], dec_square, dec_bias_two[None])

    a = jnp.exp(of_core(out_bias, pipe))[None]
    fa = a * of_core(region_factor, pipe)[None]
    ck = (keep * norm_scale)[None]
    cf_wide = jnp.broadcast_to(cell_factor[:, None], (cells, 128))
    logs = jnp.concatenate(
        [jnp.ones((1, cells), jnp.bfloat16)]
        + [t[None] for t in three_terms(jnp.log(cell_factor))]
        + [jnp.zeros((EXTRA - 4, cells), jnp.bfloat16)],
        axis=0,
    )
    early = (noise_own, ids_own, enc, dec, a, fa, ck, cf_wide, logs)
    kept_first, got_first, *span = got_parts[0]
    got_first, early = lax.optimization_barrier((got_first, early))
    noise_own, ids_own, enc, dec, a, fa, ck, cf_wide, logs = early
    got_parts[0] = (kept_first, got_first, *span)

    vmem = pl.BlockSpec(memory_space=pltpu.VMEM)
    partial = None
    for kept_w, got_w, first, at, count in got_parts:
        partial = project(half, peak_data, kept_w, got_w, partial, first, at, count, chunk, chunks)
    pieces = scatter_cells(partial)
    summed, z_low, g2_own, kl_sum = pl.pallas_call(
        functools.partial(forward_kernel, len(pieces)),
        in_specs=[vmem] * (len(pieces) + 14),
        out_specs=[vmem] * 4,
        out_shape=[
            jax.ShapeDtypeStruct((own_rows, width), jnp.float32),
            jax.ShapeDtypeStruct((own_rows, latent), jnp.bfloat16),
            jax.ShapeDtypeStruct((own_rows, width), jnp.bfloat16),
            jax.ShapeDtypeStruct((1, 1), jnp.float32),
        ],
        compiler_params=params_of(32),
        name="small_forward",
    )(*pieces, noise_own, ids_own, *enc, *dec)
    rows_b = min(512, cells // 2)
    hidden, hidden_t = assemble(
        hidden_kernel, place, gather_cells(g2_own), [],
        [
            jax.ShapeDtypeStruct((cells, 2 * width), jnp.bfloat16),
            jax.ShapeDtypeStruct((cells // rows_b, width, rows_b), jnp.bfloat16),
        ],
        "hidden",
    )

    dg2, lines, stats = None, [], []
    for got_w, at, first, end in got_spans:
        if len(lines) > 1:
            lines[-2] = line_joined(lines[-2], chunk)
            dg2 = after(dg2, *lines[-2])
            lines[-2] = line_last(lines[-2])
        dg2, st, *shares = regions_pass(
            half, peak_data, weight, got_w, hidden, hidden_t, a, fa, ck, cf_wide, dg2, first, at, end - first, chunk,
            chunks, coded,
        )
        lines.append(line_start(shares))
        stats.append(st)
    stats = jnp.concatenate(stats, axis=1)

    if len(lines) > 1:
        lines[-2] = line_last(line_joined(lines[-2], chunk))
    pieces = scatter_cells(dg2)
    grad_shapes = [w.shape for w in ordered(enc + dec)]
    places, pack_rows = pack_places(grad_shapes)
    dp_own, pack = pl.pallas_call(
        functools.partial(backward_kernel, len(pieces), norm_scale),
        in_specs=[vmem] * (len(pieces) + 16),
        out_specs=[vmem] * 2,
        out_shape=[
            jax.ShapeDtypeStruct((own_rows, width), jnp.bfloat16),
            jax.ShapeDtypeStruct((pack_rows, width), jnp.float32),
        ],
        compiler_params=params_of(32),
        name="small_backward",
    )(*pieces, summed, z_low, noise_own, ids_own, *enc, *dec)
    (left,) = assemble(
        left_kernel, place, gather_cells(dp_own), [logs],
        [jax.ShapeDtypeStruct((width + EXTRA, cells), jnp.bfloat16)],
        "left",
    )
    cuts = [0, 2, 5, chunks] if chunks == 7 else [0, chunks]
    extras, enc_lines = [], []
    under_way = [(lines, lines.pop())]
    for first, end in zip(cuts[:-1], cuts[1:]):
        if first:
            where, line = under_way.pop(0)
            line = line_joined(line, chunk)
            left = after(left, line[0])
            where.append(line_last(line))
        extra, *shares = outer(half, peak_data, left, first, end - first, chunk, chunks, coded)
        under_way.append((enc_lines, line_start(shares)))
        extras.append(extra)
    extra = jnp.concatenate(extras, axis=1)
    newest = under_way[-1][1][0]
    joined = []
    for where, line in under_way:
        line = line_joined(line, chunk)
        joined.append(line[0])
        where.append(line_last(line))

    dec_own = [line_end(line, chunk) for line in lines]
    dec_got = [lax.ppermute(share, "pipe", [(0, 1)]) for share in dec_own]
    enc_own = [line_end(line, chunk) for line in enc_lines]
    enc_got = [lax.ppermute(share, "pipe", [(1, 0)]) for share in enc_own]
    is_first = pipe == 0
    lower = jnp.where(is_first, jnp.concatenate(enc_own, axis=1), jnp.concatenate(dec_got, axis=1))
    upper = jnp.where(is_first, jnp.concatenate(enc_got, axis=1), jnp.concatenate(dec_own, axis=1))
    region_grad = jnp.transpose(jnp.concatenate([lower, upper[:, overlap:]], axis=1))[None]

    seen, seen_log = extra[0], extra[1] + extra[2] + extra[3]
    per_region = LN2 * jnp.sum(stats[8:], axis=0) + seen * (BIG_BITS * LN2 - jnp.log(fa[0])) - seen_log
    loss = jnp.sum(keep * per_region) + kl_sum[0, 0]
    pack = pack.at[pack_rows - 1, 0].set(loss)
    pack_half = pack_rows // 2
    pack = part_of(pack, pipe, pack_half) + across_cores(part_of(pack, 1 - pipe, pack_half))
    pack = all_sum(after(pack, newest, joined[0]), ["tensor"])
    sums = jnp.concatenate([pack, jnp.sum(stats[:8], axis=0).reshape(-1, 128)], axis=0)
    sums = after(sums, joined[-1])
    for bit in exchange_bits("dp"):
        if bit > 1:
            sums = after(sums, enc_lines[-1][0])
        sums = exchanged(sums, "dp", bit)
    lower, upper = join_cores(sums)
    pack = jnp.concatenate([lower[:pack_half], upper[:pack_half]], axis=0)
    bias_grad = jnp.concatenate([lower[pack_half:].reshape(-1), upper[pack_half:].reshape(-1)[overlap:]])
    small = {}
    shapes = list(enumerate(w.shape for w in enc + dec))
    named = [s for s in shapes if s[1][0] > 1] + [s for s in shapes if s[1][0] == 1]
    for row, (index, shape) in zip(places, named):
        small[index] = pack[row : row + shape[0], : shape[1]]
    (d_bias_in, d_square, d_bias_two, d_mean_w, d_var_w, d_mean_b, d_var_b, d_first_z, d_first_b, d_bias_one, d_dec_square,
     d_dec_bias_two) = [small[i] for i in range(len(small))]
    mean_loss = pack[pack_rows - 1, 0] / (cell_total * region_total)
    return (
        region_grad,
        bias_grad,
        d_bias_in[0],
        d_square,
        d_bias_two[0],
        jnp.transpose(jnp.concatenate([d_mean_w, d_var_w], axis=0)),
        jnp.concatenate([d_mean_b[0], d_var_b[0]], axis=0),
        jnp.concatenate([d_first_z, d_first_b], axis=0),
        d_bias_one[0],
        d_dec_square,
        d_dec_bias_two[0],
        mean_loss,
    )


def solution(mesh):
    in_specs = (
        P("dp", "tensor"),
        P("pipe", "tensor", None),
        P("tensor"),
        P("tensor"),
        P("tensor"),
        P("dp"),
        P("dp"),
        P("dp", None),
        *[P()] * 9,
    )
    out_specs = (P("pipe", "tensor", "dp"), P("tensor"), *[P()] * 10)
    return jax.shard_map(body, mesh=mesh, in_specs=in_specs, out_specs=out_specs, check_vma=False)
```

time: 566 us -> 359 us (0.63)
  waiting for transfers between devices: 297 us -> 85 us
  blocking collectives: 43.5 us -> 0 us
  starting transfers between devices: 18.5 us -> 47.3 us
  Pallas kernels: 151 us -> 175 us
  between operations: 19.1 us -> 4.67 us
  local copies, waits for them, and re-layouts: 22.8 us -> 33 us
    reduce_scatter x4 -> x0, waiting for transfers between devices: 137 us -> none  [the longest x1 113 us: body(): dw_enc = lax.psum_scatter(dw_enc, 'dp', scatter_dimension=0, tiled=True)]
    psum x2 -> x0, waiting for transfers between devices: 131 us -> none  [the longest x1 131 us: body(): small = lax.psum((*grads[1:], loss), ('pipe', 'dp', 'tensor'))]
    ppermute x6 -> x28, waiting for transfers between devices: 6.99 us -> 68.4 us  [the longest x6 46.6 us: line_last(): lax.ppermute(state[0], 'dp', [(i, i ^ 2) for i in range(4)])]
    psum x1 -> x0, blocking collectives: 43.5 us -> none  [body(): small = lax.psum((*grads[1:], loss), ('pipe', 'dp', 'tensor'))]
    ppermute x6 -> x28, starting transfers between devices: 7.11 us -> 36.8 us  [the longest x6 8.52 us: line_last(): lax.ppermute(state[0], 'dp', [(i, i ^ 2) for i in range(4)])]
    pallas_call x5 -> x22, Pallas kernels: 143 us -> 167 us  [the longest x3 104 us: regions_pass(): pl.pallas_call(functools.partial(regions_kernel, tile, rows, piece, start...]
    select_n x5 -> x3, other arithmetic: 8.51 us -> 1.71 us  [the longest x1 1.53 us: body(): jnp.where(is_first, jnp.concatenate(enc_own, axis=1), jnp.concatenate(dec...]
    unnamed x84 -> x138, local copies, waits for them, and re-layouts: 10.7 us -> 13 us
  transfers between devices with their start and end apart: 24 -> 48, of which waited for: 17 -> 21; matrix products, arithmetic and copies ran while one was open for 3% -> 7% of each run, Pallas kernels for 15% -> 25%
where the time goes in v2:
time: 359 us; the launch traced here: 358 us
  Pallas kernels  175 us (49%)
  waiting for transfers between devices  85 us (24%)
  starting transfers between devices  47.3 us (13%)
  local copies, waits for them, and re-layouts  33 us (9%)
  other arithmetic  13.8 us (4%)
  between operations  4.67 us (1%)
    pallas_call x3, Pallas kernels, regions_pass(): pl.pallas_call(functools.partial(regions_kernel, tile, rows, piece, start...  104 us
    ppermute x6, waiting for transfers between devices, line_last(): lax.ppermute(state[0], 'dp', [(i, i ^ 2) for i in range(4)])  46.6 us
    pallas_call x2, Pallas kernels, project(): pl.pallas_call(functools.partial(project_kernel, started), grid_spec=pltp...  27.6 us
    pallas_call x3, Pallas kernels, outer(): pl.pallas_call(functools.partial(outer_kernel, coded), grid_spec=pltpu.Pr...  26.2 us
    unnamed x138, local copies, waits for them, and re-layouts  13 us
    ppermute x6, waiting for transfers between devices, scatter_cells(): pieces.append(lax.ppermute(part_of(chip_sum, there, rows), 'tensor', route))  11.9 us
    ppermute x6, waiting for transfers between devices, line_start(): lax.ppermute(pieces[0], 'dp', [(i, i ^ 1) for i in range(4)])  11.1 us
    ppermute x6, starting transfers between devices, line_last(): lax.ppermute(state[0], 'dp', [(i, i ^ 2) for i in range(4)])  8.52 us
  transfers between devices with their start and end apart: 48, of which 21 were waited for; matrix products, arithmetic and copies ran while one was open for 7% of the time, Pallas kernels for 25%

profile of v2, /device:TPU:0, one launch (start us, length us, event | category | flops | bytes accessed | tf_op | source)
XLA Modules:
  0.0 358.2 jit_solution(4823135726992010028)
XLA Ops:
  0.7 2.8 dynamic-slice_bitcast_fusion
  3.9 2.2 dynamic-slice_bitcast_fusion.1
  12.4 1.4 fusion.5
  13.8 2.0 broadcast_in_dim.58.cf_ref
  15.8 8.5 %project.2.refs_0_ = f32[2048,128]{1,0:T(8,128)S(1)} custom-call(s32[3]{0:T(128)S(1)} %add_add_fusion.half_ref, bf16[2048,25088]{1,0:T(8,128)(2,1)} %x_ref.15, bf16[25088,128]{1,0:T(8,128)(2,1)} %bitcast.52, bf16[3584,128]{1,0:T(8,128)(2,1)S(1)} %collective-permute-done.got_ref), custom_call_target="tpu_custom_call" | custom-call | flops 1879048192 | bytes 14680064 | tf_op jit(solution)/shard_map/project/pallas_call | solution.py:262
  24.4 19.1 %project.3 = f32[2048,128]{1,0:T(8,128)S(1)} custom-call(s32[3]{0:T(128)S(1)} %add_add_fusion.half_ref, bf16[2048,25088]{1,0:T(8,128)(2,1)} %x_ref.15, bf16[25088,128]{1,0:T(8,128)(2,1)} %bitcast.53, bf16[8960,128]{1,0:T(8,128)(2,1)S(1)} %collective-permute-done.1.got_ref, f32[2048,128]{1,0:T(8,128)S(1)} %project.2.refs_0_), custom_call_target="tpu_custom_call" | custom-call | flops 4697620480 | bytes 36700160 | tf_op jit(solution)/shard_map/project/pallas_call | solution.py:262
  44.9 1.7 collective-permute-done.2
  46.8 3.0 collective-permute-start.3
  49.7 1.5 collective-permute-start.4
  51.4 2.2 collective-permute-done.3.refs_1_
  53.6 4.2 %collective-permute-done.4.refs_2_ = f32[256,128]{1,0:T(8,128)S(1)} collective-permute-done((f32[256,128]{1,0:T(8,128)S(1)}, f32[256,128]{1,0:T(8,128)S(1)}, u32[]{:S(2)}, u32[]{:S(2)}) %collective-permute-start.4) | collective-permute-done | bytes 131104 | tf_op jit(solution)/shard_map/ppermute | solution.py:480
  57.9 2.8 small_forward.1
  62.7 1.4 collective-permute-start.8
  66.3 1.6 collective-permute-done.8.refs_3_
  72.1 30.1 %regions.3 = (f32[2048,128]{1,0:T(8,128)}, f32[16,3584]{1,0:T(8,128)}, s16[960,256]{1,0:T(8,128)(2,1)}, f32[32,3584]{1,0:T(8,128)}, f32[32,3584]{1,0:T(8,128)}) custom-call(s32[3]{0:T(128)} %copy-done.37, bf16[2048,25088]{1,0:T(8,128)(2,1)} %x_ref.15, bf16[25088,128]{1,0:T(8,128)(2,1)} %bitcast.54, bf16[3584,128]{1,0:T(8,128)(2,1)} %copy-done.3, ...), custom_call_target="tpu_custom_call" | custom-call | flops 9395240960 | bytes 14680064 | tf_op jit(solution)/shard_map/regions/pallas_call | solution.py:382
  102.3 1.6 collective-permute-start.13
  103.9 42.6 %regions.4 = (f32[2048,128]{1,0:T(8,128)}, f32[16,5376]{1,0:T(8,128)}, s16[1440,256]{1,0:T(8,128)(2,1)}, f32[32,5376]{1,0:T(8,128)}, f32[32,5376]{1,0:T(8,128)}) custom-call(s32[3]{0:T(128)} %copy-done.37, bf16[2048,25088]{1,0:T(8,128)(2,1)} %x_ref.15, bf16[25088,128]{1,0:T(8,128)(2,1)} %bitcast.55, bf16[8960,128]{1,0:T(8,128)(2,1)} %copy-done.2, ...), custom_call_target="tpu_custom_call" | custom-call | flops 14092861440 | bytes 22020096 | tf_op jit(solution)/shard_map/regions/pallas_call | solution.py:382
  148.3 30.9 %regions.5 = (f32[2048,128]{1,0:T(8,128)}, f32[16,3584]{1,0:T(8,128)}, s16[960,256]{1,0:T(8,128)(2,1)}, f32[32,3584]{1,0:T(8,128)}, f32[32,3584]{1,0:T(8,128)}) custom-call(s32[3]{0:T(128)} %copy-done.37, bf16[2048,25088]{1,0:T(8,128)(2,1)} %x_ref.15, bf16[25088,128]{1,0:T(8,128)(2,1)} %bitcast.56, bf16[8960,128]{1,0:T(8,128)(2,1)} %copy-done.2, ...), custom_call_target="tpu_custom_call" | custom-call | flops 9395240960 | bytes 14680064 | tf_op jit(solution)/shard_map/regions/pallas_call | solution.py:382
  180.5 1.7 collective-permute-done.14
  183.4 1.6 collective-permute-start.15
  185.5 1.5 collective-permute-start.17
  187.6 1.7 collective-permute-done.15.refs_1_
  189.4 3.8 %collective-permute-done.16.refs_2_ = f32[256,128]{1,0:T(8,128)S(1)} collective-permute-done((f32[256,128]{1,0:T(8,128)S(1)}, f32[256,128]{1,0:T(8,128)S(1)}, u32[]{:S(2)}, u32[]{:S(2)}) %collective-permute-start.16) | collective-permute-done | bytes 131104 | tf_op jit(solution)/shard_map/ppermute | solution.py:480
  193.2 4.8 %small_backward.1 = (bf16[256,128]{1,0:T(8,128)(2,1)S(1)}, f32[336,128]{1,0:T(8,128)S(1)}) custom-call(f32[256,128]{1,0:T(8,128)S(1)} %get-tuple-element.177.refs_0_, f32[256,128]{1,0:T(8,128)S(1)} %collective-permute-done.15.refs_1_, f32[256,128]{1,0:T(8,128)S(1)} %collective-permute-done.16.refs_2_, f32[256,128]{1,0:T(8,128)S(1)} %collective-permute-done.17.refs_3_, ...), custom_call_target="tpu_custom_call" | custom-call | tf_op jit(solution)/shard_map/small_backward/pallas_call | solution.py:709
  199.8 1.8 collective-permute-start.20
  203.5 1.5 collective-permute-done.20.refs_3_
  209.0 7.3 %outer.3 = (f32[16,3584]{1,0:T(8,128)S(1)}, s16[960,256]{1,0:T(8,128)(2,1)S(1)}, f32[32,3584]{1,0:T(8,128)S(1)}, f32[32,3584]{1,0:T(8,128)S(1)}) custom-call(s32[3]{0:T(128)S(1)} %copy-done.38, bf16[2048,25088]{1,0:T(8,128)(2,1)} %x_ref.15, bf16[144,2048]{1,0:T(8,128)(2,1)S(1)} %left.1.left_ref), custom_call_target="tpu_custom_call" | custom-call | flops 1879048192 | bytes 14680064 | tf_op jit(solution)/shard_map/outer/pallas_call | solution.py:434
  216.3 1.7 collective-permute-start.25
  218.0 10.7 %outer.4 = (f32[16,5376]{1,0:T(8,128)S(1)}, s16[1440,256]{1,0:T(8,128)(2,1)}, f32[32,5376]{1,0:T(8,128)S(1)}, f32[32,5376]{1,0:T(8,128)S(1)}) custom-call(s32[3]{0:T(128)S(1)} %copy-done.38, bf16[2048,25088]{1,0:T(8,128)(2,1)} %x_ref.15, bf16[144,2048]{1,0:T(8,128)(2,1)S(1)} %left.1.left_ref), custom_call_target="tpu_custom_call" | custom-call | flops 2818572288 | bytes 22020096 | tf_op jit(solution)/shard_map/outer/pallas_call | solution.py:434
  230.0 5.8 %collective-permute-done.25.got_ref = s16[960,256]{1,0:T(8,128)(2,1)S(1)} collective-permute-done((s16[960,256]{1,0:T(8,128)(2,1)S(1)}, s16[960,256]{1,0:T(8,128)(2,1)S(1)}, u32[]{:S(2)}, u32[]{:S(2)}) %collective-permute-start.25) | collective-permute-done | bytes 491552 | tf_op jit(solution)/shard_map/ppermute | solution.py:208
  237.7 8.3 %outer.5 = (f32[16,3584]{1,0:T(8,128)S(1)}, s16[960,256]{1,0:T(8,128)(2,1)}, f32[32,3584]{1,0:T(8,128)S(1)}, f32[32,3584]{1,0:T(8,128)S(1)}) custom-call(s32[3]{0:T(128)S(1)} %copy-done.38, bf16[2048,25088]{1,0:T(8,128)(2,1)} %x_ref.15, bf16[144,2048]{1,0:T(8,128)(2,1)S(1)} %left.1.left_ref), custom_call_target="tpu_custom_call" | custom-call | flops 1879048192 | bytes 14680064 | tf_op jit(solution)/shard_map/outer/pallas_call | solution.py:434
  251.6 1.5 constant_dynamic-slice_fusion
  255.2 2.6 collective-permute-start.35
  261.1 5.2 %collective-permute-done.30.got_ref = s16[960,256]{1,0:T(8,128)(2,1)} collective-permute-done((s16[960,256]{1,0:T(8,128)(2,1)}, s16[960,256]{1,0:T(8,128)(2,1)}, u32[]{:S(2)}, u32[]{:S(2)}) %collective-permute-start.30) | collective-permute-done | bytes 491552 | tf_op jit(solution)/shard_map/ppermute | solution.py:208
  267.1 3.7 %collective-permute-done.43 = f32[168,128]{1,0:T(8,128)S(1)} collective-permute-done((f32[168,128]{1,0:T(8,128)S(1)}, f32[168,128]{1,0:T(8,128)S(1)}, u32[]{:S(2)}, u32[]{:S(2)}) %collective-permute-start.43) | collective-permute-done | bytes 86048 | tf_op jit(solution)/shard_map/ppermute | solution.py:550
  271.7 2.9 collective-permute-start.37
  274.6 11.6 %collective-permute-done.35.got_ref = s16[720,256]{1,0:T(8,128)(2,1)S(1)} collective-permute-done((s16[720,256]{1,0:T(8,128)(2,1)}, s16[720,256]{1,0:T(8,128)(2,1)S(1)}, u32[]{:S(2)}, u32[]{:S(2)}) %collective-permute-start.35) | collective-permute-done | bytes 368672 | tf_op jit(solution)/shard_map/ppermute | solution.py:223
  288.1 2.3 collective-permute-start.36
  291.8 4.1 %collective-permute-start.45 = (f32[266,128]{1,0:T(8,128)S(1)}, f32[266,128]{1,0:T(8,128)S(1)}, u32[]{:S(2)}, u32[]{:S(2)}) collective-permute-start(f32[266,128]{1,0:T(8,128)S(1)} %pad_maximum_fusion), channel_id=1, source_target_pairs={{0,4},{4,0},{8,12},{12,8},{1,5},{5,1},{9,13},{13,9},{2,6},{6,2},{1... | collective-permute-start | bytes 408584 | tf_op jit(solution)/shard_map/ppermute | solution.py:550
  296.1 2.1 collective-permute-start.33
  298.1 3.9 %collective-permute-done.37.got_ref = s16[480,256]{1,0:T(8,128)(2,1)S(1)} collective-permute-done((s16[480,256]{1,0:T(8,128)(2,1)}, s16[480,256]{1,0:T(8,128)(2,1)S(1)}, u32[]{:S(2)}, u32[]{:S(2)}) %collective-permute-start.37) | collective-permute-done | bytes 245792 | tf_op jit(solution)/shard_map/ppermute | solution.py:223
  302.1 2.1 collective-permute-start.38
  304.1 2.7 collective-permute-done.31.got_ref
  306.9 2.9 collective-permute-start.29
  310.5 19.1 %collective-permute-done.26.got_ref = s16[480,256]{1,0:T(8,128)(2,1)S(1)} collective-permute-done((s16[480,256]{1,0:T(8,128)(2,1)S(1)}, s16[480,256]{1,0:T(8,128)(2,1)S(1)}, u32[]{:S(2)}, u32[]{:S(2)}) %collective-permute-start.26) | collective-permute-done | bytes 245792 | tf_op jit(solution)/shard_map/ppermute | solution.py:223
  331.3 9.3 %collective-permute-done.29.got_ref = s16[720,256]{1,0:T(8,128)(2,1)} collective-permute-done((s16[720,256]{1,0:T(8,128)(2,1)}, s16[720,256]{1,0:T(8,128)(2,1)}, u32[]{:S(2)}, u32[]{:S(2)}) %collective-permute-start.29) | collective-permute-done | bytes 368672 | tf_op jit(solution)/shard_map/ppermute | solution.py:223
  347.9 1.5 maximum_select_fusion
  355.2 1.9 maximum_bitcast_fusion
  (271 shorter events, 62.3 us)
Async XLA Ops:
  3.4 20.9 %collective-permute-start.1 = (bf16[8960,128]{1,0:T(8,128)(2,1)}, bf16[8960,128]{1,0:T(8,128)(2,1)S(1)}, u32[]{:S(2)}, u32[]{:S(2)}) collective-permute-start(bf16[8960,128]{1,0:T(8,128)(2,1)} %dynamic-slice_bitcast_fusion), channel_id=1, source_target_pairs={{0,16},{16,0},{1,17},{17,1},{2,18},{18,2},{3,19},{19,3},{4,20},{20... | collective-permute-start | bytes 6881288 | tf_op jit(solution)/shard_map/ppermute | solution.py:460
  6.0 7.8 %collective-permute-start = (bf16[3584,128]{1,0:T(8,128)(2,1)}, bf16[3584,128]{1,0:T(8,128)(2,1)S(1)}, u32[]{:S(2)}, u32[]{:S(2)}) collective-permute-start(bf16[3584,128]{1,0:T(8,128)(2,1)} %dynamic-slice_bitcast_fusion.1), channel_id=1, source_target_pairs={{0,16},{16,0},{1,17},{17,1},{2,18},{18,2},{3,19},{19,3},{4,20},{20... | collective-permute-start | bytes 2752520 | tf_op jit(solution)/shard_map/ppermute | solution.py:460
  44.4 2.2 collective-permute-start.2
  46.8 6.9 %collective-permute-start.3 = (f32[256,128]{1,0:T(8,128)S(1)}, f32[256,128]{1,0:T(8,128)S(1)}, u32[]{:S(2)}, u32[]{:S(2)}) collective-permute-start(f32[256,128]{1,0:T(8,128)S(1)} %get-tuple-element.180), channel_id=1, source_target_pairs={{0,1},{1,0},{2,3},{3,2},{4,5},{5,4},{6,7},{7,6},{8,9},{9,8},{10,11... | collective-permute-start | bytes 393224 | tf_op jit(solution)/shard_map/ppermute | solution.py:480
  49.7 8.1 %collective-permute-start.4 = (f32[256,128]{1,0:T(8,128)S(1)}, f32[256,128]{1,0:T(8,128)S(1)}, u32[]{:S(2)}, u32[]{:S(2)}) collective-permute-start(f32[256,128]{1,0:T(8,128)S(1)} %get-tuple-element.179), channel_id=1, source_target_pairs={{0,2},{1,3},{2,0},{3,1},{4,6},{5,7},{6,4},{7,5},{8,10},{9,11},{10,... | collective-permute-start | bytes 393224 | tf_op jit(solution)/shard_map/ppermute | solution.py:480
  51.2 6.6 %collective-permute-start.5 = (f32[256,128]{1,0:T(8,128)S(1)}, f32[256,128]{1,0:T(8,128)S(1)}, u32[]{:S(2)}, u32[]{:S(2)}) collective-permute-start(f32[256,128]{1,0:T(8,128)S(1)} %get-tuple-element.178), channel_id=1, source_target_pairs={{0,3},{1,2},{2,1},{3,0},{4,7},{5,6},{6,5},{7,4},{8,11},{9,10},{10,... | collective-permute-start | bytes 393224 | tf_op jit(solution)/shard_map/ppermute | solution.py:480
  60.7 4.6 %collective-permute-start.6 = (bf16[256,128]{1,0:T(8,128)(2,1)S(1)}, bf16[256,128]{1,0:T(8,128)(2,1)S(1)}, u32[]{:S(2)}, u32[]{:S(2)}) collective-permute-start(bf16[256,128]{1,0:T(8,128)(2,1)S(1)} %get-tuple-element.113.refs_0_), channel_id=1, source_target_pairs={{0,1},{1,0},{2,3},{3,2},{4,5},{5,4},{6,7},{7,6},{8,9},{9,8},{10,11... | collective-permute-start | bytes 196616 | tf_op jit(solution)/shard_map/ppermute | solution.py:489
  61.9 4.4 %collective-permute-start.7 = (bf16[256,128]{1,0:T(8,128)(2,1)S(1)}, bf16[256,128]{1,0:T(8,128)(2,1)S(1)}, u32[]{:S(2)}, u32[]{:S(2)}) collective-permute-start(bf16[256,128]{1,0:T(8,128)(2,1)S(1)} %get-tuple-element.113.refs_0_), channel_id=1, source_target_pairs={{0,2},{1,3},{2,0},{3,1},{4,6},{5,7},{6,4},{7,5},{8,10},{9,11},{10,... | collective-permute-start | bytes 196616 | tf_op jit(solution)/shard_map/ppermute | solution.py:489
  62.7 5.2 %collective-permute-start.8 = (bf16[256,128]{1,0:T(8,128)(2,1)S(1)}, bf16[256,128]{1,0:T(8,128)(2,1)S(1)}, u32[]{:S(2)}, u32[]{:S(2)}) collective-permute-start(bf16[256,128]{1,0:T(8,128)(2,1)S(1)} %get-tuple-element.113.refs_0_), channel_id=1, source_target_pairs={{0,3},{1,2},{2,1},{3,0},{4,7},{5,6},{6,5},{7,4},{8,11},{9,10},{10,... | collective-permute-start | bytes 196616 | tf_op jit(solution)/shard_map/ppermute | solution.py:489
  64.2 3.8 %collective-permute-start.9 = (bf16[256,128]{1,0:T(8,128)(2,1)S(1)}, bf16[256,128]{1,0:T(8,128)(2,1)S(1)}, u32[]{:S(2)}, u32[]{:S(2)}) collective-permute-start(bf16[256,128]{1,0:T(8,128)(2,1)S(1)} %get-tuple-element.113.refs_0_), channel_id=1, source_target_pairs={{0,16},{16,0},{1,17},{17,1},{2,18},{18,2},{3,19},{19,3},{4,20},{20... | collective-permute-start | bytes 196616 | tf_op jit(solution)/shard_map/ppermute | solution.py:460
  65.3 2.7 collective-permute-start.10
  66.3 1.7 collective-permute-start.11
  67.9 1.3 collective-permute-start.12
  102.3 44.2 %collective-permute-start.13 = (s16[960,256]{1,0:T(8,128)(2,1)}, s16[960,256]{1,0:T(8,128)(2,1)S(1)}, u32[]{:S(2)}, u32[]{:S(2)}) collective-permute-start(s16[960,256]{1,0:T(8,128)(2,1)} %get-tuple-element.122), channel_id=1, source_target_pairs={{0,4},{4,0},{8,12},{12,8},{1,5},{5,1},{9,13},{13,9},{2,6},{6,2},{1... | collective-permute-start | bytes 1474568 | tf_op jit(solution)/shard_map/ppermute | solution.py:208
  180.3 2.0 collective-permute-start.14
  183.4 5.9 %collective-permute-start.15 = (f32[256,128]{1,0:T(8,128)S(1)}, f32[256,128]{1,0:T(8,128)S(1)}, u32[]{:S(2)}, u32[]{:S(2)}) collective-permute-start(f32[256,128]{1,0:T(8,128)S(1)} %get-tuple-element.176), channel_id=1, source_target_pairs={{0,1},{1,0},{2,3},{3,2},{4,5},{5,4},{6,7},{7,6},{8,9},{9,8},{10,11... | collective-permute-start | bytes 393224 | tf_op jit(solution)/shard_map/ppermute | solution.py:480
  185.0 8.1 %collective-permute-start.16 = (f32[256,128]{1,0:T(8,128)S(1)}, f32[256,128]{1,0:T(8,128)S(1)}, u32[]{:S(2)}, u32[]{:S(2)}) collective-permute-start(f32[256,128]{1,0:T(8,128)S(1)} %get-tuple-element.175), channel_id=1, source_target_pairs={{0,2},{1,3},{2,0},{3,1},{4,6},{5,7},{6,4},{7,5},{8,10},{9,11},{10,... | collective-permute-start | bytes 393224 | tf_op jit(solution)/shard_map/ppermute | solution.py:480
  185.5 7.6 %collective-permute-start.17 = (f32[256,128]{1,0:T(8,128)S(1)}, f32[256,128]{1,0:T(8,128)S(1)}, u32[]{:S(2)}, u32[]{:S(2)}) collective-permute-start(f32[256,128]{1,0:T(8,128)S(1)} %get-tuple-element.174), channel_id=1, source_target_pairs={{0,3},{1,2},{2,1},{3,0},{4,7},{5,6},{6,5},{7,4},{8,11},{9,10},{10,... | collective-permute-start | bytes 393224 | tf_op jit(solution)/shard_map/ppermute | solution.py:480
  187.0 18.8 %collective-permute-start.27 = (s16[960,256]{1,0:T(8,128)(2,1)S(1)}, s16[960,256]{1,0:T(8,128)(2,1)S(1)}, u32[]{:S(2)}, u32[]{:S(2)}) collective-permute-start(s16[960,256]{1,0:T(8,128)(2,1)S(1)} %copy-done.66), channel_id=1, source_target_pairs={{0,4},{4,0},{8,12},{12,8},{1,5},{5,1},{9,13},{13,9},{2,6},{6,2},{1... | collective-permute-start | bytes 1474568 | tf_op jit(solution)/shard_map/ppermute | solution.py:208
  198.0 4.6 %collective-permute-start.18 = (bf16[256,128]{1,0:T(8,128)(2,1)S(1)}, bf16[256,128]{1,0:T(8,128)(2,1)S(1)}, u32[]{:S(2)}, u32[]{:S(2)}) collective-permute-start(bf16[256,128]{1,0:T(8,128)(2,1)S(1)} %get-tuple-element.131.refs_0_), channel_id=1, source_target_pairs={{0,1},{1,0},{2,3},{3,2},{4,5},{5,4},{6,7},{7,6},{8,9},{9,8},{10,11... | collective-permute-start | bytes 196616 | tf_op jit(solution)/shard_map/ppermute | solution.py:489
  198.6 4.9 %collective-permute-start.19 = (bf16[256,128]{1,0:T(8,128)(2,1)S(1)}, bf16[256,128]{1,0:T(8,128)(2,1)S(1)}, u32[]{:S(2)}, u32[]{:S(2)}) collective-permute-start(bf16[256,128]{1,0:T(8,128)(2,1)S(1)} %get-tuple-element.131.refs_0_), channel_id=1, source_target_pairs={{0,2},{1,3},{2,0},{3,1},{4,6},{5,7},{6,4},{7,5},{8,10},{9,11},{10,... | collective-permute-start | bytes 196616 | tf_op jit(solution)/shard_map/ppermute | solution.py:489
  199.8 5.2 %collective-permute-start.20 = (bf16[256,128]{1,0:T(8,128)(2,1)S(1)}, bf16[256,128]{1,0:T(8,128)(2,1)S(1)}, u32[]{:S(2)}, u32[]{:S(2)}) collective-permute-start(bf16[256,128]{1,0:T(8,128)(2,1)S(1)} %get-tuple-element.131.refs_0_), channel_id=1, source_target_pairs={{0,3},{1,2},{2,1},{3,0},{4,7},{5,6},{6,5},{7,4},{8,11},{9,10},{10,... | collective-permute-start | bytes 196616 | tf_op jit(solution)/shard_map/ppermute | solution.py:489
  201.6 6.5 %collective-permute-start.21 = (bf16[256,128]{1,0:T(8,128)(2,1)S(1)}, bf16[256,128]{1,0:T(8,128)(2,1)S(1)}, u32[]{:S(2)}, u32[]{:S(2)}) collective-permute-start(bf16[256,128]{1,0:T(8,128)(2,1)S(1)} %get-tuple-element.131.refs_0_), channel_id=1, source_target_pairs={{0,16},{16,0},{1,17},{17,1},{2,18},{18,2},{3,19},{19,3},{4,20},{20... | collective-permute-start | bytes 196616 | tf_op jit(solution)/shard_map/ppermute | solution.py:460
  202.6 5.6 %collective-permute-start.22 = (bf16[256,128]{1,0:T(8,128)(2,1)S(1)}, bf16[256,128]{1,0:T(8,128)(2,1)S(1)}, u32[]{:S(2)}, u32[]{:S(2)}) collective-permute-start(bf16[256,128]{1,0:T(8,128)(2,1)S(1)} %collective-permute-done.18.refs_1_), channel_id=1, source_target_pairs={{0,16},{16,0},{1,17},{17,1},{2,18},{18,2},{3,19},{19,3},{4,20},{20... | collective-permute-start | bytes 196616 | tf_op jit(solution)/shard_map/ppermute | solution.py:460
  203.5 4.7 %collective-permute-start.23 = (bf16[256,128]{1,0:T(8,128)(2,1)S(1)}, bf16[256,128]{1,0:T(8,128)(2,1)S(1)}, u32[]{:S(2)}, u32[]{:S(2)}) collective-permute-start(bf16[256,128]{1,0:T(8,128)(2,1)S(1)} %collective-permute-done.19.refs_2_), channel_id=1, source_target_pairs={{0,16},{16,0},{1,17},{17,1},{2,18},{18,2},{3,19},{19,3},{4,20},{20... | collective-permute-start | bytes 196616 | tf_op jit(solution)/shard_map/ppermute | solution.py:460
  205.0 3.2 collective-permute-start.24
  205.8 47.3 %collective-permute-start.34 = (s16[1440,256]{1,0:T(8,128)(2,1)}, s16[1440,256]{1,0:T(8,128)(2,1)S(1)}, u32[]{:S(2)}, u32[]{:S(2)}) collective-permute-start(s16[1440,256]{1,0:T(8,128)(2,1)} %get-tuple-element.153), channel_id=1, source_target_pairs={{0,4},{4,0},{8,12},{12,8},{1,5},{5,1},{9,13},{13,9},{2,6},{6,2},{1... | collective-permute-start | bytes 2211848 | tf_op jit(solution)/shard_map/ppermute | solution.py:208
  216.3 19.5 %collective-permute-start.25 = (s16[960,256]{1,0:T(8,128)(2,1)S(1)}, s16[960,256]{1,0:T(8,128)(2,1)S(1)}, u32[]{:S(2)}, u32[]{:S(2)}) collective-permute-start(s16[960,256]{1,0:T(8,128)(2,1)S(1)} %get-tuple-element.132), channel_id=1, source_target_pairs={{0,4},{4,0},{8,12},{12,8},{1,5},{5,1},{9,13},{13,9},{2,6},{6,2},{1... | collective-permute-start | bytes 1474568 | tf_op jit(solution)/shard_map/ppermute | solution.py:208
  229.5 29.3 %collective-permute-start.28 = (s16[1440,256]{1,0:T(8,128)(2,1)}, s16[1440,256]{1,0:T(8,128)(2,1)S(1)}, u32[]{:S(2)}, u32[]{:S(2)}) collective-permute-start(s16[1440,256]{1,0:T(8,128)(2,1)} %get-tuple-element.142), channel_id=1, source_target_pairs={{0,4},{4,0},{8,12},{12,8},{1,5},{5,1},{9,13},{13,9},{2,6},{6,2},{1... | collective-permute-start | bytes 2211848 | tf_op jit(solution)/shard_map/ppermute | solution.py:208
  247.6 18.8 %collective-permute-start.30 = (s16[960,256]{1,0:T(8,128)(2,1)}, s16[960,256]{1,0:T(8,128)(2,1)}, u32[]{:S(2)}, u32[]{:S(2)}) collective-permute-start(s16[960,256]{1,0:T(8,128)(2,1)} %get-tuple-element.148), channel_id=1, source_target_pairs={{0,4},{4,0},{8,12},{12,8},{1,5},{5,1},{9,13},{13,9},{2,6},{6,2},{1... | collective-permute-start | bytes 1474568 | tf_op jit(solution)/shard_map/ppermute | solution.py:208
  253.2 4.7 %collective-permute-start.42 = (f32[168,128]{1,0:T(8,128)}, f32[168,128]{1,0:T(8,128)}, u32[]{:S(2)}, u32[]{:S(2)}) collective-permute-start(f32[168,128]{1,0:T(8,128)} %constant_dynamic-slice_fusion), channel_id=1, source_target_pairs={{0,16},{16,0},{1,17},{17,1},{2,18},{18,2},{3,19},{19,3},{4,20},{20... | collective-permute-start | bytes 258056 | tf_op jit(solution)/shard_map/ppermute | solution.py:460
  255.2 31.0 %collective-permute-start.35 = (s16[720,256]{1,0:T(8,128)(2,1)}, s16[720,256]{1,0:T(8,128)(2,1)S(1)}, u32[]{:S(2)}, u32[]{:S(2)}) collective-permute-start(s16[720,256]{1,0:T(8,128)(2,1)} %get-tuple-element.157), channel_id=1, source_target_pairs={{0,8},{4,12},{8,0},{12,4},{1,9},{5,13},{9,1},{13,5},{2,10},{6,14},... | collective-permute-start | bytes 1105928 | tf_op jit(solution)/shard_map/ppermute | solution.py:223
  266.3 4.5 %collective-permute-start.43 = (f32[168,128]{1,0:T(8,128)S(1)}, f32[168,128]{1,0:T(8,128)S(1)}, u32[]{:S(2)}, u32[]{:S(2)}) collective-permute-start(f32[168,128]{1,0:T(8,128)S(1)} %dynamic-slice_add_fusion.2), channel_id=1, source_target_pairs={{0,1},{1,0},{2,3},{3,2},{4,5},{5,4},{6,7},{7,6},{8,9},{9,8},{10,11... | collective-permute-start | bytes 258056 | tf_op jit(solution)/shard_map/ppermute | solution.py:550
  270.8 20.9 %collective-permute-start.44 = (f32[168,128]{1,0:T(8,128)S(1)}, f32[168,128]{1,0:T(8,128)S(1)}, u32[]{:S(2)}, u32[]{:S(2)}) collective-permute-start(f32[168,128]{1,0:T(8,128)S(1)} %add.114), channel_id=1, source_target_pairs={{0,2},{1,3},{2,0},{3,1},{4,6},{5,7},{6,4},{7,5},{8,10},{9,11},{10,... | collective-permute-start | bytes 258056 | tf_op jit(solution)/shard_map/ppermute | solution.py:550
  271.7 24.3 %collective-permute-start.32 = (s16[480,256]{1,0:T(8,128)(2,1)}, s16[480,256]{1,0:T(8,128)(2,1)S(1)}, u32[]{:S(2)}, u32[]{:S(2)}) collective-permute-start(s16[480,256]{1,0:T(8,128)(2,1)} %get-tuple-element.125), channel_id=1, source_target_pairs={{0,8},{4,12},{8,0},{12,4},{1,9},{5,13},{9,1},{13,5},{2,10},{6,14},... | collective-permute-start | bytes 737288 | tf_op jit(solution)/shard_map/ppermute | solution.py:223
  271.7 30.3 %collective-permute-start.37 = (s16[480,256]{1,0:T(8,128)(2,1)}, s16[480,256]{1,0:T(8,128)(2,1)S(1)}, u32[]{:S(2)}, u32[]{:S(2)}) collective-permute-start(s16[480,256]{1,0:T(8,128)(2,1)} %get-tuple-element.140), channel_id=1, source_target_pairs={{0,8},{4,12},{8,0},{12,4},{1,9},{5,13},{9,1},{13,5},{2,10},{6,14},... | collective-permute-start | bytes 737288 | tf_op jit(solution)/shard_map/ppermute | solution.py:223
  288.1 59.9 %collective-permute-start.36 = (f32[32,5376]{1,0:T(8,128)S(1)}, f32[32,5376]{1,0:T(8,128)}, u32[]{:S(2)}, u32[]{:S(2)}) collective-permute-start(f32[32,5376]{1,0:T(8,128)S(1)} %total.10), channel_id=1, source_target_pairs={{0,16},{1,17},{2,18},{3,19},{4,20},{5,21},{6,22},{7,23},{8,24},{9,... | collective-permute-start | bytes 2064392 | tf_op jit(solution)/shard_map/ppermute | solution.py:746
  291.7 15.2 %collective-permute-start.31 = (s16[480,256]{1,0:T(8,128)(2,1)S(1)}, s16[480,256]{1,0:T(8,128)(2,1)S(1)}, u32[]{:S(2)}, u32[]{:S(2)}) collective-permute-start(s16[480,256]{1,0:T(8,128)(2,1)S(1)} %get-tuple-element.152), channel_id=1, source_target_pairs={{0,8},{4,12},{8,0},{12,4},{1,9},{5,13},{9,1},{13,5},{2,10},{6,14},... | collective-permute-start | bytes 737288 | tf_op jit(solution)/shard_map/ppermute | solution.py:223
  291.8 15.1 %collective-permute-start.45 = (f32[266,128]{1,0:T(8,128)S(1)}, f32[266,128]{1,0:T(8,128)S(1)}, u32[]{:S(2)}, u32[]{:S(2)}) collective-permute-start(f32[266,128]{1,0:T(8,128)S(1)} %pad_maximum_fusion), channel_id=1, source_target_pairs={{0,4},{4,0},{8,12},{12,8},{1,5},{5,1},{9,13},{13,9},{2,6},{6,2},{1... | collective-permute-start | bytes 408584 | tf_op jit(solution)/shard_map/ppermute | solution.py:550
  296.1 49.3 %collective-permute-start.33 = (f32[32,3584]{1,0:T(8,128)S(1)}, f32[32,3584]{1,0:T(8,128)}, u32[]{:S(2)}, u32[]{:S(2)}) collective-permute-start(f32[32,3584]{1,0:T(8,128)S(1)} %total.9), channel_id=1, source_target_pairs={{0,16},{1,17},{2,18},{3,19},{4,20},{5,21},{6,22},{7,23},{8,24},{9,... | collective-permute-start | bytes 1376264 | tf_op jit(solution)/shard_map/ppermute | solution.py:746
  302.1 44.5 %collective-permute-start.38 = (f32[32,3584]{1,0:T(8,128)S(1)}, f32[32,3584]{1,0:T(8,128)}, u32[]{:S(2)}, u32[]{:S(2)}) collective-permute-start(f32[32,3584]{1,0:T(8,128)S(1)} %total.11), channel_id=1, source_target_pairs={{0,16},{1,17},{2,18},{3,19},{4,20},{5,21},{6,22},{7,23},{8,24},{9,... | collective-permute-start | bytes 1376264 | tf_op jit(solution)/shard_map/ppermute | solution.py:746
  306.9 22.7 %collective-permute-start.26 = (s16[480,256]{1,0:T(8,128)(2,1)S(1)}, s16[480,256]{1,0:T(8,128)(2,1)S(1)}, u32[]{:S(2)}, u32[]{:S(2)}) collective-permute-start(s16[480,256]{1,0:T(8,128)(2,1)S(1)} %copy-done.56), channel_id=1, source_target_pairs={{0,8},{4,12},{8,0},{12,4},{1,9},{5,13},{9,1},{13,5},{2,10},{6,14},... | collective-permute-start | bytes 737288 | tf_op jit(solution)/shard_map/ppermute | solution.py:223
  306.9 33.6 %collective-permute-start.29 = (s16[720,256]{1,0:T(8,128)(2,1)}, s16[720,256]{1,0:T(8,128)(2,1)}, u32[]{:S(2)}, u32[]{:S(2)}) collective-permute-start(s16[720,256]{1,0:T(8,128)(2,1)} %get-tuple-element.146), channel_id=1, source_target_pairs={{0,8},{4,12},{8,0},{12,4},{1,9},{5,13},{9,1},{13,5},{2,10},{6,14},... | collective-permute-start | bytes 1105928 | tf_op jit(solution)/shard_map/ppermute | solution.py:223
  330.2 12.8 %collective-permute-start.46 = (f32[266,128]{1,0:T(8,128)}, f32[266,128]{1,0:T(8,128)}, u32[]{:S(2)}, u32[]{:S(2)}) collective-permute-start(f32[266,128]{1,0:T(8,128)} %add.116), channel_id=1, source_target_pairs={{0,8},{4,12},{8,0},{12,4},{1,9},{5,13},{9,1},{13,5},{2,10},{6,14},... | collective-permute-start | bytes 408584 | tf_op jit(solution)/shard_map/ppermute | solution.py:550
  340.5 14.4 %collective-permute-start.39 = (f32[32,3584]{1,0:T(8,128)S(1)}, f32[32,3584]{1,0:T(8,128)S(1)}, u32[]{:S(2)}, u32[]{:S(2)}) collective-permute-start(f32[32,3584]{1,0:T(8,128)S(1)} %total.6), channel_id=1, source_target_pairs={{16,0},{17,1},{18,2},{19,3},{20,4},{21,5},{22,6},{23,7},{24,8},{25... | collective-permute-start | bytes 1376264 | tf_op jit(solution)/shard_map/ppermute | solution.py:748
  343.0 12.0 %collective-permute-start.40 = (f32[32,5376]{1,0:T(8,128)S(1)}, f32[32,5376]{1,0:T(8,128)S(1)}, u32[]{:S(2)}, u32[]{:S(2)}) collective-permute-start(f32[32,5376]{1,0:T(8,128)S(1)} %total.7), channel_id=1, source_target_pairs={{16,0},{17,1},{18,2},{19,3},{20,4},{21,5},{22,6},{23,7},{24,8},{25... | collective-permute-start | bytes 2064392 | tf_op jit(solution)/shard_map/ppermute | solution.py:748
  345.3 9.7 %collective-permute-start.41 = (f32[32,3584]{1,0:T(8,128)S(1)}, f32[32,3584]{1,0:T(8,128)S(1)}, u32[]{:S(2)}, u32[]{:S(2)}) collective-permute-start(f32[32,3584]{1,0:T(8,128)S(1)} %total.8), channel_id=1, source_target_pairs={{16,0},{17,1},{18,2},{19,3},{20,4},{21,5},{22,6},{23,7},{24,8},{25... | collective-permute-start | bytes 1376264 | tf_op jit(solution)/shard_map/ppermute | solution.py:748
  346.6 2.8 collective-permute-start.47
  (67 other events, 772.5 us)

commit v3 on v2

--- a/solution.py
+++ b/solution.py
@@ -15,7 +15,6 @@
 BIG_BITS = 56
 BIG = float(2.0**BIG_BITS)
 MIB = 1 << 20
-EXTRA = 16
 
 
 def params_of(mib):
@@ -85,12 +84,14 @@
     return places, -(-(row + 1) // 16) * 16
 
 
-def backward_kernel(count, norm_scale, *refs):
+def backward_kernel(count, norm_scale, calls, *refs):
     parts = refs[:count]
     summed, z_low, noise, ids = refs[count : count + 4]
     enc = [r[...] for r in refs[count + 4 : count + 11]]
     dec = [r[...] for r in refs[count + 11 : count + 16]]
-    dp_out, pack_out = refs[count + 16 :]
+    owed = refs[count + 16]
+    losses = refs[count + 17 : count + 17 + calls]
+    dp_out, pack_out = refs[count + 17 + calls :]
     dg2 = parts[0][...]
     for part in parts[1:]:
         dg2 = dg2 + part[...]
@@ -106,6 +107,28 @@
     grads = ordered(enc_grads + dec_grads)
     for row, grad in zip(pack_places([g.shape for g in grads])[0], grads):
         pack_out[row : row + grad.shape[0], : grad.shape[1]] = grad
+    loss = losses[0][...]
+    for ref in losses[1:]:
+        loss = loss + ref[...]
+    loss = jnp.sum(jnp.sum(loss, axis=0, keepdims=True), axis=1, keepdims=True) * (LN2 / norm_scale) + owed[...]
+    pack_out[pack_out.shape[0] - 1 :, 0:1] = loss
+
+
+def unpack_kernel(cuts, lower_ref, upper_ref, *refs):
+    pack = refs[-1]
+    half = lower_ref.shape[0]
+    pack[:half, :] = lower_ref[...]
+    pack[half:, :] = upper_ref[...]
+    for cut, out in zip(cuts, refs[:-1]):
+        at = 0
+        for row, rows, columns in cut:
+            out[at : at + rows, :] = pack[row : row + rows, :columns]
+            at += rows
+
+
+class RankedShape:
+    def __init__(self, rows, columns, index):
+        self.shape, self.index = (rows, columns), index
 
 
 def ordered(values):
@@ -190,16 +213,21 @@
             out_ref[:, cols] = sum_ref[:, cols] + decode(got_ref, j * rows, tiles, share, tile)
 
 
-def line_call(kernel, args, out_shape, name):
-    vmem = pl.BlockSpec(memory_space=pltpu.VMEM)
+def one_step(kernel, args, out_shape, name, place=None, scratch=()):
+    def whole(array):
+        return pl.BlockSpec(array.shape, lambda i, rank=len(array.shape): (0,) * rank)
+
+    front = [] if place is None else [place]
     return pl.pallas_call(
         kernel,
-        in_specs=[vmem] * len(args),
-        out_specs=[vmem] * len(out_shape),
-        out_shape=out_shape,
+        grid=(1,),
+        in_specs=[pl.BlockSpec(memory_space=pltpu.SMEM)] * len(front) + [whole(x) for x in args],
+        out_specs=[whole(x) for x in out_shape],
+        out_shape=list(out_shape),
+        scratch_shapes=list(scratch),
         compiler_params=params_of(48),
         name=name,
-    )(*args)
+    )(*front, *args)
 
 
 def line_start(pieces):
@@ -214,7 +242,7 @@
     got, own, other = state
     sent = jax.ShapeDtypeStruct((got.shape[0] // 2, 256), jnp.int16)
     kernel = functools.partial(join_kernel, chunk=chunk)
-    return line_call(kernel, state, [sent, jax.ShapeDtypeStruct(own.shape, jnp.float32)], "join")
+    return one_step(kernel, state, [sent, jax.ShapeDtypeStruct(own.shape, jnp.float32)], "join")
 
 
 def line_last(state):
@@ -228,7 +256,7 @@
         return state[0]
     got, own = state
     kernel = functools.partial(total_kernel, chunk=chunk)
-    return line_call(kernel, [own, got], [jax.ShapeDtypeStruct(own.shape, jnp.float32)], "total")[0]
+    return one_step(kernel, [own, got], [jax.ShapeDtypeStruct(own.shape, jnp.float32)], "total")[0]
 
 
 def after(value, *others):
@@ -240,45 +268,68 @@
     return jnp.where(own, kept_ref[...], got_ref[...])
 
 
-def project_kernel(started, half_ref, x_ref, kept_ref, got_ref, *refs):
-    out_ref = refs[-1]
-    size = x_ref.shape[0]
-    rows = pl.ds(pl.multiple_of(pl.program_id(1) * size, 16), size)
-    part = jnp.dot(x_ref[...], chosen(half_ref[1], True, kept_ref, got_ref), preferred_element_type=jnp.float32)
+def weight_specs(chunk, width, per_half, first, got_first, encoder):
+    owner = 0 if encoder else 1
+
+    def kept(j, h):
+        return (jnp.where(h[1] == owner, h[0] * per_half + first + j, 0), 0)
+
+    def got(j, h):
+        return (jnp.where(h[1] == owner, 0, got_first + j), 0)
+
+    return [pl.BlockSpec((chunk, width), kept), pl.BlockSpec((chunk, width), got)]
+
+
+def project_kernel(started, half_ref, x_ref, kept_ref, got_ref, keep_ref, log_ref, *refs):
+    out_ref, seen_ref = refs[-2:]
+    chunk, width = kept_ref.shape
+    keep = keep_ref[...]
+    row = lax.broadcasted_iota(jnp.int32, (width, chunk), 0)
+    terms = jnp.where(row == 0, keep, 0.0)
+    rest = keep * log_ref[...]
+    for place in range(1, 4):
+        high = rest.astype(jnp.bfloat16).astype(jnp.float32)
+        terms = jnp.where(row == place, high, terms)
+        rest = rest - high
+    right = jnp.concatenate([chosen(half_ref[1], True, kept_ref, got_ref), jnp.transpose(terms).astype(jnp.bfloat16)], axis=1)
+    part = jnp.dot(x_ref[...], right, preferred_element_type=jnp.float32)
 
     @pl.when(pl.program_id(0) == 0)
     def first():
-        out_ref[rows, :] = part + refs[0][rows, :] if started else part
+        out_ref[...] = part[:, :width] + refs[0][...] if started else part[:, :width]
+        seen_ref[...] = part[:, width:] + refs[1][...] if started else part[:, width:]
 
     @pl.when(pl.program_id(0) != 0)
     def later():
-        out_ref[rows, :] += part
-
-
-def project(half, peaks, kept, got, before, first, got_first, count, chunk, per_half):
+        out_ref[...] += part[:, :width]
+        seen_ref[...] += part[:, width:]
+
+
+def project(half, peaks, kept, got, keep, log_fa, before, first, got_first, count, chunk, per_half):
     cells, width = peaks.shape[0], kept.shape[1]
-    started = before is not None
-    whole = pl.BlockSpec((cells, width), lambda j, i, h: (0, 0))
+    whole = pl.BlockSpec((cells, width), lambda j, h: (0, 0))
+    row = pl.BlockSpec((1, chunk), lambda j, h: (0, first + j))
     return pl.pallas_call(
-        functools.partial(project_kernel, started),
+        functools.partial(project_kernel, bool(before)),
         grid_spec=pltpu.PrefetchScalarGridSpec(
             num_scalar_prefetch=1,
-            grid=(count, 2),
+            grid=(count,),
             in_specs=[
-                pl.BlockSpec((cells // 2, chunk), lambda j, i, h: (i, h[0] * per_half + first + j)),
-                pl.BlockSpec((chunk, width), lambda j, i, h: (h[0] * per_half + first + j, 0)),
-                pl.BlockSpec((chunk, width), lambda j, i, h: (got_first + j, 0)),
+                pl.BlockSpec((cells, chunk), lambda j, h: (0, h[0] * per_half + first + j)),
+                *weight_specs(chunk, width, per_half, first, got_first, True),
+                row,
+                row,
             ]
-            + [whole] * started,
-            out_specs=whole,
+            + [whole] * len(before),
+            out_specs=[whole, whole],
         ),
-        out_shape=jax.ShapeDtypeStruct((cells, width), jnp.float32),
+        out_shape=[jax.ShapeDtypeStruct((cells, width), jnp.float32)] * 2,
         compiler_params=params_of(48),
         cost_estimate=pl.CostEstimate(
             flops=2 * cells * count * chunk * width, bytes_accessed=2 * cells * count * chunk, transcendentals=0
         ),
         name="project",
-    )(half, peaks, kept, got, *([before] if started else []))
+    )(half, peaks, kept, got, keep, log_fa, *before)
 
 
 def regions_kernel(
@@ -286,8 +337,8 @@
     *refs,
 ):
     outs = refs[1 if started else 0 :]
-    dg_ref, st_ref = outs[:2]
-    m0, m1, e0, e1, w_ref, dw_ref = outs[-6:] if coded else (*outs[3:], outs[2])
+    dg_ref, bias_ref, loss_ref = outs[:3]
+    m0, m1, e0, e1, w_ref, dw_ref = outs[-6:] if coded else (*outs[4:], outs[3])
     cells, chunk = x_ref.shape
     blocks = cells // rows_at_once
     M, E = (m0, m1), (e0, e1)
@@ -297,6 +348,7 @@
     @pl.when(pl.program_id(0) == 0)
     def first():
         dg_ref[...] = refs[0][...] if started else jnp.zeros_like(dg_ref)
+        loss_ref[...] = jnp.zeros_like(loss_ref)
 
     def one_tile(t, carry):
         cols = pl.ds(pl.multiple_of(t * tile, 128), tile)
@@ -362,13 +414,15 @@
             sums = step(i, i % 2, sums, logits=i < blocks - 1, start=i == 1)
         cell_grad(blocks - 1, (blocks - 1) % 2)
         region_grad(blocks - 1, (blocks - 1) % 2, blocks == 1)
-        st_ref[0:8, cols] = sums[0]
-        st_ref[8:16, cols] = sums[1]
+        bias_ref[:, cols] = jnp.sum(sums[0], axis=0, keepdims=True)
+        kept = sums[1] * ck[0]
+        for c in range(0, tile, 128):
+            loss_ref[...] += kept[:, c : c + 128]
         return carry
 
     lax.fori_loop(0, chunk // tile, one_tile, 0)
     if coded:
-        give_shares(half_ref[2], dw_ref, *outs[2:5])
+        give_shares(half_ref[2], dw_ref, *outs[3:6])
 
 
 def regions_pass(half, peaks, kept, got, hidden, hidden_t, a, fa, ck, cf, before, first, at, count, chunk, per_half, coded):
@@ -386,14 +440,18 @@
             grid=(count,),
             in_specs=[
                 pl.BlockSpec((cells, chunk), lambda j, h: (0, h[0] * per_half + first + j)),
-                pl.BlockSpec((chunk, width), lambda j, h: (h[0] * per_half + first + j, 0)),
-                pl.BlockSpec((chunk, width), lambda j, h: (at + j, 0)),
+                *weight_specs(chunk, width, per_half, first, at, False),
                 pl.BlockSpec((cells, 2 * width), lambda j, h: (0, 0)),
                 pl.BlockSpec((blocks, width, rows), lambda j, h: (0, 0, 0)),
                 row, row, row, whole,
             ]
             + [whole] * started,
-            out_specs=[whole, pl.BlockSpec((16, chunk), lambda j, h: (0, j)), *share_specs],
+            out_specs=[
+                whole,
+                pl.BlockSpec((1, chunk), lambda j, h: (0, j)),
+                pl.BlockSpec((8, 128), lambda j, h: (0, 0)),
+                *share_specs,
+            ],
             scratch_shapes=[pltpu.VMEM((rows, tile), jnp.float32)] * 2
             + [pltpu.VMEM((rows, tile), jnp.bfloat16)] * 2
             + [pltpu.VMEM((chunk, width), jnp.bfloat16)]
@@ -401,7 +459,8 @@
         ),
         out_shape=[
             jax.ShapeDtypeStruct((cells, width), jnp.float32),
-            jax.ShapeDtypeStruct((16, count * chunk), jnp.float32),
+            jax.ShapeDtypeStruct((1, count * chunk), jnp.float32),
+            jax.ShapeDtypeStruct((8, 128), jnp.float32),
             *share_shapes,
         ],
         compiler_params=params_of(56),
@@ -414,22 +473,18 @@
     )(half, peaks, kept, got, hidden, hidden_t, a, fa, ck, cf, *([before] if started else []))
 
 
-def outer_kernel(coded, half_ref, x_ref, left_ref, extra_ref, *outs):
-    dw_ref = outs[-1] if coded else outs[0]
-    width = dw_ref.shape[0]
+def outer_kernel(coded, half_ref, x_ref, left_ref, *outs):
+    dw_ref = outs[-1]
     tile = min(256, x_ref.shape[1])
     for c in range(0, x_ref.shape[1], tile):
         cols = slice(c, c + tile)
-        part = jnp.dot(left_ref[...], x_ref[:, cols], preferred_element_type=jnp.float32)
-        dw_ref[:, cols] = part[:width]
-        extra_ref[:, cols] = part[width:]
+        dw_ref[:, cols] = jnp.dot(left_ref[...], x_ref[:, cols], preferred_element_type=jnp.float32)
     if coded:
         give_shares(half_ref[2], dw_ref, *outs[:3])
 
 
 def outer(half, peaks, left, first, count, chunk, per_half, coded):
-    cells = peaks.shape[0]
-    width = left.shape[0] - EXTRA
+    width, cells = left.shape
     share_specs, share_shapes = share_outputs(width, chunk, count, coded)
     return pl.pallas_call(
         functools.partial(outer_kernel, coded),
@@ -438,12 +493,12 @@
             grid=(count,),
             in_specs=[
                 pl.BlockSpec((cells, chunk), lambda j, h: (0, h[0] * per_half + first + j)),
-                pl.BlockSpec((width + EXTRA, cells), lambda j, h: (0, 0)),
+                pl.BlockSpec((width, cells), lambda j, h: (0, 0)),
             ],
-            out_specs=[pl.BlockSpec((EXTRA, chunk), lambda j, h: (0, j)), *share_specs],
+            out_specs=share_specs,
             scratch_shapes=[pltpu.VMEM((width, chunk), jnp.float32)] * coded,
         ),
-        out_shape=[jax.ShapeDtypeStruct((EXTRA, count * chunk), jnp.float32), *share_shapes],
+        out_shape=share_shapes,
         compiler_params=params_of(48),
         cost_estimate=pl.CostEstimate(
             flops=2 * cells * count * chunk * width, bytes_accessed=2 * cells * count * chunk, transcendentals=0
@@ -516,28 +571,21 @@
         turned_ref[block] = jnp.transpose(all_s[block * size : (block + 1) * size, :]).astype(jnp.bfloat16)
 
 
-def left_kernel(count, place_ref, log_ref, *refs):
+def left_kernel(count, place_ref, *refs):
     pieces, (left_ref, all_s) = refs[:-2], refs[-2:]
-    rows, width = pieces[0].shape
+    rows = pieces[0].shape[0]
     for index, piece in enumerate(pieces):
         at = pl.ds(pl.multiple_of(rows_at(place_ref, index, count, rows), 16), rows)
         all_s[at, :] = piece[...].astype(jnp.float32)
-    left_ref[:width, :] = jnp.transpose(all_s[...]).astype(jnp.bfloat16)
-    left_ref[width:, :] = log_ref[...]
-
-
-def assemble(kernel, place, pieces, before, out_shape, name):
-    vmem = pl.BlockSpec(memory_space=pltpu.VMEM)
+    left_ref[...] = jnp.transpose(all_s[...]).astype(jnp.bfloat16)
+
+
+def assemble(kernel, place, pieces, out_shape, name):
     rows, width = pieces[0].shape
-    return pl.pallas_call(
-        functools.partial(kernel, len(pieces) // 2),
-        in_specs=[pl.BlockSpec(memory_space=pltpu.SMEM)] + [vmem] * (len(before) + len(pieces)),
-        out_specs=[vmem] * len(out_shape),
-        out_shape=out_shape,
-        scratch_shapes=[pltpu.VMEM((rows * len(pieces), width), jnp.float32)],
-        compiler_params=params_of(32),
-        name=name,
-    )(place, *before, *pieces)
+    return one_step(
+        functools.partial(kernel, len(pieces) // 2), pieces, out_shape, name, place,
+        [pltpu.VMEM((rows * len(pieces), width), jnp.float32)],
+    )
 
 
 def exchange_bits(axis):
@@ -561,13 +609,6 @@
     other = across_cores(own)
     first = lax.axis_index("pipe") == 0
     return jnp.where(first, own, other), jnp.where(first, other, own)
-
-
-def three_terms(values):
-    high = values.astype(jnp.bfloat16)
-    rest = values - high.astype(jnp.float32)
-    middle = rest.astype(jnp.bfloat16)
-    return high, middle, (rest - middle.astype(jnp.float32)).astype(jnp.bfloat16)
 
 
 def body(
@@ -609,7 +650,7 @@
     place = jnp.stack([pipe, mine, dp_at]).astype(jnp.int32)
     chunk = next(c for c in (1792, 256, 128) if window % c == 0 and (regions_local - window) % c == 0)
     chunks = window // chunk
-    ahead = min(2, chunks - 1) * chunk
+    ahead = min(3, chunks - 1) * chunk
     coded = lax.axis_size("dp") == 4 and chunk % 256 == 0
     if overlap:
         mine_alone = (pipe == 0) | (jnp.arange(window) >= overlap)
@@ -628,7 +669,7 @@
         got_rest = across_cores(lax.dynamic_slice_in_dim(weight, other_at + ahead, window - ahead, 0))
         got_parts = [(weight, got_first, 0, 0, ahead // chunk), (weight, got_rest, ahead // chunk, 0, chunks - ahead // chunk)]
         cut = ahead // chunk
-        middle = cut + (chunks - cut + 1) // 2
+        middle = cut + (chunks - cut) // 2
         got_spans = [(got_first, 0, 0, cut), (got_rest, 0, cut, middle), (got_rest, middle - cut, middle, chunks)]
         half = jnp.stack([place[0], place[0], place[2]])
 
@@ -646,40 +687,31 @@
     a = jnp.exp(of_core(out_bias, pipe))[None]
     fa = a * of_core(region_factor, pipe)[None]
     ck = (keep * norm_scale)[None]
+    log_fa = jnp.log(fa)
     cf_wide = jnp.broadcast_to(cell_factor[:, None], (cells, 128))
-    logs = jnp.concatenate(
-        [jnp.ones((1, cells), jnp.bfloat16)]
-        + [t[None] for t in three_terms(jnp.log(cell_factor))]
-        + [jnp.zeros((EXTRA - 4, cells), jnp.bfloat16)],
-        axis=0,
-    )
-    early = (noise_own, ids_own, enc, dec, a, fa, ck, cf_wide, logs)
-    kept_first, got_first, *span = got_parts[0]
-    got_first, early = lax.optimization_barrier((got_first, early))
-    noise_own, ids_own, enc, dec, a, fa, ck, cf_wide, logs = early
-    got_parts[0] = (kept_first, got_first, *span)
-
-    vmem = pl.BlockSpec(memory_space=pltpu.VMEM)
-    partial = None
+    partial = []
     for kept_w, got_w, first, at, count in got_parts:
-        partial = project(half, peak_data, kept_w, got_w, partial, first, at, count, chunk, chunks)
+        partial = project(half, peak_data, kept_w, got_w, keep[None], log_fa, partial, first, at, count, chunk, chunks)
+    partial, seen = partial
     pieces = scatter_cells(partial)
-    summed, z_low, g2_own, kl_sum = pl.pallas_call(
+    owed = jnp.sum(seen[:, 0] * (BIG_BITS * LN2 - jnp.log(cell_factor))) - jnp.sum(seen[:, 1:4])
+    early = (noise_own, ids_own, enc, dec, a, fa, ck, cf_wide, owed[None, None])
+    pieces, early = lax.optimization_barrier((pieces, early))
+    noise_own, ids_own, enc, dec, a, fa, ck, cf_wide, owed = early
+    summed, z_low, g2_own, kl_sum = one_step(
         functools.partial(forward_kernel, len(pieces)),
-        in_specs=[vmem] * (len(pieces) + 14),
-        out_specs=[vmem] * 4,
-        out_shape=[
+        [*pieces, noise_own, ids_own, *enc, *dec],
+        [
             jax.ShapeDtypeStruct((own_rows, width), jnp.float32),
             jax.ShapeDtypeStruct((own_rows, latent), jnp.bfloat16),
             jax.ShapeDtypeStruct((own_rows, width), jnp.bfloat16),
             jax.ShapeDtypeStruct((1, 1), jnp.float32),
         ],
-        compiler_params=params_of(32),
-        name="small_forward",
-    )(*pieces, noise_own, ids_own, *enc, *dec)
+        "small_forward",
+    )
     rows_b = min(512, cells // 2)
     hidden, hidden_t = assemble(
-        hidden_kernel, place, gather_cells(g2_own), [],
+        hidden_kernel, place, gather_cells(g2_own),
         [
             jax.ShapeDtypeStruct((cells, 2 * width), jnp.bfloat16),
             jax.ShapeDtypeStruct((cells // rows_b, width, rows_b), jnp.bfloat16),
@@ -687,103 +719,123 @@
         "hidden",
     )
 
-    dg2, lines, stats = None, [], []
+    dg2, lines, biases, losses = None, [], [], []
     for got_w, at, first, end in got_spans:
         if len(lines) > 1:
             lines[-2] = line_joined(lines[-2], chunk)
-            dg2 = after(dg2, *lines[-2])
+            dg2 = after(dg2, lines[-2][0])
             lines[-2] = line_last(lines[-2])
-        dg2, st, *shares = regions_pass(
+        dg2, bias, loss, *shares = regions_pass(
             half, peak_data, weight, got_w, hidden, hidden_t, a, fa, ck, cf_wide, dg2, first, at, end - first, chunk,
             chunks, coded,
         )
+        dg2 = after(dg2, *[line[0] for line in lines])
         lines.append(line_start(shares))
-        stats.append(st)
-    stats = jnp.concatenate(stats, axis=1)
-
+        biases.append(bias)
+        losses.append(loss)
+    pieces = scatter_cells(dg2)
     if len(lines) > 1:
-        lines[-2] = line_last(line_joined(lines[-2], chunk))
-    pieces = scatter_cells(dg2)
+        lines[-2] = line_joined(lines[-2], chunk)
+        pieces[0] = after(pieces[0], lines[-2][0])
+        lines[-2] = line_last(lines[-2])
     grad_shapes = [w.shape for w in ordered(enc + dec)]
     places, pack_rows = pack_places(grad_shapes)
-    dp_own, pack = pl.pallas_call(
-        functools.partial(backward_kernel, len(pieces), norm_scale),
-        in_specs=[vmem] * (len(pieces) + 16),
-        out_specs=[vmem] * 2,
-        out_shape=[
+    pack_half = pack_rows // 2
+    dp_own, pack = one_step(
+        functools.partial(backward_kernel, len(pieces), norm_scale, len(losses)),
+        [*pieces, summed, z_low, noise_own, ids_own, *enc, *dec, kl_sum + owed, *losses],
+        [
             jax.ShapeDtypeStruct((own_rows, width), jnp.bfloat16),
             jax.ShapeDtypeStruct((pack_rows, width), jnp.float32),
         ],
-        compiler_params=params_of(32),
-        name="small_backward",
-    )(*pieces, summed, z_low, noise_own, ids_own, *enc, *dec)
+        "small_backward",
+    )
+    dp_own = after(dp_own, *[line[0] for line in lines])
+    lines[-1] = line_joined(lines[-1], chunk)
     (left,) = assemble(
-        left_kernel, place, gather_cells(dp_own), [logs],
-        [jax.ShapeDtypeStruct((width + EXTRA, cells), jnp.bfloat16)],
-        "left",
+        left_kernel, place, gather_cells(dp_own), [jax.ShapeDtypeStruct((width, cells), jnp.bfloat16)], "left"
     )
-    cuts = [0, 2, 5, chunks] if chunks == 7 else [0, chunks]
-    extras, enc_lines = [], []
-    under_way = [(lines, lines.pop())]
-    for first, end in zip(cuts[:-1], cuts[1:]):
-        if first:
-            where, line = under_way.pop(0)
-            line = line_joined(line, chunk)
+    left = after(left, lines[-1][0])
+    lines[-1] = line_last(lines[-1])
+
+    spans = [(first, end) for _, _, first, end in got_spans]
+    order = [1, 0, 2][: len(spans)] if len(spans) > 1 else [0]
+    enc_lines, under_way = [], []
+    for index, (first, end) in enumerate([spans[i] for i in order]):
+        if index:
+            left = after(left, shares[0])
+        if index > 1:
+            line = line_joined(under_way.pop(0), chunk)
             left = after(left, line[0])
-            where.append(line_last(line))
-        extra, *shares = outer(half, peak_data, left, first, end - first, chunk, chunks, coded)
-        under_way.append((enc_lines, line_start(shares)))
-        extras.append(extra)
-    extra = jnp.concatenate(extras, axis=1)
-    newest = under_way[-1][1][0]
+            enc_lines.append(line_last(line))
+        shares = list(outer(half, peak_data, left, first, end - first, chunk, chunks, coded))
+        if index == min(1, len(spans) - 1):
+            pack = after(pack, *([waiting] if index else []))
+            pack = part_of(pack, pipe, pack_half) + across_cores(part_of(pack, 1 - pipe, pack_half))
+            steps = [("tensor", bit) for bit in exchange_bits("tensor")]
+            while len(steps) > 1:
+                pack = exchanged(pack, *steps.pop(0))
+            shares[0] = after(shares[0], pack)
+        elif index:
+            pack = exchanged(pack, *steps.pop(0))
+            shares[0] = after(shares[0], pack)
+        waiting = shares[0]
+        if index:
+            beside = [line[0] for line in under_way + enc_lines] + ([lines[-1][0]] if index == 1 else [])
+            shares[0] = after(shares[0], *beside)
+        under_way.append(line_start(shares))
+    for step in steps:
+        pack = exchanged(pack, *step)
+    sums = jnp.concatenate([pack, jnp.concatenate(biases, axis=1).reshape(-1, 128)], axis=0)
+    sums = after(sums, under_way[-1][0])
     joined = []
-    for where, line in under_way:
+    for line in under_way:
+        if enc_lines:
+            line[0] = after(line[0], enc_lines[-1][0])
         line = line_joined(line, chunk)
         joined.append(line[0])
-        where.append(line_last(line))
+        enc_lines.append(line_last(line))
 
     dec_own = [line_end(line, chunk) for line in lines]
     dec_got = [lax.ppermute(share, "pipe", [(0, 1)]) for share in dec_own]
-    enc_own = [line_end(line, chunk) for line in enc_lines]
+    enc_own = [line_end(enc_lines[order.index(i)], chunk) for i in range(len(order))]
     enc_got = [lax.ppermute(share, "pipe", [(1, 0)]) for share in enc_own]
     is_first = pipe == 0
-    lower = jnp.where(is_first, jnp.concatenate(enc_own, axis=1), jnp.concatenate(dec_got, axis=1))
-    upper = jnp.where(is_first, jnp.concatenate(enc_got, axis=1), jnp.concatenate(dec_own, axis=1))
-    region_grad = jnp.transpose(jnp.concatenate([lower, upper[:, overlap:]], axis=1))[None]
-
-    seen, seen_log = extra[0], extra[1] + extra[2] + extra[3]
-    per_region = LN2 * jnp.sum(stats[8:], axis=0) + seen * (BIG_BITS * LN2 - jnp.log(fa[0])) - seen_log
-    loss = jnp.sum(keep * per_region) + kl_sum[0, 0]
-    pack = pack.at[pack_rows - 1, 0].set(loss)
-    pack_half = pack_rows // 2
-    pack = part_of(pack, pipe, pack_half) + across_cores(part_of(pack, 1 - pipe, pack_half))
-    pack = all_sum(after(pack, newest, joined[0]), ["tensor"])
-    sums = jnp.concatenate([pack, jnp.sum(stats[:8], axis=0).reshape(-1, 128)], axis=0)
-    sums = after(sums, joined[-1])
+    lower = [jnp.where(is_first, e, d) for e, d in zip(enc_own, dec_got)]
+    upper = [jnp.where(is_first, e, d) for e, d in zip(enc_got, dec_own)]
+    upper[0] = upper[0][:, overlap:]
+    region_grad = jnp.transpose(jnp.concatenate(lower + upper, axis=1))[None]
+
+    sums = after(sums, joined[0])
     for bit in exchange_bits("dp"):
         if bit > 1:
-            sums = after(sums, enc_lines[-1][0])
+            sums = after(sums, joined[-1], *dec_got)
         sums = exchanged(sums, "dp", bit)
     lower, upper = join_cores(sums)
-    pack = jnp.concatenate([lower[:pack_half], upper[:pack_half]], axis=0)
     bias_grad = jnp.concatenate([lower[pack_half:].reshape(-1), upper[pack_half:].reshape(-1)[overlap:]])
-    small = {}
-    shapes = list(enumerate(w.shape for w in enc + dec))
-    named = [s for s in shapes if s[1][0] > 1] + [s for s in shapes if s[1][0] == 1]
-    for row, (index, shape) in zip(places, named):
-        small[index] = pack[row : row + shape[0], : shape[1]]
-    (d_bias_in, d_square, d_bias_two, d_mean_w, d_var_w, d_mean_b, d_var_b, d_first_z, d_first_b, d_bias_one, d_dec_square,
-     d_dec_bias_two) = [small[i] for i in range(len(small))]
-    mean_loss = pack[pack_rows - 1, 0] / (cell_total * region_total)
+    lower, upper = lower[:pack_half], upper[:pack_half]
+
+    shapes = [w.shape for w in enc + dec]
+    ranked = ordered([RankedShape(*shape, index) for index, shape in enumerate(shapes)])
+    rows_of = {entry.index: row for row, entry in zip(places, ranked)}
+    groups = [(0,), (1,), (2,), (3, 4), (5,), (6,), (7, 8), (9,), (10,), (11,)]
+    cuts = [[(rows_of[i], *shapes[i]) for i in group] for group in groups] + [[(pack_rows - 1, 1, 1)]]
+    out_shape = [jax.ShapeDtypeStruct((sum(c[1] for c in cut), cut[0][2]), jnp.float32) for cut in cuts]
+    (d_bias_in, d_square, d_bias_two, d_heads, d_mean_b, d_var_b, d_first, d_bias_one, d_dec_square, d_dec_bias_two,
+     loss_total) = one_step(
+        functools.partial(unpack_kernel, cuts), [lower, upper], out_shape, "unpack", None,
+        [pltpu.VMEM((pack_rows, width), jnp.float32)],
+    )
+    mean_loss = loss_total[0, 0] / (cell_total * region_total)
     return (
         region_grad,
         bias_grad,
         d_bias_in[0],
         d_square,
         d_bias_two[0],
-        jnp.transpose(jnp.concatenate([d_mean_w, d_var_w], axis=0)),
+        jnp.transpose(d_heads),
         jnp.concatenate([d_mean_b[0], d_var_b[0]], axis=0),
-        jnp.concatenate([d_first_z, d_first_b], axis=0),
+        d_first,
         d_bias_one[0],
         d_dec_square,
         d_dec_bias_two[0],

time: 359 us -> 320 us (0.89)
  waiting for transfers between devices: 85 us -> 60.1 us
  other arithmetic: 13.8 us -> 6.34 us
  Pallas kernels: 175 us -> 169 us
  local copies, waits for them, and re-layouts: 33 us -> 28.1 us
    ppermute x6, waiting for transfers between devices: 46.6 us -> 29.5 us  [line_last(): lax.ppermute(state[0], 'dp', [(i, i ^ 2) for i in range(4)])]
    ppermute x6, waiting for transfers between devices: 11.1 us -> 5.06 us  [line_start(): lax.ppermute(pieces[0], 'dp', [(i, i ^ 1) for i in range(4)])]
    pallas_call x18 -> x19, Pallas kernels: 44.7 us -> 41 us  [the longest x2 26.4 us: project(): pl.pallas_call(functools.partial(project_kernel, bool(before)), grid_spec...]
    unnamed x138 -> x110, local copies, waits for them, and re-layouts: 13 us -> 13.4 us
  transfers between devices with their start and end apart: 48 -> 48, of which waited for: 21 -> 21; matrix products, arithmetic and copies ran while one was open for 7% -> 5% of each run, Pallas kernels for 25% -> 31%
where the time goes in v3:
time: 320 us; the launch traced here: 319 us
  Pallas kernels  169 us (53%)
  waiting for transfers between devices  60.1 us (19%)
  starting transfers between devices  50.8 us (16%)
  local copies, waits for them, and re-layouts  28.1 us (9%)
  other arithmetic  6.34 us (2%)
  between operations  5.36 us (2%)
    pallas_call x3, Pallas kernels, regions_pass(): pl.pallas_call(functools.partial(regions_kernel, tile, rows, piece, start...  102 us
    ppermute x6, waiting for transfers between devices, line_last(): lax.ppermute(state[0], 'dp', [(i, i ^ 2) for i in range(4)])  29.5 us
    pallas_call x2, Pallas kernels, project(): pl.pallas_call(functools.partial(project_kernel, bool(before)), grid_spec...  26.4 us
    pallas_call x3, Pallas kernels, outer(): pl.pallas_call(functools.partial(outer_kernel, coded), grid_spec=pltpu.Pr...  25.3 us
    pallas_call x17, Pallas kernels, one_step(): pl.pallas_call(kernel, grid=(1,), in_specs=[pl.BlockSpec(memory_space=plt...  14.6 us
    unnamed x110, local copies, waits for them, and re-layouts  13.4 us
    ppermute x6, starting transfers between devices, line_last(): lax.ppermute(state[0], 'dp', [(i, i ^ 2) for i in range(4)])  10.9 us
    ppermute x6, waiting for transfers between devices, scatter_cells(): pieces.append(lax.ppermute(part_of(chip_sum, there, rows), 'tensor', route))  8.85 us
  transfers between devices with their start and end apart: 48, of which 21 were waited for; matrix products, arithmetic and copies ran while one was open for 5% of the time, Pallas kernels for 31%

profile of v3, /device:TPU:0, one launch (start us, length us, event | category | flops | bytes accessed | tf_op | source)
XLA Modules:
  0.0 319.4 jit_solution(10197959424336114316)
XLA Ops:
  0.7 2.9 dynamic-slice_bitcast_fusion
  4.0 2.5 dynamic-slice_bitcast_fusion.1
  6.6 1.6 broadcast_multiply_fusion
  9.8 1.5 broadcast_in_dim.49.a_ref
  11.2 1.5 broadcast_in_dim.50.ck_ref
  12.7 1.5 mul.71.fa_ref
  15.1 11.8 %project.2 = (f32[2048,128]{1,0:T(8,128)S(1)}, f32[2048,128]{1,0:T(8,128)S(1)}) custom-call(s32[3]{0:T(128)S(1)} %add_add_fusion.half_ref, bf16[2048,25088]{1,0:T(8,128)(2,1)} %x_ref.15, bf16[25088,128]{1,0:T(8,128)(2,1)} %bitcast.45, bf16[5376,128]{1,0:T(8,128)(2,1)S(1)} %collective-permute-done.1.got_ref, f32[1,12544]{1,0:T(1,128)S(1)} %broadcast_in_dim.42.keep_ref, ...), custom_call_target="tpu_custom_call" | custom-call | flops 2818572288 | bytes 22020096 | tf_op jit(solution)/shard_map/project/pallas_call | solution.py:312
  27.0 14.6 %project.3 = (f32[2048,128]{1,0:T(8,128)S(1)}, f32[2048,128]{1,0:T(8,128)S(1)}) custom-call(s32[3]{0:T(128)S(1)} %add_add_fusion.half_ref, bf16[2048,25088]{1,0:T(8,128)(2,1)} %x_ref.15, bf16[25088,128]{1,0:T(8,128)(2,1)} %bitcast.46, bf16[7168,128]{1,0:T(8,128)(2,1)S(1)} %collective-permute-done.got_ref, f32[1,12544]{1,0:T(1,128)S(1)} %broadcast_in_dim.42.keep_ref, ...), custom_call_target="tpu_custom_call" | custom-call | flops 3758096384 | bytes 29360128 | tf_op jit(solution)/shard_map/project/pallas_call | solution.py:312
  43.8 3.0 collective-permute-start.3
  46.8 1.5 collective-permute-start.4
  51.2 3.7 %collective-permute-done.4.refs_2_ = f32[256,128]{1,0:T(8,128)S(1)} collective-permute-done((f32[256,128]{1,0:T(8,128)S(1)}, f32[256,128]{1,0:T(8,128)S(1)}, u32[]{:S(2)}, u32[]{:S(2)}) %collective-permute-start.4) | collective-permute-done | bytes 131104 | tf_op jit(solution)/shard_map/ppermute | solution.py:535
  54.9 1.3 broadcast_in_dim.51.cf_ref
  56.4 2.8 small_forward.1
  61.2 1.4 collective-permute-start.8
  64.8 1.6 collective-permute-done.8.refs_3_
  70.6 41.8 %regions.3 = (f32[2048,128]{1,0:T(8,128)}, f32[1,5376]{1,0:T(1,128)}, f32[8,128]{1,0:T(8,128)}, s16[1440,256]{1,0:T(8,128)(2,1)}, f32[32,5376]{1,0:T(8,128)}, /*index=5*/f32[32,5376]{1,0:T(8,128)}) custom-call(s32[3]{0:T(128)} %copy-done.32, bf16[2048,25088]{1,0:T(8,128)(2,1)} %x_ref.15, bf16[25088,128]{1,0:T(8,128)(2,1)} %bitcast.47, ...), custom_call_target="tpu_custom_call" | custom-call | flops 14092861440 | bytes 22020096 | tf_op jit(solution)/shard_map/regions/pallas_call | solution.py:436
  112.4 1.6 collective-permute-start.13
  114.0 30.5 %regions.4 = (f32[2048,128]{1,0:T(8,128)}, f32[1,3584]{1,0:T(1,128)}, f32[8,128]{1,0:T(8,128)}, s16[960,256]{1,0:T(8,128)(2,1)}, f32[32,3584]{1,0:T(8,128)}, /*index=5*/f32[32,3584]{1,0:T(8,128)}) custom-call(s32[3]{0:T(128)} %copy-done.32, bf16[2048,25088]{1,0:T(8,128)(2,1)} %x_ref.15, bf16[25088,128]{1,0:T(8,128)(2,1)} %bitcast.48, ...), custom_call_target="tpu_custom_call" | custom-call | flops 9395240960 | bytes 14680064 | tf_op jit(solution)/shard_map/regions/pallas_call | solution.py:436
  145.5 2.7 collective-permute-start.14
  148.2 30.2 %regions.5 = (f32[2048,128]{1,0:T(8,128)}, f32[1,3584]{1,0:T(1,128)}, f32[8,128]{1,0:T(8,128)}, s16[960,256]{1,0:T(8,128)(2,1)}, f32[32,3584]{1,0:T(8,128)}, /*index=5*/f32[32,3584]{1,0:T(8,128)}) custom-call(s32[3]{0:T(128)} %copy-done.32, bf16[2048,25088]{1,0:T(8,128)(2,1)} %x_ref.15, bf16[25088,128]{1,0:T(8,128)(2,1)} %bitcast.49, ...), custom_call_target="tpu_custom_call" | custom-call | flops 9395240960 | bytes 14680064 | tf_op jit(solution)/shard_map/regions/pallas_call | solution.py:436
  181.3 1.6 collective-permute-start.21
  184.1 1.5 collective-permute-start.17
  186.1 1.5 collective-permute-start.19
  188.3 1.5 collective-permute-done.17.refs_1_
  189.8 3.6 %collective-permute-done.18.refs_2_ = f32[256,128]{1,0:T(8,128)S(1)} collective-permute-done((f32[256,128]{1,0:T(8,128)S(1)}, f32[256,128]{1,0:T(8,128)S(1)}, u32[]{:S(2)}, u32[]{:S(2)}) %collective-permute-start.18) | collective-permute-done | bytes 131104 | tf_op jit(solution)/shard_map/ppermute | solution.py:535
  193.5 4.8 %small_backward.1 = (bf16[256,128]{1,0:T(8,128)(2,1)S(1)}, f32[336,128]{1,0:T(8,128)S(1)}) custom-call(f32[256,128]{1,0:T(8,128)S(1)} %get-tuple-element.159.refs_0_, f32[256,128]{1,0:T(8,128)S(1)} %collective-permute-done.17.refs_1_, f32[256,128]{1,0:T(8,128)S(1)} %collective-permute-done.18.refs_2_, f32[256,128]{1,0:T(8,128)S(1)} %collective-permute-done.19.refs_3_, ...), custom_call_target="tpu_custom_call" | custom-call | tf_op jit(solution)/shard_map/small_backward/pallas_call | solution.py:221
  200.1 1.5 collective-permute-start.22
  202.1 1.5 collective-permute-start.24
  204.4 1.8 collective-permute-done.23.refs_2_
  209.4 7.4 %outer.3 = (s16[960,256]{1,0:T(8,128)(2,1)S(1)}, f32[32,3584]{1,0:T(8,128)S(1)}, f32[32,3584]{1,0:T(8,128)S(1)}) custom-call(s32[3]{0:T(128)S(1)} %copy-done.33, bf16[2048,25088]{1,0:T(8,128)(2,1)} %x_ref.15, bf16[128,2048]{1,0:T(8,128)(2,1)S(1)} %left.1.left_ref), custom_call_target="tpu_custom_call" | custom-call | flops 1879048192 | bytes 14680064 | tf_op jit(solution)/shard_map/outer/pallas_call | solution.py:489
  217.7 2.3 collective-permute-start.32
  220.0 1.8 collective-permute-start.31
  223.2 9.9 %outer.4 = (s16[1440,256]{1,0:T(8,128)(2,1)S(1)}, f32[32,5376]{1,0:T(8,128)S(1)}, f32[32,5376]{1,0:T(8,128)S(1)}) custom-call(s32[3]{0:T(128)S(1)} %copy-done.33, bf16[2048,25088]{1,0:T(8,128)(2,1)} %x_ref.15, bf16[128,2048]{1,0:T(8,128)(2,1)S(1)} %left.1.left_ref), custom_call_target="tpu_custom_call" | custom-call | flops 2818572288 | bytes 22020096 | tf_op jit(solution)/shard_map/outer/pallas_call | solution.py:489
  233.8 4.1 %collective-permute-done.31.got_ref = s16[960,256]{1,0:T(8,128)(2,1)S(1)} collective-permute-done((s16[960,256]{1,0:T(8,128)(2,1)}, s16[960,256]{1,0:T(8,128)(2,1)S(1)}, u32[]{:S(2)}, u32[]{:S(2)}) %collective-permute-start.31) | collective-permute-done | bytes 491552 | tf_op jit(solution)/shard_map/ppermute | solution.py:236
  238.9 1.5 collective-permute-start.38
  241.5 2.0 collective-permute-start.34
  243.6 2.2 collective-permute-start.36
  245.8 7.9 %outer.5 = (s16[960,256]{1,0:T(8,128)(2,1)}, f32[32,3584]{1,0:T(8,128)S(1)}, f32[32,3584]{1,0:T(8,128)S(1)}) custom-call(s32[3]{0:T(128)S(1)} %copy-done.33, bf16[2048,25088]{1,0:T(8,128)(2,1)} %x_ref.15, bf16[128,2048]{1,0:T(8,128)(2,1)S(1)} %left.1.left_ref), custom_call_target="tpu_custom_call" | custom-call | flops 1879048192 | bytes 14680064 | tf_op jit(solution)/shard_map/outer/pallas_call | solution.py:489
  253.7 6.0 %collective-permute-done.34.got_ref = s16[480,256]{1,0:T(8,128)(2,1)S(1)} collective-permute-done((s16[480,256]{1,0:T(8,128)(2,1)S(1)}, s16[480,256]{1,0:T(8,128)(2,1)S(1)}, u32[]{:S(2)}, u32[]{:S(2)}) %collective-permute-start.34) | collective-permute-done | bytes 245792 | tf_op jit(solution)/shard_map/ppermute | solution.py:251
  261.0 2.2 collective-permute-start.39
  266.3 1.3 collective-permute-start.37
  268.8 1.4 collective-permute-start.41
  272.4 8.7 %collective-permute-done.35.got_ref = s16[720,256]{1,0:T(8,128)(2,1)} collective-permute-done((s16[720,256]{1,0:T(8,128)(2,1)}, s16[720,256]{1,0:T(8,128)(2,1)}, u32[]{:S(2)}, u32[]{:S(2)}) %collective-permute-start.35) | collective-permute-done | bytes 368672 | tf_op jit(solution)/shard_map/ppermute | solution.py:251
  284.7 3.0 collective-permute-start.45
  288.1 3.7 %collective-permute-done.45 = f32[266,128]{1,0:T(8,128)S(1)} collective-permute-done((f32[266,128]{1,0:T(8,128)S(1)}, f32[266,128]{1,0:T(8,128)S(1)}, u32[]{:S(2)}, u32[]{:S(2)}) %collective-permute-start.45) | collective-permute-done | bytes 136224 | tf_op jit(solution)/shard_map/ppermute | solution.py:598
  291.8 2.7 collective-permute-start.40
  294.9 14.8 %collective-permute-done.40.got_ref = s16[480,256]{1,0:T(8,128)(2,1)S(1)} collective-permute-done((s16[480,256]{1,0:T(8,128)(2,1)S(1)}, s16[480,256]{1,0:T(8,128)(2,1)S(1)}, u32[]{:S(2)}, u32[]{:S(2)}) %collective-permute-start.40) | collective-permute-done | bytes 245792 | tf_op jit(solution)/shard_map/ppermute | solution.py:251
  316.6 1.7 copy-done.46
  (230 shorter events, 50.1 us)
Async XLA Ops:
  3.6 23.3 %collective-permute-start = (bf16[7168,128]{1,0:T(8,128)(2,1)}, bf16[7168,128]{1,0:T(8,128)(2,1)S(1)}, u32[]{:S(2)}, u32[]{:S(2)}) collective-permute-start(bf16[7168,128]{1,0:T(8,128)(2,1)} %dynamic-slice_bitcast_fusion), channel_id=1, source_target_pairs={{0,16},{16,0},{1,17},{17,1},{2,18},{18,2},{3,19},{19,3},{4,20},{20... | collective-permute-start | bytes 5505032 | tf_op jit(solution)/shard_map/ppermute | solution.py:515
  6.6 7.7 %collective-permute-start.1 = (bf16[5376,128]{1,0:T(8,128)(2,1)}, bf16[5376,128]{1,0:T(8,128)(2,1)S(1)}, u32[]{:S(2)}, u32[]{:S(2)}) collective-permute-start(bf16[5376,128]{1,0:T(8,128)(2,1)} %dynamic-slice_bitcast_fusion.1), channel_id=1, source_target_pairs={{0,16},{16,0},{1,17},{17,1},{2,18},{18,2},{3,19},{19,3},{4,20},{20... | collective-permute-start | bytes 4128776 | tf_op jit(solution)/shard_map/ppermute | solution.py:515
  41.7 2.0 collective-permute-start.2
  43.8 7.4 %collective-permute-start.3 = (f32[256,128]{1,0:T(8,128)S(1)}, f32[256,128]{1,0:T(8,128)S(1)}, u32[]{:S(2)}, u32[]{:S(2)}) collective-permute-start(f32[256,128]{1,0:T(8,128)S(1)} %get-tuple-element.230), channel_id=1, source_target_pairs={{0,1},{1,0},{2,3},{3,2},{4,5},{5,4},{6,7},{7,6},{8,9},{9,8},{10,11... | collective-permute-start | bytes 393224 | tf_op jit(solution)/shard_map/ppermute | solution.py:535
  46.8 8.1 %collective-permute-start.4 = (f32[256,128]{1,0:T(8,128)S(1)}, f32[256,128]{1,0:T(8,128)S(1)}, u32[]{:S(2)}, u32[]{:S(2)}) collective-permute-start(f32[256,128]{1,0:T(8,128)S(1)} %get-tuple-element.229), channel_id=1, source_target_pairs={{0,2},{1,3},{2,0},{3,1},{4,6},{5,7},{6,4},{7,5},{8,10},{9,11},{10,... | collective-permute-start | bytes 393224 | tf_op jit(solution)/shard_map/ppermute | solution.py:535
  48.3 6.6 %collective-permute-start.5 = (f32[256,128]{1,0:T(8,128)S(1)}, f32[256,128]{1,0:T(8,128)S(1)}, u32[]{:S(2)}, u32[]{:S(2)}) collective-permute-start(f32[256,128]{1,0:T(8,128)S(1)} %get-tuple-element.228), channel_id=1, source_target_pairs={{0,3},{1,2},{2,1},{3,0},{4,7},{5,6},{6,5},{7,4},{8,11},{9,10},{10,... | collective-permute-start | bytes 393224 | tf_op jit(solution)/shard_map/ppermute | solution.py:535
  59.2 4.6 %collective-permute-start.6 = (bf16[256,128]{1,0:T(8,128)(2,1)S(1)}, bf16[256,128]{1,0:T(8,128)(2,1)S(1)}, u32[]{:S(2)}, u32[]{:S(2)}) collective-permute-start(bf16[256,128]{1,0:T(8,128)(2,1)S(1)} %get-tuple-element.138.refs_0_), channel_id=1, source_target_pairs={{0,1},{1,0},{2,3},{3,2},{4,5},{5,4},{6,7},{7,6},{8,9},{9,8},{10,11... | collective-permute-start | bytes 196616 | tf_op jit(solution)/shard_map/ppermute | solution.py:544
  60.4 4.4 %collective-permute-start.7 = (bf16[256,128]{1,0:T(8,128)(2,1)S(1)}, bf16[256,128]{1,0:T(8,128)(2,1)S(1)}, u32[]{:S(2)}, u32[]{:S(2)}) collective-permute-start(bf16[256,128]{1,0:T(8,128)(2,1)S(1)} %get-tuple-element.138.refs_0_), channel_id=1, source_target_pairs={{0,2},{1,3},{2,0},{3,1},{4,6},{5,7},{6,4},{7,5},{8,10},{9,11},{10,... | collective-permute-start | bytes 196616 | tf_op jit(solution)/shard_map/ppermute | solution.py:544
  61.2 5.2 %collective-permute-start.8 = (bf16[256,128]{1,0:T(8,128)(2,1)S(1)}, bf16[256,128]{1,0:T(8,128)(2,1)S(1)}, u32[]{:S(2)}, u32[]{:S(2)}) collective-permute-start(bf16[256,128]{1,0:T(8,128)(2,1)S(1)} %get-tuple-element.138.refs_0_), channel_id=1, source_target_pairs={{0,3},{1,2},{2,1},{3,0},{4,7},{5,6},{6,5},{7,4},{8,11},{9,10},{10,... | collective-permute-start | bytes 196616 | tf_op jit(solution)/shard_map/ppermute | solution.py:544
  62.7 3.8 %collective-permute-start.9 = (bf16[256,128]{1,0:T(8,128)(2,1)S(1)}, bf16[256,128]{1,0:T(8,128)(2,1)S(1)}, u32[]{:S(2)}, u32[]{:S(2)}) collective-permute-start(bf16[256,128]{1,0:T(8,128)(2,1)S(1)} %get-tuple-element.138.refs_0_), channel_id=1, source_target_pairs={{0,16},{16,0},{1,17},{17,1},{2,18},{18,2},{3,19},{19,3},{4,20},{20... | collective-permute-start | bytes 196616 | tf_op jit(solution)/shard_map/ppermute | solution.py:515
  63.7 2.7 collective-permute-start.10
  64.8 1.7 collective-permute-start.11
  66.4 1.3 collective-permute-start.12
  112.4 32.6 %collective-permute-start.13 = (s16[1440,256]{1,0:T(8,128)(2,1)}, s16[1440,256]{1,0:T(8,128)(2,1)S(1)}, u32[]{:S(2)}, u32[]{:S(2)}) collective-permute-start(s16[1440,256]{1,0:T(8,128)(2,1)} %get-tuple-element.147), channel_id=1, source_target_pairs={{0,4},{4,0},{8,12},{12,8},{1,5},{5,1},{9,13},{13,9},{2,6},{6,2},{1... | collective-permute-start | bytes 2211848 | tf_op jit(solution)/shard_map/ppermute | solution.py:236
  144.5 34.0 %collective-permute-start.15 = (s16[960,256]{1,0:T(8,128)(2,1)}, s16[960,256]{1,0:T(8,128)(2,1)S(1)}, u32[]{:S(2)}, u32[]{:S(2)}) collective-permute-start(s16[960,256]{1,0:T(8,128)(2,1)} %get-tuple-element.154), channel_id=1, source_target_pairs={{0,4},{4,0},{8,12},{12,8},{1,5},{5,1},{9,13},{13,9},{2,6},{6,2},{1... | collective-permute-start | bytes 1474568 | tf_op jit(solution)/shard_map/ppermute | solution.py:236
  145.5 33.0 %collective-permute-start.14 = (s16[720,256]{1,0:T(8,128)(2,1)S(1)}, s16[720,256]{1,0:T(8,128)(2,1)S(1)}, u32[]{:S(2)}, u32[]{:S(2)}) collective-permute-start(s16[720,256]{1,0:T(8,128)(2,1)S(1)} %get-tuple-element.151), channel_id=1, source_target_pairs={{0,8},{4,12},{8,0},{12,4},{1,9},{5,13},{9,1},{13,5},{2,10},{6,14},... | collective-permute-start | bytes 1105928 | tf_op jit(solution)/shard_map/ppermute | solution.py:251
  179.8 3.1 collective-permute-start.16
  181.0 18.0 %collective-permute-start.20 = (s16[480,256]{1,0:T(8,128)(2,1)S(1)}, s16[480,256]{1,0:T(8,128)(2,1)S(1)}, u32[]{:S(2)}, u32[]{:S(2)}) collective-permute-start(s16[480,256]{1,0:T(8,128)(2,1)S(1)} %get-tuple-element.158), channel_id=1, source_target_pairs={{0,8},{4,12},{8,0},{12,4},{1,9},{5,13},{9,1},{13,5},{2,10},{6,14},... | collective-permute-start | bytes 737288 | tf_op jit(solution)/shard_map/ppermute | solution.py:251
  181.3 18.8 %collective-permute-start.21 = (s16[960,256]{1,0:T(8,128)(2,1)}, s16[960,256]{1,0:T(8,128)(2,1)S(1)}, u32[]{:S(2)}, u32[]{:S(2)}) collective-permute-start(s16[960,256]{1,0:T(8,128)(2,1)} %get-tuple-element.168), channel_id=1, source_target_pairs={{0,4},{4,0},{8,12},{12,8},{1,5},{5,1},{9,13},{13,9},{2,6},{6,2},{1... | collective-permute-start | bytes 1474568 | tf_op jit(solution)/shard_map/ppermute | solution.py:236
  184.1 5.8 %collective-permute-start.17 = (f32[256,128]{1,0:T(8,128)S(1)}, f32[256,128]{1,0:T(8,128)S(1)}, u32[]{:S(2)}, u32[]{:S(2)}) collective-permute-start(f32[256,128]{1,0:T(8,128)S(1)} %get-tuple-element.226), channel_id=1, source_target_pairs={{0,1},{1,0},{2,3},{3,2},{4,5},{5,4},{6,7},{7,6},{8,9},{9,8},{10,11... | collective-permute-start | bytes 393224 | tf_op jit(solution)/shard_map/ppermute | solution.py:535
  185.6 7.8 %collective-permute-start.18 = (f32[256,128]{1,0:T(8,128)S(1)}, f32[256,128]{1,0:T(8,128)S(1)}, u32[]{:S(2)}, u32[]{:S(2)}) collective-permute-start(f32[256,128]{1,0:T(8,128)S(1)} %get-tuple-element.225), channel_id=1, source_target_pairs={{0,2},{1,3},{2,0},{3,1},{4,6},{5,7},{6,4},{7,5},{8,10},{9,11},{10,... | collective-permute-start | bytes 393224 | tf_op jit(solution)/shard_map/ppermute | solution.py:535
  186.1 7.3 %collective-permute-start.19 = (f32[256,128]{1,0:T(8,128)S(1)}, f32[256,128]{1,0:T(8,128)S(1)}, u32[]{:S(2)}, u32[]{:S(2)}) collective-permute-start(f32[256,128]{1,0:T(8,128)S(1)} %get-tuple-element.224), channel_id=1, source_target_pairs={{0,3},{1,2},{2,1},{3,0},{4,7},{5,6},{6,5},{7,4},{8,11},{9,10},{10,... | collective-permute-start | bytes 393224 | tf_op jit(solution)/shard_map/ppermute | solution.py:535
  200.1 4.3 %collective-permute-start.22 = (bf16[256,128]{1,0:T(8,128)(2,1)S(1)}, bf16[256,128]{1,0:T(8,128)(2,1)S(1)}, u32[]{:S(2)}, u32[]{:S(2)}) collective-permute-start(bf16[256,128]{1,0:T(8,128)(2,1)S(1)} %get-tuple-element.169.refs_0_), channel_id=1, source_target_pairs={{0,1},{1,0},{2,3},{3,2},{4,5},{5,4},{6,7},{7,6},{8,9},{9,8},{10,11... | collective-permute-start | bytes 196616 | tf_op jit(solution)/shard_map/ppermute | solution.py:544
  201.6 4.6 %collective-permute-start.23 = (bf16[256,128]{1,0:T(8,128)(2,1)S(1)}, bf16[256,128]{1,0:T(8,128)(2,1)S(1)}, u32[]{:S(2)}, u32[]{:S(2)}) collective-permute-start(bf16[256,128]{1,0:T(8,128)(2,1)S(1)} %get-tuple-element.169.refs_0_), channel_id=1, source_target_pairs={{0,2},{1,3},{2,0},{3,1},{4,6},{5,7},{6,4},{7,5},{8,10},{9,11},{10,... | collective-permute-start | bytes 196616 | tf_op jit(solution)/shard_map/ppermute | solution.py:544
  202.1 5.2 %collective-permute-start.24 = (bf16[256,128]{1,0:T(8,128)(2,1)S(1)}, bf16[256,128]{1,0:T(8,128)(2,1)S(1)}, u32[]{:S(2)}, u32[]{:S(2)}) collective-permute-start(bf16[256,128]{1,0:T(8,128)(2,1)S(1)} %get-tuple-element.169.refs_0_), channel_id=1, source_target_pairs={{0,3},{1,2},{2,1},{3,0},{4,7},{5,6},{6,5},{7,4},{8,11},{9,10},{10,... | collective-permute-start | bytes 196616 | tf_op jit(solution)/shard_map/ppermute | solution.py:544
  203.6 4.0 %collective-permute-start.25 = (bf16[256,128]{1,0:T(8,128)(2,1)S(1)}, bf16[256,128]{1,0:T(8,128)(2,1)S(1)}, u32[]{:S(2)}, u32[]{:S(2)}) collective-permute-start(bf16[256,128]{1,0:T(8,128)(2,1)S(1)} %get-tuple-element.169.refs_0_), channel_id=1, source_target_pairs={{0,16},{16,0},{1,17},{17,1},{2,18},{18,2},{3,19},{19,3},{4,20},{20... | collective-permute-start | bytes 196616 | tf_op jit(solution)/shard_map/ppermute | solution.py:515
  204.4 3.2 %collective-permute-start.26 = (bf16[256,128]{1,0:T(8,128)(2,1)S(1)}, bf16[256,128]{1,0:T(8,128)(2,1)S(1)}, u32[]{:S(2)}, u32[]{:S(2)}) collective-permute-start(bf16[256,128]{1,0:T(8,128)(2,1)S(1)} %collective-permute-done.22.refs_1_), channel_id=1, source_target_pairs={{0,16},{16,0},{1,17},{17,1},{2,18},{18,2},{3,19},{19,3},{4,20},{20... | collective-permute-start | bytes 196616 | tf_op jit(solution)/shard_map/ppermute | solution.py:515
  206.2 1.4 collective-permute-start.27
  207.3 1.3 collective-permute-start.28
  217.6 4.2 %collective-permute-start.29 = (f32[168,128]{1,0:T(8,128)S(1)}, f32[168,128]{1,0:T(8,128)S(1)}, u32[]{:S(2)}, u32[]{:S(2)}) collective-permute-start(f32[168,128]{1,0:T(8,128)S(1)} %constant_dynamic-slice_fusion), channel_id=1, source_target_pairs={{0,16},{16,0},{1,17},{17,1},{2,18},{18,2},{3,19},{19,3},{4,20},{20... | collective-permute-start | bytes 258056 | tf_op jit(solution)/shard_map/ppermute | solution.py:515
  217.7 15.4 %collective-permute-start.32 = (s16[480,256]{1,0:T(8,128)(2,1)S(1)}, s16[480,256]{1,0:T(8,128)(2,1)S(1)}, u32[]{:S(2)}, u32[]{:S(2)}) collective-permute-start(s16[480,256]{1,0:T(8,128)(2,1)S(1)} %get-tuple-element.172), channel_id=1, source_target_pairs={{0,8},{4,12},{8,0},{12,4},{1,9},{5,13},{9,1},{13,5},{2,10},{6,14},... | collective-permute-start | bytes 737288 | tf_op jit(solution)/shard_map/ppermute | solution.py:251
  220.0 17.9 %collective-permute-start.31 = (s16[960,256]{1,0:T(8,128)(2,1)}, s16[960,256]{1,0:T(8,128)(2,1)S(1)}, u32[]{:S(2)}, u32[]{:S(2)}) collective-permute-start(s16[960,256]{1,0:T(8,128)(2,1)} %copy-done.45), channel_id=1, source_target_pairs={{0,4},{4,0},{8,12},{12,8},{1,5},{5,1},{9,13},{13,9},{2,6},{6,2},{1... | collective-permute-start | bytes 1474568 | tf_op jit(solution)/shard_map/ppermute | solution.py:236
  221.9 11.2 %collective-permute-start.30 = (f32[168,128]{1,0:T(8,128)S(1)}, f32[168,128]{1,0:T(8,128)S(1)}, u32[]{:S(2)}, u32[]{:S(2)}) collective-permute-start(f32[168,128]{1,0:T(8,128)S(1)} %dynamic-slice_add_fusion.2), channel_id=1, source_target_pairs={{0,1},{1,0},{2,3},{3,2},{4,5},{5,4},{6,7},{7,6},{8,9},{9,8},{10,11... | collective-permute-start | bytes 258056 | tf_op jit(solution)/shard_map/ppermute | solution.py:598
  237.9 23.1 %collective-permute-start.33 = (s16[1440,256]{1,0:T(8,128)(2,1)S(1)}, s16[1440,256]{1,0:T(8,128)(2,1)S(1)}, u32[]{:S(2)}, u32[]{:S(2)}) collective-permute-start(s16[1440,256]{1,0:T(8,128)(2,1)S(1)} %get-tuple-element.180), channel_id=1, source_target_pairs={{0,4},{4,0},{8,12},{12,8},{1,5},{5,1},{9,13},{13,9},{2,6},{6,2},{1... | collective-permute-start | bytes 2211848 | tf_op jit(solution)/shard_map/ppermute | solution.py:236
  238.9 6.9 %collective-permute-start.38 = (f32[168,128]{1,0:T(8,128)S(1)}, f32[168,128]{1,0:T(8,128)S(1)}, u32[]{:S(2)}, u32[]{:S(2)}) collective-permute-start(f32[168,128]{1,0:T(8,128)S(1)} %add.95), channel_id=1, source_target_pairs={{0,2},{1,3},{2,0},{3,1},{4,6},{5,7},{6,4},{7,5},{8,10},{9,11},{10,... | collective-permute-start | bytes 258056 | tf_op jit(solution)/shard_map/ppermute | solution.py:598
  241.5 18.2 %collective-permute-start.34 = (s16[480,256]{1,0:T(8,128)(2,1)S(1)}, s16[480,256]{1,0:T(8,128)(2,1)S(1)}, u32[]{:S(2)}, u32[]{:S(2)}) collective-permute-start(s16[480,256]{1,0:T(8,128)(2,1)S(1)} %get-tuple-element.183), channel_id=1, source_target_pairs={{0,8},{4,12},{8,0},{12,4},{1,9},{5,13},{9,1},{13,5},{2,10},{6,14},... | collective-permute-start | bytes 737288 | tf_op jit(solution)/shard_map/ppermute | solution.py:251
  243.6 41.1 %collective-permute-start.36 = (f32[32,5376]{1,0:T(8,128)S(1)}, f32[32,5376]{1,0:T(8,128)}, u32[]{:S(2)}, u32[]{:S(2)}) collective-permute-start(f32[32,5376]{1,0:T(8,128)S(1)} %total.7), channel_id=1, source_target_pairs={{0,16},{1,17},{2,18},{3,19},{4,20},{5,21},{6,22},{7,23},{8,24},{9,... | collective-permute-start | bytes 2064392 | tf_op jit(solution)/shard_map/ppermute | solution.py:800
  261.0 22.4 %collective-permute-start.39 = (s16[960,256]{1,0:T(8,128)(2,1)}, s16[960,256]{1,0:T(8,128)(2,1)S(1)}, u32[]{:S(2)}, u32[]{:S(2)}) collective-permute-start(s16[960,256]{1,0:T(8,128)(2,1)} %get-tuple-element.196), channel_id=1, source_target_pairs={{0,4},{4,0},{8,12},{12,8},{1,5},{5,1},{9,13},{13,9},{2,6},{6,2},{1... | collective-permute-start | bytes 1474568 | tf_op jit(solution)/shard_map/ppermute | solution.py:236
  264.4 16.6 %collective-permute-start.35 = (s16[720,256]{1,0:T(8,128)(2,1)}, s16[720,256]{1,0:T(8,128)(2,1)}, u32[]{:S(2)}, u32[]{:S(2)}) collective-permute-start(s16[720,256]{1,0:T(8,128)(2,1)} %get-tuple-element.188), channel_id=1, source_target_pairs={{0,8},{4,12},{8,0},{12,4},{1,9},{5,13},{9,1},{13,5},{2,10},{6,14},... | collective-permute-start | bytes 1105928 | tf_op jit(solution)/shard_map/ppermute | solution.py:251
  266.3 28.2 %collective-permute-start.37 = (f32[32,3584]{1,0:T(8,128)S(1)}, f32[32,3584]{1,0:T(8,128)S(1)}, u32[]{:S(2)}, u32[]{:S(2)}) collective-permute-start(f32[32,3584]{1,0:T(8,128)S(1)} %total.9), channel_id=1, source_target_pairs={{0,16},{1,17},{2,18},{3,19},{4,20},{5,21},{6,22},{7,23},{8,24},{9,... | collective-permute-start | bytes 1376264 | tf_op jit(solution)/shard_map/ppermute | solution.py:800
  268.8 25.7 %collective-permute-start.41 = (f32[32,3584]{1,0:T(8,128)S(1)}, f32[32,3584]{1,0:T(8,128)S(1)}, u32[]{:S(2)}, u32[]{:S(2)}) collective-permute-start(f32[32,3584]{1,0:T(8,128)S(1)} %total.11), channel_id=1, source_target_pairs={{0,16},{1,17},{2,18},{3,19},{4,20},{5,21},{6,22},{7,23},{8,24},{9,... | collective-permute-start | bytes 1376264 | tf_op jit(solution)/shard_map/ppermute | solution.py:800
  281.0 35.4 %collective-permute-start.43 = (f32[32,3584]{1,0:T(8,128)S(1)}, f32[32,3584]{1,0:T(8,128)S(1)}, u32[]{:S(2)}, u32[]{:S(2)}) collective-permute-start(f32[32,3584]{1,0:T(8,128)S(1)} %total.8), channel_id=1, source_target_pairs={{16,0},{17,1},{18,2},{19,3},{20,4},{21,5},{22,6},{23,7},{24,8},{25... | collective-permute-start | bytes 1376264 | tf_op jit(solution)/shard_map/ppermute | solution.py:802
  283.4 32.9 %collective-permute-start.42 = (f32[32,5376]{1,0:T(8,128)S(1)}, f32[32,5376]{1,0:T(8,128)S(1)}, u32[]{:S(2)}, u32[]{:S(2)}) collective-permute-start(f32[32,5376]{1,0:T(8,128)S(1)} %total.6), channel_id=1, source_target_pairs={{16,0},{17,1},{18,2},{19,3},{20,4},{21,5},{22,6},{23,7},{24,8},{25... | collective-permute-start | bytes 2064392 | tf_op jit(solution)/shard_map/ppermute | solution.py:802
  284.7 7.1 %collective-permute-start.45 = (f32[266,128]{1,0:T(8,128)S(1)}, f32[266,128]{1,0:T(8,128)S(1)}, u32[]{:S(2)}, u32[]{:S(2)}) collective-permute-start(f32[266,128]{1,0:T(8,128)S(1)} %pad_maximum_fusion), channel_id=1, source_target_pairs={{0,4},{4,0},{8,12},{12,8},{1,5},{5,1},{9,13},{13,9},{2,6},{6,2},{1... | collective-permute-start | bytes 408584 | tf_op jit(solution)/shard_map/ppermute | solution.py:598
  291.8 17.9 %collective-permute-start.40 = (s16[480,256]{1,0:T(8,128)(2,1)S(1)}, s16[480,256]{1,0:T(8,128)(2,1)S(1)}, u32[]{:S(2)}, u32[]{:S(2)}) collective-permute-start(s16[480,256]{1,0:T(8,128)(2,1)S(1)} %get-tuple-element.201), channel_id=1, source_target_pairs={{0,8},{4,12},{8,0},{12,4},{1,9},{5,13},{9,1},{13,5},{2,10},{6,14},... | collective-permute-start | bytes 737288 | tf_op jit(solution)/shard_map/ppermute | solution.py:251
  294.5 17.5 %collective-permute-start.46 = (f32[266,128]{1,0:T(8,128)S(1)}, f32[266,128]{1,0:T(8,128)S(1)}, u32[]{:S(2)}, u32[]{:S(2)}) collective-permute-start(f32[266,128]{1,0:T(8,128)S(1)} %add.97), channel_id=1, source_target_pairs={{0,8},{4,12},{8,0},{12,4},{1,9},{5,13},{9,1},{13,5},{2,10},{6,14},... | collective-permute-start | bytes 408584 | tf_op jit(solution)/shard_map/ppermute | solution.py:598
  309.8 6.7 %collective-permute-start.44 = (f32[32,3584]{1,0:T(8,128)S(1)}, f32[32,3584]{1,0:T(8,128)S(1)}, u32[]{:S(2)}, u32[]{:S(2)}) collective-permute-start(f32[32,3584]{1,0:T(8,128)S(1)} %total.10), channel_id=1, source_target_pairs={{16,0},{17,1},{18,2},{19,3},{20,4},{21,5},{22,6},{23,7},{24,8},{25... | collective-permute-start | bytes 1376264 | tf_op jit(solution)/shard_map/ppermute | solution.py:802
  312.1 1.6 collective-permute-start.47
  (55 other events, 704.2 us)

commit v4 on v3

--- a/solution.py
+++ b/solution.py
@@ -280,13 +280,13 @@
     return [pl.BlockSpec((chunk, width), kept), pl.BlockSpec((chunk, width), got)]
 
 
-def project_kernel(started, half_ref, x_ref, kept_ref, got_ref, keep_ref, log_ref, *refs):
+def project_kernel(started, half_ref, x_ref, kept_ref, got_ref, bias_ref, factor_ref, keep_ref, *refs):
     out_ref, seen_ref = refs[-2:]
     chunk, width = kept_ref.shape
     keep = keep_ref[...]
     row = lax.broadcasted_iota(jnp.int32, (width, chunk), 0)
     terms = jnp.where(row == 0, keep, 0.0)
-    rest = keep * log_ref[...]
+    rest = keep * (bias_ref[...] + jnp.log(factor_ref[...]))
     for place in range(1, 4):
         high = rest.astype(jnp.bfloat16).astype(jnp.float32)
         terms = jnp.where(row == place, high, terms)
@@ -305,10 +305,10 @@
         seen_ref[...] += part[:, width:]
 
 
-def project(half, peaks, kept, got, keep, log_fa, before, first, got_first, count, chunk, per_half):
+def project(half, peaks, kept, got, region_rows, before, first, got_first, count, chunk, per_half):
     cells, width = peaks.shape[0], kept.shape[1]
     whole = pl.BlockSpec((cells, width), lambda j, h: (0, 0))
-    row = pl.BlockSpec((1, chunk), lambda j, h: (0, first + j))
+    row = pl.BlockSpec((1, chunk), lambda j, h: (0, h[0] * per_half + first + j))
     return pl.pallas_call(
         functools.partial(project_kernel, bool(before)),
         grid_spec=pltpu.PrefetchScalarGridSpec(
@@ -317,6 +317,7 @@
             in_specs=[
                 pl.BlockSpec((cells, chunk), lambda j, h: (0, h[0] * per_half + first + j)),
                 *weight_specs(chunk, width, per_half, first, got_first, True),
+                row,
                 row,
                 row,
             ]
@@ -329,12 +330,12 @@
             flops=2 * cells * count * chunk * width, bytes_accessed=2 * cells * count * chunk, transcendentals=0
         ),
         name="project",
-    )(half, peaks, kept, got, keep, log_fa, *before)
+    )(half, peaks, kept, got, *region_rows, *before)
 
 
 def regions_kernel(
-    tile, rows_at_once, piece, started, coded, half_ref, x_ref, kept_ref, got_ref, g_ref, gt_ref, a_ref, fa_ref, ck_ref, cf_ref,
-    *refs,
+    tile, rows_at_once, piece, norm_scale, cut, started, coded, half_ref, x_ref, kept_ref, got_ref, rest_ref, g_ref, gt_ref, bias_in_ref, factor_ref, keep_ref,
+    cf_ref, *refs,
 ):
     outs = refs[1 if started else 0 :]
     dg_ref, bias_ref, loss_ref = outs[:3]
@@ -343,7 +344,8 @@
     blocks = cells // rows_at_once
     M, E = (m0, m1), (e0, e1)
 
-    w_ref[...] = chosen(half_ref[1], False, kept_ref, got_ref)
+    got = jnp.where(pl.program_id(0) < cut, got_ref[...], rest_ref[...])
+    w_ref[...] = jnp.where(half_ref[1] == 1, kept_ref[...], got)
 
     @pl.when(pl.program_id(0) == 0)
     def first():
@@ -355,9 +357,10 @@
         w = w_ref[cols, :]
         w2 = jnp.concatenate([w, w], axis=1)
         wide = (8, tile)
-        a = jnp.broadcast_to(a_ref[:, cols], wide)[None]
-        fa = jnp.broadcast_to(fa_ref[:, cols], wide)[None]
-        ck = jnp.broadcast_to(ck_ref[:, cols], wide)[None]
+        bias_row = jnp.exp(bias_in_ref[:, cols])
+        a = jnp.broadcast_to(bias_row, wide)[None]
+        fa = jnp.broadcast_to(bias_row * factor_ref[:, cols], wide)[None]
+        ck = jnp.broadcast_to(keep_ref[:, cols] * norm_scale, wide)[None]
 
         def rows(i, o=0, n=rows_at_once):
             return pl.ds(pl.multiple_of(i * rows_at_once + o, 16), n)
@@ -395,12 +398,11 @@
                 dw_ref[:, cols] += part
 
         def step(i, s, sums, logits=True, grads=True, start=False):
-            dots = rows_at_once // 2
+            if logits:
+                logit(i + 1, 1 - s, 0, rows_at_once)
             for o in range(0, rows_at_once, piece):
-                if logits and o % dots == 0:
-                    logit(i + 1, 1 - s, o, dots)
                 sums = elementwise(i, s, o, sums)
-                if grads and o == dots:
+                if grads and o == rows_at_once // 2:
                     cell_grad(i - 1, 1 - s)
             if grads:
                 region_grad(i - 1, 1 - s, start)
@@ -425,22 +427,25 @@
         give_shares(half_ref[2], dw_ref, *outs[3:6])
 
 
-def regions_pass(half, peaks, kept, got, hidden, hidden_t, a, fa, ck, cf, before, first, at, count, chunk, per_half, coded):
+def regions_pass(norm_scale, half, peaks, kept, got_pair, hidden, hidden_t, region_rows, cf, before, first, count, chunk, per_half, coded):
     cells, width = peaks.shape[0], kept.shape[1]
     blocks, _, rows = hidden_t.shape
     tile, piece = min(256, chunk), 64
+    cut = got_pair[0].shape[0] // chunk
     started = before is not None
     whole = pl.BlockSpec((cells, width), lambda j, h: (0, 0))
-    row = pl.BlockSpec((1, chunk), lambda j, h: (0, first + j))
+    row = pl.BlockSpec((1, chunk), lambda j, h: (0, h[0] * per_half + first + j))
     share_specs, share_shapes = share_outputs(width, chunk, count, coded)
     return pl.pallas_call(
-        functools.partial(regions_kernel, tile, rows, piece, started, coded),
+        functools.partial(regions_kernel, tile, rows, piece, norm_scale, cut - first, started, coded),
         grid_spec=pltpu.PrefetchScalarGridSpec(
             num_scalar_prefetch=1,
             grid=(count,),
             in_specs=[
                 pl.BlockSpec((cells, chunk), lambda j, h: (0, h[0] * per_half + first + j)),
-                *weight_specs(chunk, width, per_half, first, at, False),
+                *weight_specs(chunk, width, per_half, first, first, False)[:1],
+                pl.BlockSpec((chunk, width), lambda j, h: (jnp.where(h[1] == 1, 0, jnp.minimum(first + j, cut - 1)), 0)),
+                pl.BlockSpec((chunk, width), lambda j, h: (jnp.where(h[1] == 1, 0, jnp.maximum(first + j - cut, 0)), 0)),
                 pl.BlockSpec((cells, 2 * width), lambda j, h: (0, 0)),
                 pl.BlockSpec((blocks, width, rows), lambda j, h: (0, 0, 0)),
                 row, row, row, whole,
@@ -470,7 +475,7 @@
             transcendentals=16 * cells * count * chunk,
         ),
         name="regions",
-    )(half, peaks, kept, got, hidden, hidden_t, a, fa, ck, cf, *([before] if started else []))
+    )(half, peaks, kept, *got_pair, hidden, hidden_t, *region_rows, cf, *([before] if started else []))
 
 
 def outer_kernel(coded, half_ref, x_ref, left_ref, *outs):
@@ -645,22 +650,23 @@
     def of_core(values, core, axis=0):
         return lax.dynamic_slice_in_dim(values, core * (regions_local - window), window, axis)
 
-    keep = of_core(region_keep, pipe).astype(jnp.float32)
+    region_rows = [out_bias, region_factor, region_keep.astype(jnp.float32)]
     dp_at = lax.axis_index("dp")
     place = jnp.stack([pipe, mine, dp_at]).astype(jnp.int32)
     chunk = next(c for c in (1792, 256, 128) if window % c == 0 and (regions_local - window) % c == 0)
     chunks = window // chunk
-    ahead = min(3, chunks - 1) * chunk
+    ahead = min(2, chunks - 1) * chunk
     coded = lax.axis_size("dp") == 4 and chunk % 256 == 0
     if overlap:
         mine_alone = (pipe == 0) | (jnp.arange(window) >= overlap)
-        keep = jnp.where(mine_alone, keep, 0.0)
+        region_rows = [of_core(row, pipe) for row in region_rows]
+        region_rows[2] = jnp.where(mine_alone, region_rows[2], 0.0)
         peak_data = of_core(peak_data, pipe, 1)
         own = of_core(weight, pipe)
         got = across_cores(of_core(weight, 1 - pipe))
         kept_enc = got_enc = jnp.where(mine_alone[:, None], jnp.where(pipe == 0, own, got), 0)
         weight = jnp.where(pipe == 0, got, own)
-        got_spans = [(weight, 0, 0, chunks)]
+        got_pair, got_spans = (weight, weight), [(0, chunks)]
         got_parts = [(kept_enc, got_enc, 0, 0, chunks)]
         half = jnp.stack([jnp.zeros_like(place[0]), place[0], place[2]])
     else:
@@ -669,8 +675,8 @@
         got_rest = across_cores(lax.dynamic_slice_in_dim(weight, other_at + ahead, window - ahead, 0))
         got_parts = [(weight, got_first, 0, 0, ahead // chunk), (weight, got_rest, ahead // chunk, 0, chunks - ahead // chunk)]
         cut = ahead // chunk
-        middle = cut + (chunks - cut) // 2
-        got_spans = [(got_first, 0, 0, cut), (got_rest, 0, cut, middle), (got_rest, middle - cut, middle, chunks)]
+        most = -(-chunks * 4 // 7)
+        got_pair, got_spans = (got_first, got_rest), [(0, most), (most, chunks)]
         half = jnp.stack([place[0], place[0], place[2]])
 
     own_rows = cells // (2 * tensors)
@@ -684,20 +690,17 @@
     )
     dec = (dec_first[:latent], dec_first[latent:], dec_bias_one[None], dec_square, dec_bias_two[None])
 
-    a = jnp.exp(of_core(out_bias, pipe))[None]
-    fa = a * of_core(region_factor, pipe)[None]
-    ck = (keep * norm_scale)[None]
-    log_fa = jnp.log(fa)
+    region_rows = [row[None] for row in region_rows]
     cf_wide = jnp.broadcast_to(cell_factor[:, None], (cells, 128))
     partial = []
     for kept_w, got_w, first, at, count in got_parts:
-        partial = project(half, peak_data, kept_w, got_w, keep[None], log_fa, partial, first, at, count, chunk, chunks)
+        partial = project(half, peak_data, kept_w, got_w, region_rows, partial, first, at, count, chunk, chunks)
     partial, seen = partial
     pieces = scatter_cells(partial)
     owed = jnp.sum(seen[:, 0] * (BIG_BITS * LN2 - jnp.log(cell_factor))) - jnp.sum(seen[:, 1:4])
-    early = (noise_own, ids_own, enc, dec, a, fa, ck, cf_wide, owed[None, None])
+    early = (noise_own, ids_own, enc, dec, cf_wide, owed[None, None])
     pieces, early = lax.optimization_barrier((pieces, early))
-    noise_own, ids_own, enc, dec, a, fa, ck, cf_wide, owed = early
+    noise_own, ids_own, enc, dec, cf_wide, owed = early
     summed, z_low, g2_own, kl_sum = one_step(
         functools.partial(forward_kernel, len(pieces)),
         [*pieces, noise_own, ids_own, *enc, *dec],
@@ -720,14 +723,14 @@
     )
 
     dg2, lines, biases, losses = None, [], [], []
-    for got_w, at, first, end in got_spans:
+    for first, end in got_spans:
         if len(lines) > 1:
             lines[-2] = line_joined(lines[-2], chunk)
             dg2 = after(dg2, lines[-2][0])
             lines[-2] = line_last(lines[-2])
         dg2, bias, loss, *shares = regions_pass(
-            half, peak_data, weight, got_w, hidden, hidden_t, a, fa, ck, cf_wide, dg2, first, at, end - first, chunk,
-            chunks, coded,
+            norm_scale, half, peak_data, weight, got_pair, hidden, hidden_t, region_rows, cf_wide, dg2, first,
+            end - first, chunk, chunks, coded,
         )
         dg2 = after(dg2, *[line[0] for line in lines])
         lines.append(line_start(shares))
@@ -750,23 +753,23 @@
         ],
         "small_backward",
     )
-    dp_own = after(dp_own, *[line[0] for line in lines])
+    gathered = gather_cells(dp_own)
+    lines[-1][0] = after(lines[-1][0], gathered[-1])
     lines[-1] = line_joined(lines[-1], chunk)
-    (left,) = assemble(
-        left_kernel, place, gather_cells(dp_own), [jax.ShapeDtypeStruct((width, cells), jnp.bfloat16)], "left"
-    )
-    left = after(left, lines[-1][0])
+    (left,) = assemble(left_kernel, place, gathered, [jax.ShapeDtypeStruct((width, cells), jnp.bfloat16)], "left")
+    left = after(left, *[line[0] for line in lines])
     lines[-1] = line_last(lines[-1])
 
-    spans = [(first, end) for _, _, first, end in got_spans]
-    order = [1, 0, 2][: len(spans)] if len(spans) > 1 else [0]
+    first, second = max(1, chunks * 2 // 7), max(2, chunks * 5 // 7)
+    spans = [(0, first), (first, second), (second, chunks)] if chunks > 2 else [(0, chunks)]
+    order = list(range(len(spans)))
     enc_lines, under_way = [], []
     for index, (first, end) in enumerate([spans[i] for i in order]):
         if index:
             left = after(left, shares[0])
         if index > 1:
             line = line_joined(under_way.pop(0), chunk)
-            left = after(left, line[0])
+            left = after(left, line[0], pack)
             enc_lines.append(line_last(line))
         shares = list(outer(half, peak_data, left, first, end - first, chunk, chunks, coded))
         if index == min(1, len(spans) - 1):
@@ -775,14 +778,12 @@
             steps = [("tensor", bit) for bit in exchange_bits("tensor")]
             while len(steps) > 1:
                 pack = exchanged(pack, *steps.pop(0))
-            shares[0] = after(shares[0], pack)
         elif index:
             pack = exchanged(pack, *steps.pop(0))
             shares[0] = after(shares[0], pack)
         waiting = shares[0]
-        if index:
-            beside = [line[0] for line in under_way + enc_lines] + ([lines[-1][0]] if index == 1 else [])
-            shares[0] = after(shares[0], *beside)
+        beside = [line[0] for line in under_way + enc_lines] + ([] if index else [lines[-1][0]])
+        shares[0] = after(shares[0], *beside)
         under_way.append(line_start(shares))
     for step in steps:
         pack = exchanged(pack, *step)
@@ -790,8 +791,6 @@
     sums = after(sums, under_way[-1][0])
     joined = []
     for line in under_way:
-        if enc_lines:
-            line[0] = after(line[0], enc_lines[-1][0])
         line = line_joined(line, chunk)
         joined.append(line[0])
         enc_lines.append(line_last(line))
@@ -801,15 +800,12 @@
     enc_own = [line_end(enc_lines[order.index(i)], chunk) for i in range(len(order))]
     enc_got = [lax.ppermute(share, "pipe", [(1, 0)]) for share in enc_own]
     is_first = pipe == 0
-    lower = [jnp.where(is_first, e, d) for e, d in zip(enc_own, dec_got)]
-    upper = [jnp.where(is_first, e, d) for e, d in zip(enc_got, dec_own)]
-    upper[0] = upper[0][:, overlap:]
-    region_grad = jnp.transpose(jnp.concatenate(lower + upper, axis=1))[None]
-
-    sums = after(sums, joined[0])
+    lower = jnp.where(is_first, jnp.concatenate(enc_own, axis=1), jnp.concatenate(dec_got, axis=1))
+    upper = jnp.where(is_first, jnp.concatenate(enc_got, axis=1), jnp.concatenate(dec_own, axis=1))
+    region_grad = jnp.transpose(jnp.concatenate([lower, upper[:, overlap:]], axis=1))[None]
+
+    sums = after(sums, *joined, *dec_got, *[line[0] for line in enc_lines[:-1]])
     for bit in exchange_bits("dp"):
-        if bit > 1:
-            sums = after(sums, joined[-1], *dec_got)
         sums = exchanged(sums, "dp", bit)
     lower, upper = join_cores(sums)
     bias_grad = jnp.concatenate([lower[pack_half:].reshape(-1), upper[pack_half:].reshape(-1)[overlap:]])

time: 320 us -> 304 us (0.950)
  starting transfers between devices: 50.8 us -> 39.8 us
  Pallas kernels: 169 us -> 160 us
  waiting for transfers between devices: 60.1 us -> 67.4 us
    ppermute x6 -> x5, waiting for transfers between devices: 29.5 us -> 11.2 us  [line_last(): lax.ppermute(state[0], 'dp', [(i, i ^ 2) for i in range(4)])]
    ppermute x6 -> x5, waiting for transfers between devices: 5.06 us -> 22.6 us  [line_start(): lax.ppermute(pieces[0], 'dp', [(i, i ^ 1) for i in range(4)])]
    pallas_call x3 -> x2, Pallas kernels: 102 us -> 93.5 us  [regions_pass(): pl.pallas_call(functools.partial(regions_kernel, tile, rows, piece, norm_...]
    ppermute x6 -> x5, starting transfers between devices: 8.75 us -> 3.85 us  [line_start(): lax.ppermute(pieces[0], 'dp', [(i, i ^ 1) for i in range(4)])]
    ppermute x4, starting transfers between devices: 6.03 us -> 2.77 us  [exchanged(): lax.ppermute(values, axis, [(i, i ^ bit) for i in range(count)])]
    ppermute x6 -> x5, starting transfers between devices: 10.9 us -> 7.83 us  [line_last(): lax.ppermute(state[0], 'dp', [(i, i ^ 2) for i in range(4)])]
    unnamed x110 -> x162, local copies, waits for them, and re-layouts: 13.4 us -> 16.1 us
    pallas_call x17 -> x15, Pallas kernels: 14.6 us -> 14.5 us  [one_step(): pl.pallas_call(kernel, grid=(1,), in_specs=[pl.BlockSpec(memory_space=plt...]
  transfers between devices with their start and end apart: 48 -> 45, of which waited for: 21 -> 25; matrix products, arithmetic and copies ran while one was open for 5% -> 2% of each run, Pallas kernels for 31% -> 28%
where the time goes in v4:
time: 304 us
  Pallas kernels  160 us (53%)
  waiting for transfers between devices  67.4 us (22%)
  starting transfers between devices  39.8 us (13%)
  local copies, waits for them, and re-layouts  25.1 us (8%)
  other arithmetic  5.66 us (2%)
  between operations  5.55 us (2%)
    pallas_call x2, Pallas kernels, regions_pass(): pl.pallas_call(functools.partial(regions_kernel, tile, rows, piece, norm_...  93.5 us
    pallas_call x2, Pallas kernels, project(): pl.pallas_call(functools.partial(project_kernel, bool(before)), grid_spec...  26.6 us
    pallas_call x3, Pallas kernels, outer(): pl.pallas_call(functools.partial(outer_kernel, coded), grid_spec=pltpu.Pr...  25.5 us
    ppermute x5, waiting for transfers between devices, line_start(): lax.ppermute(pieces[0], 'dp', [(i, i ^ 1) for i in range(4)])  22.6 us
    unnamed x162, local copies, waits for them, and re-layouts  16.1 us
    pallas_call x15, Pallas kernels, one_step(): pl.pallas_call(kernel, grid=(1,), in_specs=[pl.BlockSpec(memory_space=plt...  14.5 us
    ppermute x5, waiting for transfers between devices, line_last(): lax.ppermute(state[0], 'dp', [(i, i ^ 2) for i in range(4)])  11.2 us
    ppermute x6, waiting for transfers between devices, gather_cells(): pieces.append(lax.ppermute(own, 'tensor', route))  10.5 us
  transfers between devices with their start and end apart: 45, of which 25 were waited for; matrix products, arithmetic and copies ran while one was open for 2% of the time, Pallas kernels for 28%

profile of v4, /device:TPU:0, one launch (start us, length us, event | category | flops | bytes accessed | tf_op | source)
XLA Modules:
  0.0 303.5 jit_solution(17182584934004827556)
XLA Ops:
  0.7 2.8 dynamic-slice_bitcast_fusion
  3.9 1.2 dynamic-slice_bitcast_fusion.1
  6.7 2.7 collective-permute-done.got_ref
  9.3 8.6 %project.2 = (f32[2048,128]{1,0:T(8,128)S(1)}, f32[2048,128]{1,0:T(8,128)S(1)}) custom-call(s32[3]{0:T(128)S(1)} %add_add_fusion.half_ref, bf16[2048,25088]{1,0:T(8,128)(2,1)} %x_ref.13, bf16[25088,128]{1,0:T(8,128)(2,1)} %bitcast.46, bf16[3584,128]{1,0:T(8,128)(2,1)S(1)} %collective-permute-done.got_ref, ...), custom_call_target="tpu_custom_call" | custom-call | flops 1879048192 | bytes 14680064 | tf_op jit(solution)/shard_map/project/pallas_call | solution.py:312
  18.1 17.9 %project.3 = (f32[2048,128]{1,0:T(8,128)S(1)}, f32[2048,128]{1,0:T(8,128)S(1)}) custom-call(s32[3]{0:T(128)S(1)} %add_add_fusion.half_ref, bf16[2048,25088]{1,0:T(8,128)(2,1)} %x_ref.13, bf16[25088,128]{1,0:T(8,128)(2,1)} %bitcast.47, bf16[8960,128]{1,0:T(8,128)(2,1)} %collective-permute-done.1.got_ref.rest_ref, ...), custom_call_target="tpu_custom_call" | custom-call | flops 4697620480 | bytes 36700160 | tf_op jit(solution)/shard_map/project/pallas_call | solution.py:312
  38.2 3.9 %collective-permute-start.5 = (f32[256,128]{1,0:T(8,128)S(1)}, f32[256,128]{1,0:T(8,128)S(1)}, u32[]{:S(2)}, u32[]{:S(2)}) collective-permute-start(f32[256,128]{1,0:T(8,128)S(1)} %get-tuple-element.192), channel_id=1, source_target_pairs={{0,3},{1,2},{2,1},{3,0},{4,7},{5,6},{6,5},{7,4},{8,11},{9,10},{10,... | collective-permute-start | bytes 393224 | tf_op jit(solution)/shard_map/ppermute | solution.py:540
  46.0 2.7 collective-permute-done.4.refs_2_
  49.0 1.3 broadcast_in_dim.49.cf_ref
  50.6 2.8 small_forward.1
  53.3 1.6 collective-permute-start.8
  54.9 1.4 collective-permute-start.7
  56.8 2.2 collective-permute-done.8.refs_3_
  61.8 1.2 hidden.1
  64.7 52.1 %regions.2 = (f32[2048,128]{1,0:T(8,128)}, f32[1,7168]{1,0:T(1,128)}, f32[8,128]{1,0:T(8,128)}, s16[1920,256]{1,0:T(8,128)(2,1)}, f32[32,7168]{1,0:T(8,128)}, /*index=5*/f32[32,7168]{1,0:T(8,128)}) custom-call(s32[3]{0:T(128)} %copy-done.47, bf16[2048,25088]{1,0:T(8,128)(2,1)} %x_ref.13, bf16[25088,128]{1,0:T(8,128)(2,1)} %bitcast.48, ...), custom_call_target="tpu_custom_call" | custom-call | flops 18790481920 | bytes 29360128 | tf_op jit(solution)/shard_map/regions/pallas_call | solution.py:439
  116.9 1.6 collective-permute-start.13
  118.5 41.3 %regions.3 = (f32[2048,128]{1,0:T(8,128)}, f32[1,5376]{1,0:T(1,128)}, f32[8,128]{1,0:T(8,128)}, s16[1440,256]{1,0:T(8,128)(2,1)}, f32[32,5376]{1,0:T(8,128)}, /*index=5*/f32[32,5376]{1,0:T(8,128)}) custom-call(s32[3]{0:T(128)} %copy-done.47, bf16[2048,25088]{1,0:T(8,128)(2,1)} %x_ref.13, bf16[25088,128]{1,0:T(8,128)(2,1)} %bitcast.49, ...), custom_call_target="tpu_custom_call" | custom-call | flops 14092861440 | bytes 22020096 | tf_op jit(solution)/shard_map/regions/pallas_call | solution.py:439
  159.9 1.2 constant_dynamic-slice_fusion.5
  162.4 2.6 collective-permute-start.25
  165.2 1.5 collective-permute-start.17
  167.5 1.3 collective-permute-start.15
  169.4 3.1 %collective-permute-done.17.refs_3_ = f32[256,128]{1,0:T(8,128)S(1)} collective-permute-done((f32[256,128]{1,0:T(8,128)S(1)}, f32[256,128]{1,0:T(8,128)S(1)}, u32[]{:S(2)}, u32[]{:S(2)}) %collective-permute-start.17) | collective-permute-done | bytes 131104 | tf_op jit(solution)/shard_map/ppermute | solution.py:540
  172.6 1.7 collective-permute-done.16.refs_2_
  174.4 4.8 %small_backward.1 = (bf16[256,128]{1,0:T(8,128)(2,1)S(1)}, f32[336,128]{1,0:T(8,128)S(1)}) custom-call(f32[256,128]{1,0:T(8,128)S(1)} %get-tuple-element.133.refs_0_, f32[256,128]{1,0:T(8,128)S(1)} %collective-permute-done.15.refs_1_, f32[256,128]{1,0:T(8,128)S(1)} %collective-permute-done.16.refs_2_, f32[256,128]{1,0:T(8,128)S(1)} %collective-permute-done.17.refs_3_, ...), custom_call_target="tpu_custom_call" | custom-call | tf_op jit(solution)/shard_map/small_backward/pallas_call | solution.py:221
  179.3 1.5 collective-permute-start.20
  180.7 3.8 %collective-permute-done.20.refs_3_ = bf16[256,128]{1,0:T(8,128)(2,1)S(1)} collective-permute-done((bf16[256,128]{1,0:T(8,128)(2,1)S(1)}, bf16[256,128]{1,0:T(8,128)(2,1)S(1)}, u32[]{:S(2)}, u32[]{:S(2)}) %collective-permute-start.20) | collective-permute-done | bytes 65568 | tf_op jit(solution)/shard_map/ppermute | solution.py:549
  184.5 6.3 %collective-permute-done.26.got_ref = s16[1440,256]{1,0:T(8,128)(2,1)S(1)} collective-permute-done((s16[1440,256]{1,0:T(8,128)(2,1)}, s16[1440,256]{1,0:T(8,128)(2,1)S(1)}, u32[]{:S(2)}, u32[]{:S(2)}) %collective-permute-start.26) | collective-permute-done | bytes 737312 | tf_op jit(solution)/shard_map/ppermute | solution.py:236
  193.5 1.2 collective-permute-start.18
  194.7 2.3 collective-permute-done.19.refs_2_
  199.9 7.8 %outer.3 = (s16[960,256]{1,0:T(8,128)(2,1)}, f32[32,3584]{1,0:T(8,128)S(1)}, f32[32,3584]{1,0:T(8,128)S(1)}) custom-call(s32[3]{0:T(128)S(1)} %copy-done.48, bf16[2048,25088]{1,0:T(8,128)(2,1)} %x_ref.13, bf16[128,2048]{1,0:T(8,128)(2,1)S(1)} %left.1.left_ref), custom_call_target="tpu_custom_call" | custom-call | flops 1879048192 | bytes 14680064 | tf_op jit(solution)/shard_map/outer/pallas_call | solution.py:494
  209.2 1.7 collective-permute-done.27.got_ref
  212.4 10.4 %outer.4 = (s16[1440,256]{1,0:T(8,128)(2,1)}, f32[32,5376]{1,0:T(8,128)S(1)}, f32[32,5376]{1,0:T(8,128)S(1)}) custom-call(s32[3]{0:T(128)S(1)} %copy-done.48, bf16[2048,25088]{1,0:T(8,128)(2,1)} %x_ref.13, bf16[128,2048]{1,0:T(8,128)(2,1)S(1)} %left.1.left_ref), custom_call_target="tpu_custom_call" | custom-call | flops 2818572288 | bytes 22020096 | tf_op jit(solution)/shard_map/outer/pallas_call | solution.py:494
  228.6 2.8 collective-permute-start.37
  231.5 1.3 collective-permute-start.33
  232.8 3.2 %collective-permute-done.33 = f32[168,128]{1,0:T(8,128)S(1)} collective-permute-done((f32[168,128]{1,0:T(8,128)S(1)}, f32[168,128]{1,0:T(8,128)S(1)}, u32[]{:S(2)}, u32[]{:S(2)}) %collective-permute-start.33) | collective-permute-done | bytes 86048 | tf_op jit(solution)/shard_map/ppermute | solution.py:603
  236.1 1.4 collective-permute-start.34
  240.6 1.3 collective-permute-start.38
  242.0 7.3 %outer.5 = (s16[960,256]{1,0:T(8,128)(2,1)S(1)}, f32[32,3584]{1,0:T(8,128)S(1)}, f32[32,3584]{1,0:T(8,128)S(1)}) custom-call(s32[3]{0:T(128)S(1)} %copy-done.48, bf16[2048,25088]{1,0:T(8,128)(2,1)} %x_ref.13, bf16[128,2048]{1,0:T(8,128)(2,1)S(1)} %left.1.left_ref), custom_call_target="tpu_custom_call" | custom-call | flops 1879048192 | bytes 14680064 | tf_op jit(solution)/shard_map/outer/pallas_call | solution.py:494
  249.3 3.0 collective-permute-done.29.got_ref
  252.8 2.0 collective-permute-start.31
  254.9 15.7 %collective-permute-done.35.got_ref = s16[960,256]{1,0:T(8,128)(2,1)S(1)} collective-permute-done((s16[960,256]{1,0:T(8,128)(2,1)S(1)}, s16[960,256]{1,0:T(8,128)(2,1)S(1)}, u32[]{:S(2)}, u32[]{:S(2)}) %collective-permute-start.35) | collective-permute-done | bytes 491552 | tf_op jit(solution)/shard_map/ppermute | solution.py:236
  274.0 1.9 collective-permute-start.36
  276.0 4.2 %collective-permute-done.42 = f32[266,128]{1,0:T(8,128)S(1)} collective-permute-done((f32[266,128]{1,0:T(8,128)S(1)}, f32[266,128]{1,0:T(8,128)S(1)}, u32[]{:S(2)}, u32[]{:S(2)}) %collective-permute-start.42) | collective-permute-done | bytes 136224 | tf_op jit(solution)/shard_map/ppermute | solution.py:603
  281.3 1.3 collective-permute-start.39
  283.7 1.4 collective-permute-start.40
  285.2 6.5 %collective-permute-done.36.got_ref = s16[480,256]{1,0:T(8,128)(2,1)} collective-permute-done((s16[480,256]{1,0:T(8,128)(2,1)}, s16[480,256]{1,0:T(8,128)(2,1)}, u32[]{:S(2)}, u32[]{:S(2)}) %collective-permute-start.36) | collective-permute-done | bytes 245792 | tf_op jit(solution)/shard_map/ppermute | solution.py:251
  293.7 1.3 collective-permute-start.41
  295.1 1.2 collective-permute-start.44
  300.5 1.9 maximum_bitcast_fusion
  (268 shorter events, 43.8 us)
Async XLA Ops:
  3.4 14.6 %collective-permute-start.1 = (bf16[8960,128]{1,0:T(8,128)(2,1)}, bf16[8960,128]{1,0:T(8,128)(2,1)}, u32[]{:S(2)}, u32[]{:S(2)}) collective-permute-start(bf16[8960,128]{1,0:T(8,128)(2,1)} %dynamic-slice_bitcast_fusion), channel_id=1, source_target_pairs={{0,16},{16,0},{1,17},{17,1},{2,18},{18,2},{3,19},{19,3},{4,20},{20... | collective-permute-start | bytes 6881288 | tf_op jit(solution)/shard_map/ppermute | solution.py:520
  5.2 4.1 %collective-permute-start = (bf16[3584,128]{1,0:T(8,128)(2,1)S(1)}, bf16[3584,128]{1,0:T(8,128)(2,1)S(1)}, u32[]{:S(2)}, u32[]{:S(2)}) collective-permute-start(bf16[3584,128]{1,0:T(8,128)(2,1)S(1)} %dynamic-slice_bitcast_fusion.1), channel_id=1, source_target_pairs={{0,16},{16,0},{1,17},{17,1},{2,18},{18,2},{3,19},{19,3},{4,20},{20... | collective-permute-start | bytes 2752520 | tf_op jit(solution)/shard_map/ppermute | solution.py:520
  36.1 2.0 collective-permute-start.2
  38.2 7.8 %collective-permute-start.5 = (f32[256,128]{1,0:T(8,128)S(1)}, f32[256,128]{1,0:T(8,128)S(1)}, u32[]{:S(2)}, u32[]{:S(2)}) collective-permute-start(f32[256,128]{1,0:T(8,128)S(1)} %get-tuple-element.192), channel_id=1, source_target_pairs={{0,3},{1,2},{2,1},{3,0},{4,7},{5,6},{6,5},{7,4},{8,11},{9,10},{10,... | collective-permute-start | bytes 393224 | tf_op jit(solution)/shard_map/ppermute | solution.py:540
  42.1 6.6 %collective-permute-start.4 = (f32[256,128]{1,0:T(8,128)S(1)}, f32[256,128]{1,0:T(8,128)S(1)}, u32[]{:S(2)}, u32[]{:S(2)}) collective-permute-start(f32[256,128]{1,0:T(8,128)S(1)} %get-tuple-element.193), channel_id=1, source_target_pairs={{0,2},{1,3},{2,0},{3,1},{4,6},{5,7},{6,4},{7,5},{8,10},{9,11},{10,... | collective-permute-start | bytes 393224 | tf_op jit(solution)/shard_map/ppermute | solution.py:540
  42.6 6.4 %collective-permute-start.3 = (f32[256,128]{1,0:T(8,128)S(1)}, f32[256,128]{1,0:T(8,128)S(1)}, u32[]{:S(2)}, u32[]{:S(2)}) collective-permute-start(f32[256,128]{1,0:T(8,128)S(1)} %get-tuple-element.194), channel_id=1, source_target_pairs={{0,1},{1,0},{2,3},{3,2},{4,5},{5,4},{6,7},{7,6},{8,9},{9,8},{10,11... | collective-permute-start | bytes 393224 | tf_op jit(solution)/shard_map/ppermute | solution.py:540
  53.3 5.7 %collective-permute-start.8 = (bf16[256,128]{1,0:T(8,128)(2,1)S(1)}, bf16[256,128]{1,0:T(8,128)(2,1)S(1)}, u32[]{:S(2)}, u32[]{:S(2)}) collective-permute-start(bf16[256,128]{1,0:T(8,128)(2,1)S(1)} %get-tuple-element.122.refs_0_), channel_id=1, source_target_pairs={{0,3},{1,2},{2,1},{3,0},{4,7},{5,6},{6,5},{7,4},{8,11},{9,10},{10,... | collective-permute-start | bytes 196616 | tf_op jit(solution)/shard_map/ppermute | solution.py:549
  54.9 4.5 %collective-permute-start.7 = (bf16[256,128]{1,0:T(8,128)(2,1)S(1)}, bf16[256,128]{1,0:T(8,128)(2,1)S(1)}, u32[]{:S(2)}, u32[]{:S(2)}) collective-permute-start(bf16[256,128]{1,0:T(8,128)(2,1)S(1)} %get-tuple-element.122.refs_0_), channel_id=1, source_target_pairs={{0,2},{1,3},{2,0},{3,1},{4,6},{5,7},{6,4},{7,5},{8,10},{9,11},{10,... | collective-permute-start | bytes 196616 | tf_op jit(solution)/shard_map/ppermute | solution.py:549
  56.3 4.3 %collective-permute-start.6 = (bf16[256,128]{1,0:T(8,128)(2,1)S(1)}, bf16[256,128]{1,0:T(8,128)(2,1)S(1)}, u32[]{:S(2)}, u32[]{:S(2)}) collective-permute-start(bf16[256,128]{1,0:T(8,128)(2,1)S(1)} %get-tuple-element.122.refs_0_), channel_id=1, source_target_pairs={{0,1},{1,0},{2,3},{3,2},{4,5},{5,4},{6,7},{7,6},{8,9},{9,8},{10,11... | collective-permute-start | bytes 196616 | tf_op jit(solution)/shard_map/ppermute | solution.py:549
  56.8 3.8 %collective-permute-start.9 = (bf16[256,128]{1,0:T(8,128)(2,1)S(1)}, bf16[256,128]{1,0:T(8,128)(2,1)S(1)}, u32[]{:S(2)}, u32[]{:S(2)}) collective-permute-start(bf16[256,128]{1,0:T(8,128)(2,1)S(1)} %get-tuple-element.122.refs_0_), channel_id=1, source_target_pairs={{0,16},{16,0},{1,17},{17,1},{2,18},{18,2},{3,19},{19,3},{4,20},{20... | collective-permute-start | bytes 196616 | tf_op jit(solution)/shard_map/ppermute | solution.py:520
  59.0 1.7 collective-permute-start.12
  59.4 1.3 collective-permute-start.11
  60.6 1.3 collective-permute-start.10
  116.9 43.0 %collective-permute-start.13 = (s16[1920,256]{1,0:T(8,128)(2,1)}, s16[1920,256]{1,0:T(8,128)(2,1)S(1)}, u32[]{:S(2)}, u32[]{:S(2)}) collective-permute-start(s16[1920,256]{1,0:T(8,128)(2,1)} %get-tuple-element.128), channel_id=1, source_target_pairs={{0,4},{4,0},{8,12},{12,8},{1,5},{5,1},{9,13},{13,9},{2,6},{6,2},{1... | collective-permute-start | bytes 2949128 | tf_op jit(solution)/shard_map/ppermute | solution.py:236
  118.5 43.1 %copy-start.3 = (f32[32,7168]{1,0:T(8,128)S(1)}, f32[32,7168]{1,0:T(8,128)}, u32[]{:S(2)}) copy-start(f32[32,7168]{1,0:T(8,128)} %get-tuple-element.131.other_ref) | copy-start | bytes 2752516
  161.1 4.0 %collective-permute-start.14 = (f32[1024,128]{1,0:T(8,128)S(1)}, f32[1024,128]{1,0:T(8,128)S(1)}, u32[]{:S(2)}, u32[]{:S(2)}) collective-permute-start(f32[1024,128]{1,0:T(8,128)S(1)} %constant_dynamic-slice_fusion.5), channel_id=1, source_target_pairs={{0,16},{16,0},{1,17},{17,1},{2,18},{18,2},{3,19},{19,3},{4,20},{20... | collective-permute-start | bytes 1572872 | tf_op jit(solution)/shard_map/ppermute | solution.py:520
  161.1 29.6 %collective-permute-start.26 = (s16[1440,256]{1,0:T(8,128)(2,1)}, s16[1440,256]{1,0:T(8,128)(2,1)S(1)}, u32[]{:S(2)}, u32[]{:S(2)}) collective-permute-start(s16[1440,256]{1,0:T(8,128)(2,1)} %get-tuple-element.141), channel_id=1, source_target_pairs={{0,4},{4,0},{8,12},{12,8},{1,5},{5,1},{9,13},{13,9},{2,6},{6,2},{1... | collective-permute-start | bytes 2211848 | tf_op jit(solution)/shard_map/ppermute | solution.py:236
  162.4 28.4 %copy-start.9 = (f32[32,5376]{1,0:T(8,128)S(1)}, f32[32,5376]{1,0:T(8,128)}, u32[]{:S(2)}) copy-start(f32[32,5376]{1,0:T(8,128)} %get-tuple-element.143.own_ref) | copy-start | bytes 2064388
  162.4 28.4 %copy-start.10 = (f32[32,5376]{1,0:T(8,128)S(1)}, f32[32,5376]{1,0:T(8,128)}, u32[]{:S(2)}) copy-start(f32[32,5376]{1,0:T(8,128)} %get-tuple-element.144.other_ref) | copy-start | bytes 2064388
  162.4 37.4 %collective-permute-start.25 = (s16[960,256]{1,0:T(8,128)(2,1)S(1)}, s16[960,256]{1,0:T(8,128)(2,1)S(1)}, u32[]{:S(2)}, u32[]{:S(2)}) collective-permute-start(s16[960,256]{1,0:T(8,128)(2,1)S(1)} %get-tuple-element.132), channel_id=1, source_target_pairs={{0,8},{4,12},{8,0},{12,4},{1,9},{5,13},{9,1},{13,5},{2,10},{6,14},... | collective-permute-start | bytes 1474568 | tf_op jit(solution)/shard_map/ppermute | solution.py:251
  165.2 7.3 %collective-permute-start.17 = (f32[256,128]{1,0:T(8,128)S(1)}, f32[256,128]{1,0:T(8,128)S(1)}, u32[]{:S(2)}, u32[]{:S(2)}) collective-permute-start(f32[256,128]{1,0:T(8,128)S(1)} %get-tuple-element.188), channel_id=1, source_target_pairs={{0,3},{1,2},{2,1},{3,0},{4,7},{5,6},{6,5},{7,4},{8,11},{9,10},{10,... | collective-permute-start | bytes 393224 | tf_op jit(solution)/shard_map/ppermute | solution.py:540
  166.7 7.6 %collective-permute-start.16 = (f32[256,128]{1,0:T(8,128)S(1)}, f32[256,128]{1,0:T(8,128)S(1)}, u32[]{:S(2)}, u32[]{:S(2)}) collective-permute-start(f32[256,128]{1,0:T(8,128)S(1)} %get-tuple-element.189), channel_id=1, source_target_pairs={{0,2},{1,3},{2,0},{3,1},{4,6},{5,7},{6,4},{7,5},{8,10},{9,11},{10,... | collective-permute-start | bytes 393224 | tf_op jit(solution)/shard_map/ppermute | solution.py:540
  167.5 6.8 %collective-permute-start.15 = (f32[256,128]{1,0:T(8,128)S(1)}, f32[256,128]{1,0:T(8,128)S(1)}, u32[]{:S(2)}, u32[]{:S(2)}) collective-permute-start(f32[256,128]{1,0:T(8,128)S(1)} %get-tuple-element.190), channel_id=1, source_target_pairs={{0,1},{1,0},{2,3},{3,2},{4,5},{5,4},{6,7},{7,6},{8,9},{9,8},{10,11... | collective-permute-start | bytes 393224 | tf_op jit(solution)/shard_map/ppermute | solution.py:540
  179.3 5.2 %collective-permute-start.20 = (bf16[256,128]{1,0:T(8,128)(2,1)S(1)}, bf16[256,128]{1,0:T(8,128)(2,1)S(1)}, u32[]{:S(2)}, u32[]{:S(2)}) collective-permute-start(bf16[256,128]{1,0:T(8,128)(2,1)S(1)} %get-tuple-element.140.refs_0_), channel_id=1, source_target_pairs={{0,3},{1,2},{2,1},{3,0},{4,7},{5,6},{6,5},{7,4},{8,11},{9,10},{10,... | collective-permute-start | bytes 196616 | tf_op jit(solution)/shard_map/ppermute | solution.py:549
  184.5 6.3 %collective-permute-start.24 = (bf16[256,128]{1,0:T(8,128)(2,1)S(1)}, bf16[256,128]{1,0:T(8,128)(2,1)S(1)}, u32[]{:S(2)}, u32[]{:S(2)}) collective-permute-start(bf16[256,128]{1,0:T(8,128)(2,1)S(1)} %collective-permute-done.20.refs_3_), channel_id=1, source_target_pairs={{0,16},{16,0},{1,17},{17,1},{2,18},{18,2},{3,19},{19,3},{4,20},{20... | collective-permute-start | bytes 196616 | tf_op jit(solution)/shard_map/ppermute | solution.py:520
  192.1 18.8 %collective-permute-start.27 = (s16[720,256]{1,0:T(8,128)(2,1)S(1)}, s16[720,256]{1,0:T(8,128)(2,1)S(1)}, u32[]{:S(2)}, u32[]{:S(2)}) collective-permute-start(s16[720,256]{1,0:T(8,128)(2,1)S(1)} %get-tuple-element.145), channel_id=1, source_target_pairs={{0,8},{4,12},{8,0},{12,4},{1,9},{5,13},{9,1},{13,5},{2,10},{6,14},... | collective-permute-start | bytes 1105928 | tf_op jit(solution)/shard_map/ppermute | solution.py:251
  192.8 4.3 %collective-permute-start.19 = (bf16[256,128]{1,0:T(8,128)(2,1)S(1)}, bf16[256,128]{1,0:T(8,128)(2,1)S(1)}, u32[]{:S(2)}, u32[]{:S(2)}) collective-permute-start(bf16[256,128]{1,0:T(8,128)(2,1)S(1)} %get-tuple-element.140.refs_0_), channel_id=1, source_target_pairs={{0,2},{1,3},{2,0},{3,1},{4,6},{5,7},{6,4},{7,5},{8,10},{9,11},{10,... | collective-permute-start | bytes 196616 | tf_op jit(solution)/shard_map/ppermute | solution.py:549
  193.5 4.3 %collective-permute-start.18 = (bf16[256,128]{1,0:T(8,128)(2,1)S(1)}, bf16[256,128]{1,0:T(8,128)(2,1)S(1)}, u32[]{:S(2)}, u32[]{:S(2)}) collective-permute-start(bf16[256,128]{1,0:T(8,128)(2,1)S(1)} %get-tuple-element.140.refs_0_), channel_id=1, source_target_pairs={{0,1},{1,0},{2,3},{3,2},{4,5},{5,4},{6,7},{7,6},{8,9},{9,8},{10,11... | collective-permute-start | bytes 196616 | tf_op jit(solution)/shard_map/ppermute | solution.py:549
  194.7 3.0 collective-permute-start.21
  197.1 1.3 collective-permute-start.23
  197.8 1.3 collective-permute-start.22
  211.7 13.4 %collective-permute-start.28 = (s16[960,256]{1,0:T(8,128)(2,1)}, s16[960,256]{1,0:T(8,128)(2,1)S(1)}, u32[]{:S(2)}, u32[]{:S(2)}) collective-permute-start(s16[960,256]{1,0:T(8,128)(2,1)} %get-tuple-element.148), channel_id=1, source_target_pairs={{0,4},{4,0},{8,12},{12,8},{1,5},{5,1},{9,13},{13,9},{2,6},{6,2},{1... | collective-permute-start | bytes 1474568 | tf_op jit(solution)/shard_map/ppermute | solution.py:236
  225.8 26.4 %collective-permute-start.30 = (s16[1440,256]{1,0:T(8,128)(2,1)}, s16[1440,256]{1,0:T(8,128)(2,1)S(1)}, u32[]{:S(2)}, u32[]{:S(2)}) collective-permute-start(s16[1440,256]{1,0:T(8,128)(2,1)} %get-tuple-element.155), channel_id=1, source_target_pairs={{0,4},{4,0},{8,12},{12,8},{1,5},{5,1},{9,13},{13,9},{2,6},{6,2},{1... | collective-permute-start | bytes 2211848 | tf_op jit(solution)/shard_map/ppermute | solution.py:236
  227.5 4.0 %collective-permute-start.32 = (f32[168,128]{1,0:T(8,128)}, f32[168,128]{1,0:T(8,128)S(1)}, u32[]{:S(2)}, u32[]{:S(2)}) collective-permute-start(f32[168,128]{1,0:T(8,128)} %constant_dynamic-slice_fusion), channel_id=1, source_target_pairs={{0,16},{16,0},{1,17},{17,1},{2,18},{18,2},{3,19},{19,3},{4,20},{20... | collective-permute-start | bytes 258056 | tf_op jit(solution)/shard_map/ppermute | solution.py:520
  228.6 43.7 %collective-permute-start.37 = (f32[32,7168]{1,0:T(8,128)S(1)}, f32[32,7168]{1,0:T(8,128)S(1)}, u32[]{:S(2)}, u32[]{:S(2)}) collective-permute-start(f32[32,7168]{1,0:T(8,128)S(1)} %total.8), channel_id=1, source_target_pairs={{0,16},{1,17},{2,18},{3,19},{4,20},{5,21},{6,22},{7,23},{8,24},{9,... | collective-permute-start | bytes 2752520 | tf_op jit(solution)/shard_map/ppermute | solution.py:799
  231.5 4.6 %collective-permute-start.33 = (f32[168,128]{1,0:T(8,128)S(1)}, f32[168,128]{1,0:T(8,128)S(1)}, u32[]{:S(2)}, u32[]{:S(2)}) collective-permute-start(f32[168,128]{1,0:T(8,128)S(1)} %dynamic-slice_add_fusion.2), channel_id=1, source_target_pairs={{0,1},{1,0},{2,3},{3,2},{4,5},{5,4},{6,7},{7,6},{8,9},{9,8},{10,11... | collective-permute-start | bytes 258056 | tf_op jit(solution)/shard_map/ppermute | solution.py:603
  236.1 5.8 %collective-permute-start.34 = (f32[168,128]{1,0:T(8,128)S(1)}, f32[168,128]{1,0:T(8,128)S(1)}, u32[]{:S(2)}, u32[]{:S(2)}) collective-permute-start(f32[168,128]{1,0:T(8,128)S(1)} %add.89), channel_id=1, source_target_pairs={{0,2},{1,3},{2,0},{3,1},{4,6},{5,7},{6,4},{7,5},{8,10},{9,11},{10,... | collective-permute-start | bytes 258056 | tf_op jit(solution)/shard_map/ppermute | solution.py:603
  239.8 12.4 %collective-permute-start.29 = (s16[480,256]{1,0:T(8,128)(2,1)S(1)}, s16[480,256]{1,0:T(8,128)(2,1)S(1)}, u32[]{:S(2)}, u32[]{:S(2)}) collective-permute-start(s16[480,256]{1,0:T(8,128)(2,1)S(1)} %get-tuple-element.152), channel_id=1, source_target_pairs={{0,8},{4,12},{8,0},{12,4},{1,9},{5,13},{9,1},{13,5},{2,10},{6,14},... | collective-permute-start | bytes 737288 | tf_op jit(solution)/shard_map/ppermute | solution.py:251
  240.6 31.8 %collective-permute-start.38 = (f32[32,5376]{1,0:T(8,128)S(1)}, f32[32,5376]{1,0:T(8,128)S(1)}, u32[]{:S(2)}, u32[]{:S(2)}) collective-permute-start(f32[32,5376]{1,0:T(8,128)S(1)} %total.9), channel_id=1, source_target_pairs={{0,16},{1,17},{2,18},{3,19},{4,20},{5,21},{6,22},{7,23},{8,24},{9,... | collective-permute-start | bytes 2064392 | tf_op jit(solution)/shard_map/ppermute | solution.py:799
  252.3 18.3 %collective-permute-start.35 = (s16[960,256]{1,0:T(8,128)(2,1)S(1)}, s16[960,256]{1,0:T(8,128)(2,1)S(1)}, u32[]{:S(2)}, u32[]{:S(2)}) collective-permute-start(s16[960,256]{1,0:T(8,128)(2,1)S(1)} %get-tuple-element.166), channel_id=1, source_target_pairs={{0,4},{4,0},{8,12},{12,8},{1,5},{5,1},{9,13},{13,9},{2,6},{6,2},{1... | collective-permute-start | bytes 1474568 | tf_op jit(solution)/shard_map/ppermute | solution.py:236
  252.8 19.6 %collective-permute-start.31 = (s16[720,256]{1,0:T(8,128)(2,1)S(1)}, s16[720,256]{1,0:T(8,128)(2,1)S(1)}, u32[]{:S(2)}, u32[]{:S(2)}) collective-permute-start(s16[720,256]{1,0:T(8,128)(2,1)S(1)} %get-tuple-element.159), channel_id=1, source_target_pairs={{0,8},{4,12},{8,0},{12,4},{1,9},{5,13},{9,1},{13,5},{2,10},{6,14},... | collective-permute-start | bytes 1105928 | tf_op jit(solution)/shard_map/ppermute | solution.py:251
  274.0 6.2 %collective-permute-start.42 = (f32[266,128]{1,0:T(8,128)S(1)}, f32[266,128]{1,0:T(8,128)S(1)}, u32[]{:S(2)}, u32[]{:S(2)}) collective-permute-start(f32[266,128]{1,0:T(8,128)S(1)} %pad_maximum_fusion), channel_id=1, source_target_pairs={{0,4},{4,0},{8,12},{12,8},{1,5},{5,1},{9,13},{13,9},{2,6},{6,2},{1... | collective-permute-start | bytes 408584 | tf_op jit(solution)/shard_map/ppermute | solution.py:603
  274.0 17.6 %collective-permute-start.36 = (s16[480,256]{1,0:T(8,128)(2,1)}, s16[480,256]{1,0:T(8,128)(2,1)}, u32[]{:S(2)}, u32[]{:S(2)}) collective-permute-start(s16[480,256]{1,0:T(8,128)(2,1)} %get-tuple-element.170), channel_id=1, source_target_pairs={{0,8},{4,12},{8,0},{12,4},{1,9},{5,13},{9,1},{13,5},{2,10},{6,14},... | collective-permute-start | bytes 737288 | tf_op jit(solution)/shard_map/ppermute | solution.py:251
  280.2 14.8 %collective-permute-start.43 = (f32[266,128]{1,0:T(8,128)S(1)}, f32[266,128]{1,0:T(8,128)S(1)}, u32[]{:S(2)}, u32[]{:S(2)}) collective-permute-start(f32[266,128]{1,0:T(8,128)S(1)} %add.91), channel_id=1, source_target_pairs={{0,8},{4,12},{8,0},{12,4},{1,9},{5,13},{9,1},{13,5},{2,10},{6,14},... | collective-permute-start | bytes 408584 | tf_op jit(solution)/shard_map/ppermute | solution.py:603
  281.3 19.0 %collective-permute-start.39 = (f32[32,3584]{1,0:T(8,128)S(1)}, f32[32,3584]{1,0:T(8,128)S(1)}, u32[]{:S(2)}, u32[]{:S(2)}) collective-permute-start(f32[32,3584]{1,0:T(8,128)S(1)} %total.5), channel_id=1, source_target_pairs={{16,0},{17,1},{18,2},{19,3},{20,4},{21,5},{22,6},{23,7},{24,8},{25... | collective-permute-start | bytes 1376264 | tf_op jit(solution)/shard_map/ppermute | solution.py:801
  283.7 16.6 %collective-permute-start.40 = (f32[32,5376]{1,0:T(8,128)S(1)}, f32[32,5376]{1,0:T(8,128)S(1)}, u32[]{:S(2)}, u32[]{:S(2)}) collective-permute-start(f32[32,5376]{1,0:T(8,128)S(1)} %total.6), channel_id=1, source_target_pairs={{16,0},{17,1},{18,2},{19,3},{20,4},{21,5},{22,6},{23,7},{24,8},{25... | collective-permute-start | bytes 2064392 | tf_op jit(solution)/shard_map/ppermute | solution.py:801
  293.7 6.6 %collective-permute-start.41 = (f32[32,3584]{1,0:T(8,128)S(1)}, f32[32,3584]{1,0:T(8,128)S(1)}, u32[]{:S(2)}, u32[]{:S(2)}) collective-permute-start(f32[32,3584]{1,0:T(8,128)S(1)} %total.7), channel_id=1, source_target_pairs={{16,0},{17,1},{18,2},{19,3},{20,4},{21,5},{22,6},{23,7},{24,8},{25... | collective-permute-start | bytes 1376264 | tf_op jit(solution)/shard_map/ppermute | solution.py:801
  295.1 2.6 collective-permute-start.44
  (78 other events, 702.5 us)

commit v5 on v4

--- a/solution.py
+++ b/solution.py
@@ -754,7 +754,7 @@
         "small_backward",
     )
     gathered = gather_cells(dp_own)
-    lines[-1][0] = after(lines[-1][0], gathered[-1])
+    lines[-1][0] = after(lines[-1][0], *gathered)
     lines[-1] = line_joined(lines[-1], chunk)
     (left,) = assemble(left_kernel, place, gathered, [jax.ShapeDtypeStruct((width, cells), jnp.bfloat16)], "left")
     left = after(left, *[line[0] for line in lines])
@@ -766,34 +766,28 @@
     enc_lines, under_way = [], []
     for index, (first, end) in enumerate([spans[i] for i in order]):
         if index:
-            left = after(left, shares[0])
+            left = after(left, shares[0], *([lines[-1][0]] if index == 1 else []))
         if index > 1:
             line = line_joined(under_way.pop(0), chunk)
-            left = after(left, line[0], pack)
+            left = after(left, line[0])
             enc_lines.append(line_last(line))
         shares = list(outer(half, peak_data, left, first, end - first, chunk, chunks, coded))
-        if index == min(1, len(spans) - 1):
-            pack = after(pack, *([waiting] if index else []))
-            pack = part_of(pack, pipe, pack_half) + across_cores(part_of(pack, 1 - pipe, pack_half))
-            steps = [("tensor", bit) for bit in exchange_bits("tensor")]
-            while len(steps) > 1:
-                pack = exchanged(pack, *steps.pop(0))
-        elif index:
-            pack = exchanged(pack, *steps.pop(0))
-            shares[0] = after(shares[0], pack)
-        waiting = shares[0]
-        beside = [line[0] for line in under_way + enc_lines] + ([] if index else [lines[-1][0]])
+        newest = shares[0]
+        beside = [line[0] for line in under_way + enc_lines]
         shares[0] = after(shares[0], *beside)
         under_way.append(line_start(shares))
-    for step in steps:
-        pack = exchanged(pack, *step)
-    sums = jnp.concatenate([pack, jnp.concatenate(biases, axis=1).reshape(-1, 128)], axis=0)
-    sums = after(sums, under_way[-1][0])
-    joined = []
+    joined, newest_got = [], under_way[-1][0]
     for line in under_way:
+        line[0] = after(line[0], newest)
         line = line_joined(line, chunk)
         joined.append(line[0])
         enc_lines.append(line_last(line))
+
+    pack, *ends = lax.optimization_barrier((after(pack, joined[0]), *[line[0] for line in lines]))
+    lines = [[end, *line[1:]] for end, line in zip(ends, lines)]
+    pack = part_of(pack, pipe, pack_half) + across_cores(part_of(pack, 1 - pipe, pack_half))
+    pack = all_sum(after(pack, newest_got), ["tensor"])
+    sums = jnp.concatenate([pack, jnp.concatenate(biases, axis=1).reshape(-1, 128)], axis=0)
 
     dec_own = [line_end(line, chunk) for line in lines]
     dec_got = [lax.ppermute(share, "pipe", [(0, 1)]) for share in dec_own]
@@ -804,8 +798,9 @@
     upper = jnp.where(is_first, jnp.concatenate(enc_got, axis=1), jnp.concatenate(dec_own, axis=1))
     region_grad = jnp.transpose(jnp.concatenate([lower, upper[:, overlap:]], axis=1))[None]
 
-    sums = after(sums, *joined, *dec_got, *[line[0] for line in enc_lines[:-1]])
     for bit in exchange_bits("dp"):
+        if bit == 1:
+            sums = after(sums, *joined, *dec_got, *[line[0] for line in enc_lines[:-1]])
         sums = exchanged(sums, "dp", bit)
     lower, upper = join_cores(sums)
     bias_grad = jnp.concatenate([lower[pack_half:].reshape(-1), upper[pack_half:].reshape(-1)[overlap:]])

time: 304 us -> 306 us (level)
  local copies, waits for them, and re-layouts: 25.1 us -> 18 us
  starting transfers between devices: 39.8 us -> 43.8 us
  other arithmetic: 5.66 us -> 8.74 us
    unnamed x162 -> x86, local copies, waits for them, and re-layouts: 16.1 us -> 8.79 us
    ppermute x5, waiting for transfers between devices: 22.6 us -> 29.5 us  [line_start(): lax.ppermute(pieces[0], 'dp', [(i, i ^ 1) for i in range(4)])]
    ppermute x6, waiting for transfers between devices: 10.5 us -> 3.73 us  [gather_cells(): pieces.append(lax.ppermute(own, 'tensor', route))]
    ppermute x4, waiting for transfers between devices: 7.48 us -> 10.8 us  [exchanged(): lax.ppermute(values, axis, [(i, i ^ bit) for i in range(count)])]
  transfers between devices with their start and end apart: 45 -> 45, of which waited for: 25 -> 21; matrix products, arithmetic and copies ran while one was open for 2% -> 4% of each run, Pallas kernels for 28% -> 28%
where the time goes in v5:
time: 306 us; the launch traced here: 305 us
  Pallas kernels  161 us (53%)
  waiting for transfers between devices  68.3 us (22%)
  starting transfers between devices  43.8 us (14%)
  local copies, waits for them, and re-layouts  18 us (6%)
  other arithmetic  8.74 us (3%)
  between operations  5.16 us (2%)
    pallas_call x2, Pallas kernels, regions_pass(): pl.pallas_call(functools.partial(regions_kernel, tile, rows, piece, norm_...  93.5 us
    ppermute x5, waiting for transfers between devices, line_start(): lax.ppermute(pieces[0], 'dp', [(i, i ^ 1) for i in range(4)])  29.5 us
    pallas_call x2, Pallas kernels, project(): pl.pallas_call(functools.partial(project_kernel, bool(before)), grid_spec...  26.5 us
    pallas_call x3, Pallas kernels, outer(): pl.pallas_call(functools.partial(outer_kernel, coded), grid_spec=pltpu.Pr...  25.2 us
    pallas_call x15, Pallas kernels, one_step(): pl.pallas_call(kernel, grid=(1,), in_specs=[pl.BlockSpec(memory_space=plt...  15.5 us
    ppermute x4, waiting for transfers between devices, exchanged(): lax.ppermute(values, axis, [(i, i ^ bit) for i in range(count)])  10.8 us
    ppermute x5, waiting for transfers between devices, line_last(): lax.ppermute(state[0], 'dp', [(i, i ^ 2) for i in range(4)])  9.47 us
    ppermute x6, waiting for transfers between devices, scatter_cells(): pieces.append(lax.ppermute(part_of(chip_sum, there, rows), 'tensor', route))  8.83 us
  transfers between devices with their start and end apart: 45, of which 21 were waited for; matrix products, arithmetic and copies ran while one was open for 4% of the time, Pallas kernels for 28%

profile of v5, /device:TPU:0, one launch (start us, length us, event | category | flops | bytes accessed | tf_op | source)
XLA Modules:
  0.0 304.6 jit_solution(10824506037870119794)
XLA Ops:
  0.7 2.8 dynamic-slice_bitcast_fusion
  3.9 1.2 dynamic-slice_bitcast_fusion.1
  6.6 2.7 collective-permute-done.got_ref
  9.3 8.6 %project.2 = (f32[2048,128]{1,0:T(8,128)S(1)}, f32[2048,128]{1,0:T(8,128)S(1)}) custom-call(s32[3]{0:T(128)S(1)} %add_add_fusion.half_ref, bf16[2048,25088]{1,0:T(8,128)(2,1)} %x_ref.13, bf16[25088,128]{1,0:T(8,128)(2,1)} %bitcast.46, bf16[3584,128]{1,0:T(8,128)(2,1)S(1)} %collective-permute-done.got_ref, ...), custom_call_target="tpu_custom_call" | custom-call | flops 1879048192 | bytes 14680064 | tf_op jit(solution)/shard_map/project/pallas_call | solution.py:312
  18.1 17.8 %project.3 = (f32[2048,128]{1,0:T(8,128)S(1)}, f32[2048,128]{1,0:T(8,128)S(1)}) custom-call(s32[3]{0:T(128)S(1)} %add_add_fusion.half_ref, bf16[2048,25088]{1,0:T(8,128)(2,1)} %x_ref.13, bf16[25088,128]{1,0:T(8,128)(2,1)} %bitcast.47, bf16[8960,128]{1,0:T(8,128)(2,1)} %collective-permute-done.1.got_ref.rest_ref, ...), custom_call_target="tpu_custom_call" | custom-call | flops 4697620480 | bytes 36700160 | tf_op jit(solution)/shard_map/project/pallas_call | solution.py:312
  36.8 1.2 collective-permute-done.2
  38.1 2.9 collective-permute-start.3
  41.1 1.5 collective-permute-start.4
  45.5 3.7 %collective-permute-done.4.refs_2_ = f32[256,128]{1,0:T(8,128)S(1)} collective-permute-done((f32[256,128]{1,0:T(8,128)S(1)}, f32[256,128]{1,0:T(8,128)S(1)}, u32[]{:S(2)}, u32[]{:S(2)}) %collective-permute-start.4) | collective-permute-done | bytes 131104 | tf_op jit(solution)/shard_map/ppermute | solution.py:540
  49.1 1.3 broadcast_in_dim.49.cf_ref
  50.6 2.8 small_forward.1
  53.4 1.2 collective-permute-start.6
  55.5 1.4 collective-permute-start.8
  59.0 1.6 collective-permute-done.8.refs_3_
  64.9 52.1 %regions.2 = (f32[2048,128]{1,0:T(8,128)}, f32[1,7168]{1,0:T(1,128)}, f32[8,128]{1,0:T(8,128)}, s16[1920,256]{1,0:T(8,128)(2,1)}, f32[32,7168]{1,0:T(8,128)}, /*index=5*/f32[32,7168]{1,0:T(8,128)}) custom-call(s32[3]{0:T(128)} %copy-done.22, bf16[2048,25088]{1,0:T(8,128)(2,1)} %x_ref.13, bf16[25088,128]{1,0:T(8,128)(2,1)} %bitcast.48, ...), custom_call_target="tpu_custom_call" | custom-call | flops 18790481920 | bytes 29360128 | tf_op jit(solution)/shard_map/regions/pallas_call | solution.py:439
  117.0 1.6 collective-permute-start.13
  118.6 41.3 %regions.3 = (f32[2048,128]{1,0:T(8,128)}, f32[1,5376]{1,0:T(1,128)}, f32[8,128]{1,0:T(8,128)}, s16[1440,256]{1,0:T(8,128)(2,1)}, f32[32,5376]{1,0:T(8,128)}, /*index=5*/f32[32,5376]{1,0:T(8,128)}) custom-call(s32[3]{0:T(128)} %copy-done.22, bf16[2048,25088]{1,0:T(8,128)(2,1)} %x_ref.13, bf16[25088,128]{1,0:T(8,128)(2,1)} %bitcast.49, ...), custom_call_target="tpu_custom_call" | custom-call | flops 14092861440 | bytes 22020096 | tf_op jit(solution)/shard_map/regions/pallas_call | solution.py:439
  162.4 2.7 collective-permute-start.25
  165.2 1.6 collective-permute-start.15
  167.3 1.5 collective-permute-start.17
  169.4 1.5 collective-permute-done.15.refs_1_
  170.9 3.6 %collective-permute-done.16.refs_2_ = f32[256,128]{1,0:T(8,128)S(1)} collective-permute-done((f32[256,128]{1,0:T(8,128)S(1)}, f32[256,128]{1,0:T(8,128)S(1)}, u32[]{:S(2)}, u32[]{:S(2)}) %collective-permute-start.16) | collective-permute-done | bytes 131104 | tf_op jit(solution)/shard_map/ppermute | solution.py:540
  174.6 4.8 %small_backward.1 = (bf16[256,128]{1,0:T(8,128)(2,1)S(1)}, f32[336,128]{1,0:T(8,128)S(1)}) custom-call(f32[256,128]{1,0:T(8,128)S(1)} %get-tuple-element.136.refs_0_, f32[256,128]{1,0:T(8,128)S(1)} %collective-permute-done.15.refs_1_, f32[256,128]{1,0:T(8,128)S(1)} %collective-permute-done.16.refs_2_, f32[256,128]{1,0:T(8,128)S(1)} %collective-permute-done.17.refs_3_, ...), custom_call_target="tpu_custom_call" | custom-call | tf_op jit(solution)/shard_map/small_backward/pallas_call | solution.py:221
  180.6 1.2 collective-permute-start.19
  181.8 1.8 collective-permute-start.20
  183.6 7.3 %collective-permute-done.26.got_ref = s16[1440,256]{1,0:T(8,128)(2,1)S(1)} collective-permute-done((s16[1440,256]{1,0:T(8,128)(2,1)}, s16[1440,256]{1,0:T(8,128)(2,1)S(1)}, u32[]{:S(2)}, u32[]{:S(2)}) %collective-permute-start.26) | collective-permute-done | bytes 737312 | tf_op jit(solution)/shard_map/ppermute | solution.py:236
  194.8 7.2 %outer.3 = (s16[960,256]{1,0:T(8,128)(2,1)S(1)}, f32[32,3584]{1,0:T(8,128)S(1)}, f32[32,3584]{1,0:T(8,128)S(1)}) custom-call(s32[3]{0:T(128)S(1)} %copy-done.23, bf16[2048,25088]{1,0:T(8,128)(2,1)} %x_ref.13, bf16[128,2048]{1,0:T(8,128)(2,1)S(1)} %left.1.left_ref), custom_call_target="tpu_custom_call" | custom-call | flops 1879048192 | bytes 14680064 | tf_op jit(solution)/shard_map/outer/pallas_call | solution.py:494
  202.1 2.4 collective-permute-start.27
  204.5 8.4 %collective-permute-done.29.got_ref = s16[720,256]{1,0:T(8,128)(2,1)S(1)} collective-permute-done((s16[720,256]{1,0:T(8,128)(2,1)S(1)}, s16[720,256]{1,0:T(8,128)(2,1)S(1)}, u32[]{:S(2)}, u32[]{:S(2)}) %collective-permute-start.29) | collective-permute-done | bytes 368672 | tf_op jit(solution)/shard_map/ppermute | solution.py:251
  212.9 9.8 %outer.4 = (s16[1440,256]{1,0:T(8,128)(2,1)S(1)}, f32[32,5376]{1,0:T(8,128)S(1)}, f32[32,5376]{1,0:T(8,128)S(1)}) custom-call(s32[3]{0:T(128)S(1)} %copy-done.23, bf16[2048,25088]{1,0:T(8,128)(2,1)} %x_ref.13, bf16[128,2048]{1,0:T(8,128)(2,1)S(1)} %left.1.left_ref), custom_call_target="tpu_custom_call" | custom-call | flops 2818572288 | bytes 22020096 | tf_op jit(solution)/shard_map/outer/pallas_call | solution.py:494
  224.5 2.3 collective-permute-start.28
  226.7 8.2 %outer.5 = (s16[960,256]{1,0:T(8,128)(2,1)}, f32[32,3584]{1,0:T(8,128)S(1)}, f32[32,3584]{1,0:T(8,128)S(1)}) custom-call(s32[3]{0:T(128)S(1)} %copy-done.23, bf16[2048,25088]{1,0:T(8,128)(2,1)} %x_ref.13, bf16[128,2048]{1,0:T(8,128)(2,1)S(1)} %left.1.left_ref), custom_call_target="tpu_custom_call" | custom-call | flops 1879048192 | bytes 14680064 | tf_op jit(solution)/shard_map/outer/pallas_call | solution.py:494
  234.9 12.2 %collective-permute-done.30.got_ref = s16[1440,256]{1,0:T(8,128)(2,1)S(1)} collective-permute-done((s16[1440,256]{1,0:T(8,128)(2,1)S(1)}, s16[1440,256]{1,0:T(8,128)(2,1)S(1)}, u32[]{:S(2)}, u32[]{:S(2)}) %collective-permute-start.30) | collective-permute-done | bytes 737312 | tf_op jit(solution)/shard_map/ppermute | solution.py:236
  247.7 2.2 collective-permute-start.34
  250.8 2.3 collective-permute-start.35
  254.0 2.4 collective-permute-start.31
  257.2 9.4 %collective-permute-done.32.got_ref = s16[960,256]{1,0:T(8,128)(2,1)} collective-permute-done((s16[960,256]{1,0:T(8,128)(2,1)}, s16[960,256]{1,0:T(8,128)(2,1)}, u32[]{:S(2)}, u32[]{:S(2)}) %collective-permute-start.32) | collective-permute-done | bytes 491552 | tf_op jit(solution)/shard_map/ppermute | solution.py:236
  266.6 1.5 collective-permute-start.40
  268.1 3.0 collective-permute-done.40
  271.1 1.3 collective-permute-start.41
  274.6 2.0 join.9
  277.6 2.5 collective-permute-start.42
  281.1 1.3 collective-permute-start.36
  283.5 1.3 collective-permute-start.37
  286.8 1.3 collective-permute-start.38
  289.1 1.6 maximum_select_fusion
  290.7 7.8 %collective-permute-done.43 = f32[266,128]{1,0:T(8,128)S(1)} collective-permute-done((f32[266,128]{1,0:T(8,128)S(1)}, f32[266,128]{1,0:T(8,128)S(1)}, u32[]{:S(2)}, u32[]{:S(2)}) %collective-permute-start.43) | collective-permute-done | bytes 136224 | tf_op jit(solution)/shard_map/ppermute | solution.py:603
  298.9 1.9 maximum_bitcast_fusion
  (192 shorter events, 35.4 us)
Async XLA Ops:
  3.4 14.6 %collective-permute-start.1 = (bf16[8960,128]{1,0:T(8,128)(2,1)}, bf16[8960,128]{1,0:T(8,128)(2,1)}, u32[]{:S(2)}, u32[]{:S(2)}) collective-permute-start(bf16[8960,128]{1,0:T(8,128)(2,1)} %dynamic-slice_bitcast_fusion), channel_id=1, source_target_pairs={{0,16},{16,0},{1,17},{17,1},{2,18},{18,2},{3,19},{19,3},{4,20},{20... | collective-permute-start | bytes 6881288 | tf_op jit(solution)/shard_map/ppermute | solution.py:520
  5.2 4.1 %collective-permute-start = (bf16[3584,128]{1,0:T(8,128)(2,1)S(1)}, bf16[3584,128]{1,0:T(8,128)(2,1)S(1)}, u32[]{:S(2)}, u32[]{:S(2)}) collective-permute-start(bf16[3584,128]{1,0:T(8,128)(2,1)S(1)} %dynamic-slice_bitcast_fusion.1), channel_id=1, source_target_pairs={{0,16},{16,0},{1,17},{17,1},{2,18},{18,2},{3,19},{19,3},{4,20},{20... | collective-permute-start | bytes 2752520 | tf_op jit(solution)/shard_map/ppermute | solution.py:520
  36.0 2.0 collective-permute-start.2
  38.1 7.3 %collective-permute-start.3 = (f32[256,128]{1,0:T(8,128)S(1)}, f32[256,128]{1,0:T(8,128)S(1)}, u32[]{:S(2)}, u32[]{:S(2)}) collective-permute-start(f32[256,128]{1,0:T(8,128)S(1)} %get-tuple-element.200), channel_id=1, source_target_pairs={{0,1},{1,0},{2,3},{3,2},{4,5},{5,4},{6,7},{7,6},{8,9},{9,8},{10,11... | collective-permute-start | bytes 393224 | tf_op jit(solution)/shard_map/ppermute | solution.py:540
  41.1 8.1 %collective-permute-start.4 = (f32[256,128]{1,0:T(8,128)S(1)}, f32[256,128]{1,0:T(8,128)S(1)}, u32[]{:S(2)}, u32[]{:S(2)}) collective-permute-start(f32[256,128]{1,0:T(8,128)S(1)} %get-tuple-element.199), channel_id=1, source_target_pairs={{0,2},{1,3},{2,0},{3,1},{4,6},{5,7},{6,4},{7,5},{8,10},{9,11},{10,... | collective-permute-start | bytes 393224 | tf_op jit(solution)/shard_map/ppermute | solution.py:540
  42.6 6.6 %collective-permute-start.5 = (f32[256,128]{1,0:T(8,128)S(1)}, f32[256,128]{1,0:T(8,128)S(1)}, u32[]{:S(2)}, u32[]{:S(2)}) collective-permute-start(f32[256,128]{1,0:T(8,128)S(1)} %get-tuple-element.198), channel_id=1, source_target_pairs={{0,3},{1,2},{2,1},{3,0},{4,7},{5,6},{6,5},{7,4},{8,11},{9,10},{10,... | collective-permute-start | bytes 393224 | tf_op jit(solution)/shard_map/ppermute | solution.py:540
  53.4 4.6 %collective-permute-start.6 = (bf16[256,128]{1,0:T(8,128)(2,1)S(1)}, bf16[256,128]{1,0:T(8,128)(2,1)S(1)}, u32[]{:S(2)}, u32[]{:S(2)}) collective-permute-start(bf16[256,128]{1,0:T(8,128)(2,1)S(1)} %get-tuple-element.125.refs_0_), channel_id=1, source_target_pairs={{0,1},{1,0},{2,3},{3,2},{4,5},{5,4},{6,7},{7,6},{8,9},{9,8},{10,11... | collective-permute-start | bytes 196616 | tf_op jit(solution)/shard_map/ppermute | solution.py:549
  54.6 4.4 %collective-permute-start.7 = (bf16[256,128]{1,0:T(8,128)(2,1)S(1)}, bf16[256,128]{1,0:T(8,128)(2,1)S(1)}, u32[]{:S(2)}, u32[]{:S(2)}) collective-permute-start(bf16[256,128]{1,0:T(8,128)(2,1)S(1)} %get-tuple-element.125.refs_0_), channel_id=1, source_target_pairs={{0,2},{1,3},{2,0},{3,1},{4,6},{5,7},{6,4},{7,5},{8,10},{9,11},{10,... | collective-permute-start | bytes 196616 | tf_op jit(solution)/shard_map/ppermute | solution.py:549
  55.5 5.2 %collective-permute-start.8 = (bf16[256,128]{1,0:T(8,128)(2,1)S(1)}, bf16[256,128]{1,0:T(8,128)(2,1)S(1)}, u32[]{:S(2)}, u32[]{:S(2)}) collective-permute-start(bf16[256,128]{1,0:T(8,128)(2,1)S(1)} %get-tuple-element.125.refs_0_), channel_id=1, source_target_pairs={{0,3},{1,2},{2,1},{3,0},{4,7},{5,6},{6,5},{7,4},{8,11},{9,10},{10,... | collective-permute-start | bytes 196616 | tf_op jit(solution)/shard_map/ppermute | solution.py:549
  56.9 3.8 %collective-permute-start.9 = (bf16[256,128]{1,0:T(8,128)(2,1)S(1)}, bf16[256,128]{1,0:T(8,128)(2,1)S(1)}, u32[]{:S(2)}, u32[]{:S(2)}) collective-permute-start(bf16[256,128]{1,0:T(8,128)(2,1)S(1)} %get-tuple-element.125.refs_0_), channel_id=1, source_target_pairs={{0,16},{16,0},{1,17},{17,1},{2,18},{18,2},{3,19},{19,3},{4,20},{20... | collective-permute-start | bytes 196616 | tf_op jit(solution)/shard_map/ppermute | solution.py:520
  58.0 2.7 collective-permute-start.10
  59.0 1.7 collective-permute-start.11
  60.6 1.3 collective-permute-start.12
  117.0 43.0 %collective-permute-start.13 = (s16[1920,256]{1,0:T(8,128)(2,1)}, s16[1920,256]{1,0:T(8,128)(2,1)S(1)}, u32[]{:S(2)}, u32[]{:S(2)}) collective-permute-start(s16[1920,256]{1,0:T(8,128)(2,1)} %get-tuple-element.131), channel_id=1, source_target_pairs={{0,4},{4,0},{8,12},{12,8},{1,5},{5,1},{9,13},{13,9},{2,6},{6,2},{1... | collective-permute-start | bytes 2949128 | tf_op jit(solution)/shard_map/ppermute | solution.py:236
  118.6 43.1 %copy-start.3 = (f32[32,7168]{1,0:T(8,128)S(1)}, f32[32,7168]{1,0:T(8,128)}, u32[]{:S(2)}) copy-start(f32[32,7168]{1,0:T(8,128)} %get-tuple-element.134.other_ref) | copy-start | bytes 2752516
  161.2 3.9 %collective-permute-start.14 = (f32[1024,128]{1,0:T(8,128)S(1)}, f32[1024,128]{1,0:T(8,128)S(1)}, u32[]{:S(2)}, u32[]{:S(2)}) collective-permute-start(f32[1024,128]{1,0:T(8,128)S(1)} %constant_dynamic-slice_fusion.5), channel_id=1, source_target_pairs={{0,16},{16,0},{1,17},{17,1},{2,18},{18,2},{3,19},{19,3},{4,20},{20... | collective-permute-start | bytes 1572872 | tf_op jit(solution)/shard_map/ppermute | solution.py:520
  161.3 29.6 %collective-permute-start.26 = (s16[1440,256]{1,0:T(8,128)(2,1)}, s16[1440,256]{1,0:T(8,128)(2,1)S(1)}, u32[]{:S(2)}, u32[]{:S(2)}) collective-permute-start(s16[1440,256]{1,0:T(8,128)(2,1)} %get-tuple-element.144), channel_id=1, source_target_pairs={{0,4},{4,0},{8,12},{12,8},{1,5},{5,1},{9,13},{13,9},{2,6},{6,2},{1... | collective-permute-start | bytes 2211848 | tf_op jit(solution)/shard_map/ppermute | solution.py:236
  162.4 30.4 %copy-start.7 = (f32[32,5376]{1,0:T(8,128)S(1)}, f32[32,5376]{1,0:T(8,128)}, u32[]{:S(2)}) copy-start(f32[32,5376]{1,0:T(8,128)} %get-tuple-element.146.own_ref) | copy-start | bytes 2064388
  162.4 30.4 %copy-start.8 = (f32[32,5376]{1,0:T(8,128)S(1)}, f32[32,5376]{1,0:T(8,128)}, u32[]{:S(2)}) copy-start(f32[32,5376]{1,0:T(8,128)} %get-tuple-element.147.other_ref) | copy-start | bytes 2064388
  162.4 32.4 %collective-permute-start.25 = (s16[960,256]{1,0:T(8,128)(2,1)S(1)}, s16[960,256]{1,0:T(8,128)(2,1)S(1)}, u32[]{:S(2)}, u32[]{:S(2)}) collective-permute-start(s16[960,256]{1,0:T(8,128)(2,1)S(1)} %get-tuple-element.135), channel_id=1, source_target_pairs={{0,8},{4,12},{8,0},{12,4},{1,9},{5,13},{9,1},{13,5},{2,10},{6,14},... | collective-permute-start | bytes 1474568 | tf_op jit(solution)/shard_map/ppermute | solution.py:251
  165.2 5.7 %collective-permute-start.15 = (f32[256,128]{1,0:T(8,128)S(1)}, f32[256,128]{1,0:T(8,128)S(1)}, u32[]{:S(2)}, u32[]{:S(2)}) collective-permute-start(f32[256,128]{1,0:T(8,128)S(1)} %get-tuple-element.196), channel_id=1, source_target_pairs={{0,1},{1,0},{2,3},{3,2},{4,5},{5,4},{6,7},{7,6},{8,9},{9,8},{10,11... | collective-permute-start | bytes 393224 | tf_op jit(solution)/shard_map/ppermute | solution.py:540
  166.7 7.8 %collective-permute-start.16 = (f32[256,128]{1,0:T(8,128)S(1)}, f32[256,128]{1,0:T(8,128)S(1)}, u32[]{:S(2)}, u32[]{:S(2)}) collective-permute-start(f32[256,128]{1,0:T(8,128)S(1)} %get-tuple-element.195), channel_id=1, source_target_pairs={{0,2},{1,3},{2,0},{3,1},{4,6},{5,7},{6,4},{7,5},{8,10},{9,11},{10,... | collective-permute-start | bytes 393224 | tf_op jit(solution)/shard_map/ppermute | solution.py:540
  167.3 7.3 %collective-permute-start.17 = (f32[256,128]{1,0:T(8,128)S(1)}, f32[256,128]{1,0:T(8,128)S(1)}, u32[]{:S(2)}, u32[]{:S(2)}) collective-permute-start(f32[256,128]{1,0:T(8,128)S(1)} %get-tuple-element.194), channel_id=1, source_target_pairs={{0,3},{1,2},{2,1},{3,0},{4,7},{5,6},{6,5},{7,4},{8,11},{9,10},{10,... | collective-permute-start | bytes 393224 | tf_op jit(solution)/shard_map/ppermute | solution.py:540
  180.1 10.8 %collective-permute-start.18 = (bf16[256,128]{1,0:T(8,128)(2,1)S(1)}, bf16[256,128]{1,0:T(8,128)(2,1)S(1)}, u32[]{:S(2)}, u32[]{:S(2)}) collective-permute-start(bf16[256,128]{1,0:T(8,128)(2,1)S(1)} %get-tuple-element.143.refs_0_), channel_id=1, source_target_pairs={{0,1},{1,0},{2,3},{3,2},{4,5},{5,4},{6,7},{7,6},{8,9},{9,8},{10,11... | collective-permute-start | bytes 196616 | tf_op jit(solution)/shard_map/ppermute | solution.py:549
  180.6 10.8 %collective-permute-start.19 = (bf16[256,128]{1,0:T(8,128)(2,1)S(1)}, bf16[256,128]{1,0:T(8,128)(2,1)S(1)}, u32[]{:S(2)}, u32[]{:S(2)}) collective-permute-start(bf16[256,128]{1,0:T(8,128)(2,1)S(1)} %get-tuple-element.143.refs_0_), channel_id=1, source_target_pairs={{0,2},{1,3},{2,0},{3,1},{4,6},{5,7},{6,4},{7,5},{8,10},{9,11},{10,... | collective-permute-start | bytes 196616 | tf_op jit(solution)/shard_map/ppermute | solution.py:549
  181.8 9.7 %collective-permute-start.20 = (bf16[256,128]{1,0:T(8,128)(2,1)S(1)}, bf16[256,128]{1,0:T(8,128)(2,1)S(1)}, u32[]{:S(2)}, u32[]{:S(2)}) collective-permute-start(bf16[256,128]{1,0:T(8,128)(2,1)S(1)} %get-tuple-element.143.refs_0_), channel_id=1, source_target_pairs={{0,3},{1,2},{2,1},{3,0},{4,7},{5,6},{6,5},{7,4},{8,11},{9,10},{10,... | collective-permute-start | bytes 196616 | tf_op jit(solution)/shard_map/ppermute | solution.py:549
  190.9 1.3 collective-permute-start.21
  190.9 1.4 collective-permute-start.22
  191.4 1.3 collective-permute-start.23
  191.5 1.3 collective-permute-start.24
  193.3 19.7 %collective-permute-start.29 = (s16[720,256]{1,0:T(8,128)(2,1)S(1)}, s16[720,256]{1,0:T(8,128)(2,1)S(1)}, u32[]{:S(2)}, u32[]{:S(2)}) collective-permute-start(s16[720,256]{1,0:T(8,128)(2,1)S(1)} %get-tuple-element.148), channel_id=1, source_target_pairs={{0,8},{4,12},{8,0},{12,4},{1,9},{5,13},{9,1},{13,5},{2,10},{6,14},... | collective-permute-start | bytes 1105928 | tf_op jit(solution)/shard_map/ppermute | solution.py:251
  202.1 21.3 %collective-permute-start.27 = (s16[960,256]{1,0:T(8,128)(2,1)S(1)}, s16[960,256]{1,0:T(8,128)(2,1)S(1)}, u32[]{:S(2)}, u32[]{:S(2)}) collective-permute-start(s16[960,256]{1,0:T(8,128)(2,1)S(1)} %get-tuple-element.150), channel_id=1, source_target_pairs={{0,4},{4,0},{8,12},{12,8},{1,5},{5,1},{9,13},{13,9},{2,6},{6,2},{1... | collective-permute-start | bytes 1474568 | tf_op jit(solution)/shard_map/ppermute | solution.py:236
  223.4 23.7 %collective-permute-start.30 = (s16[1440,256]{1,0:T(8,128)(2,1)S(1)}, s16[1440,256]{1,0:T(8,128)(2,1)S(1)}, u32[]{:S(2)}, u32[]{:S(2)}) collective-permute-start(s16[1440,256]{1,0:T(8,128)(2,1)S(1)} %get-tuple-element.157), channel_id=1, source_target_pairs={{0,4},{4,0},{8,12},{12,8},{1,5},{5,1},{9,13},{13,9},{2,6},{6,2},{1... | collective-permute-start | bytes 2211848 | tf_op jit(solution)/shard_map/ppermute | solution.py:236
  224.5 25.5 %collective-permute-start.28 = (s16[480,256]{1,0:T(8,128)(2,1)S(1)}, s16[480,256]{1,0:T(8,128)(2,1)S(1)}, u32[]{:S(2)}, u32[]{:S(2)}) collective-permute-start(s16[480,256]{1,0:T(8,128)(2,1)S(1)} %get-tuple-element.154), channel_id=1, source_target_pairs={{0,8},{4,12},{8,0},{12,4},{1,9},{5,13},{9,1},{13,5},{2,10},{6,14},... | collective-permute-start | bytes 737288 | tf_op jit(solution)/shard_map/ppermute | solution.py:251
  247.7 29.8 %collective-permute-start.34 = (f32[32,7168]{1,0:T(8,128)S(1)}, f32[32,7168]{1,0:T(8,128)}, u32[]{:S(2)}, u32[]{:S(2)}) collective-permute-start(f32[32,7168]{1,0:T(8,128)S(1)} %total.8), channel_id=1, source_target_pairs={{0,16},{1,17},{2,18},{3,19},{4,20},{5,21},{6,22},{7,23},{8,24},{9,... | collective-permute-start | bytes 2752520 | tf_op jit(solution)/shard_map/ppermute | solution.py:793
  250.7 16.0 %collective-permute-start.32 = (s16[960,256]{1,0:T(8,128)(2,1)}, s16[960,256]{1,0:T(8,128)(2,1)}, u32[]{:S(2)}, u32[]{:S(2)}) collective-permute-start(s16[960,256]{1,0:T(8,128)(2,1)} %get-tuple-element.166), channel_id=1, source_target_pairs={{0,4},{4,0},{8,12},{12,8},{1,5},{5,1},{9,13},{13,9},{2,6},{6,2},{1... | collective-permute-start | bytes 1474568 | tf_op jit(solution)/shard_map/ppermute | solution.py:236
  250.8 26.8 %collective-permute-start.35 = (f32[32,5376]{1,0:T(8,128)S(1)}, f32[32,5376]{1,0:T(8,128)}, u32[]{:S(2)}, u32[]{:S(2)}) collective-permute-start(f32[32,5376]{1,0:T(8,128)S(1)} %total.9), channel_id=1, source_target_pairs={{0,16},{1,17},{2,18},{3,19},{4,20},{5,21},{6,22},{7,23},{8,24},{9,... | collective-permute-start | bytes 2064392 | tf_op jit(solution)/shard_map/ppermute | solution.py:793
  254.0 2.4 collective-permute-start.39
  254.0 22.8 %collective-permute-start.31 = (s16[720,256]{1,0:T(8,128)(2,1)}, s16[720,256]{1,0:T(8,128)(2,1)S(1)}, u32[]{:S(2)}, u32[]{:S(2)}) collective-permute-start(s16[720,256]{1,0:T(8,128)(2,1)} %copy-done.32), channel_id=1, source_target_pairs={{0,8},{4,12},{8,0},{12,4},{1,9},{5,13},{9,1},{13,5},{2,10},{6,14},... | collective-permute-start | bytes 1105928 | tf_op jit(solution)/shard_map/ppermute | solution.py:251
  266.6 4.5 %collective-permute-start.40 = (f32[168,128]{1,0:T(8,128)S(1)}, f32[168,128]{1,0:T(8,128)S(1)}, u32[]{:S(2)}, u32[]{:S(2)}) collective-permute-start(f32[168,128]{1,0:T(8,128)S(1)} %dynamic-slice_add_fusion.2), channel_id=1, source_target_pairs={{0,1},{1,0},{2,3},{3,2},{4,5},{5,4},{6,7},{7,6},{8,9},{9,8},{10,11... | collective-permute-start | bytes 258056 | tf_op jit(solution)/shard_map/ppermute | solution.py:603
  271.1 5.6 %collective-permute-start.41 = (f32[168,128]{1,0:T(8,128)S(1)}, f32[168,128]{1,0:T(8,128)S(1)}, u32[]{:S(2)}, u32[]{:S(2)}) collective-permute-start(f32[168,128]{1,0:T(8,128)S(1)} %add.89), channel_id=1, source_target_pairs={{0,2},{1,3},{2,0},{3,1},{4,6},{5,7},{6,4},{7,5},{8,10},{9,11},{10,... | collective-permute-start | bytes 258056 | tf_op jit(solution)/shard_map/ppermute | solution.py:603
  276.6 9.2 %collective-permute-start.33 = (s16[480,256]{1,0:T(8,128)(2,1)}, s16[480,256]{1,0:T(8,128)(2,1)}, u32[]{:S(2)}, u32[]{:S(2)}) collective-permute-start(s16[480,256]{1,0:T(8,128)(2,1)} %get-tuple-element.171), channel_id=1, source_target_pairs={{0,8},{4,12},{8,0},{12,4},{1,9},{5,13},{9,1},{13,5},{2,10},{6,14},... | collective-permute-start | bytes 737288 | tf_op jit(solution)/shard_map/ppermute | solution.py:251
  277.6 10.6 %collective-permute-start.42 = (f32[266,128]{1,0:T(8,128)S(1)}, f32[266,128]{1,0:T(8,128)}, u32[]{:S(2)}, u32[]{:S(2)}) collective-permute-start(f32[266,128]{1,0:T(8,128)S(1)} %pad_maximum_fusion), channel_id=1, source_target_pairs={{0,4},{4,0},{8,12},{12,8},{1,5},{5,1},{9,13},{13,9},{2,6},{6,2},{1... | collective-permute-start | bytes 408584 | tf_op jit(solution)/shard_map/ppermute | solution.py:603
  281.1 17.7 %collective-permute-start.36 = (f32[32,3584]{1,0:T(8,128)S(1)}, f32[32,3584]{1,0:T(8,128)S(1)}, u32[]{:S(2)}, u32[]{:S(2)}) collective-permute-start(f32[32,3584]{1,0:T(8,128)S(1)} %total.5), channel_id=1, source_target_pairs={{16,0},{17,1},{18,2},{19,3},{20,4},{21,5},{22,6},{23,7},{24,8},{25... | collective-permute-start | bytes 1376264 | tf_op jit(solution)/shard_map/ppermute | solution.py:795
  283.5 15.3 %collective-permute-start.37 = (f32[32,5376]{1,0:T(8,128)S(1)}, f32[32,5376]{1,0:T(8,128)S(1)}, u32[]{:S(2)}, u32[]{:S(2)}) collective-permute-start(f32[32,5376]{1,0:T(8,128)S(1)} %total.6), channel_id=1, source_target_pairs={{16,0},{17,1},{18,2},{19,3},{20,4},{21,5},{22,6},{23,7},{24,8},{25... | collective-permute-start | bytes 2064392 | tf_op jit(solution)/shard_map/ppermute | solution.py:795
  286.8 11.9 %collective-permute-start.38 = (f32[32,3584]{1,0:T(8,128)S(1)}, f32[32,3584]{1,0:T(8,128)S(1)}, u32[]{:S(2)}, u32[]{:S(2)}) collective-permute-start(f32[32,3584]{1,0:T(8,128)S(1)} %total.7), channel_id=1, source_target_pairs={{16,0},{17,1},{18,2},{19,3},{20,4},{21,5},{22,6},{23,7},{24,8},{25... | collective-permute-start | bytes 1376264 | tf_op jit(solution)/shard_map/ppermute | solution.py:795
  289.1 9.5 %collective-permute-start.43 = (f32[266,128]{1,0:T(8,128)S(1)}, f32[266,128]{1,0:T(8,128)S(1)}, u32[]{:S(2)}, u32[]{:S(2)}) collective-permute-start(f32[266,128]{1,0:T(8,128)S(1)} %add.91), channel_id=1, source_target_pairs={{0,8},{4,12},{8,0},{12,4},{1,9},{5,13},{9,1},{13,5},{2,10},{6,14},... | collective-permute-start | bytes 408584 | tf_op jit(solution)/shard_map/ppermute | solution.py:603
  298.5 2.3 collective-permute-start.44
  (40 other events, 365.8 us)
